TPU v7x, 256 devices: a whole 4x4x8 slice. The times are simulated.
256 devices in a mesh: dp: 32 (over z, x), tensor: 8 (over y, core).
Axes of the slice: x: 4, y: 4, z: 8, core: 2. Of those that a mesh axis runs over, the one named last changes fastest.
Arguments:
- grads: bfloat16 [32, 2, 4096, 1024], P('dp', None, None, 'tensor'), may hold values from -6 to 6
- momentum: bfloat16 [32, 2, 4096, 1024], P('dp', None, None, 'tensor'), may hold values from -6 to 6
- error: bfloat16 [32, 2, 4096, 1024], P('dp', None, None, 'tensor'), may hold values from -4 to 4
- q_warm: bfloat16 [1024, 128], P('tensor'), may hold values from -0.1875 to 0.1875
Outputs:
- momentum_out: bfloat16 [32, 2, 4096, 1024], P('dp', None, None, 'tensor')
- error_out: bfloat16 [32, 2, 4096, 1024], P('dp', None, None, 'tensor')
- p_factor: bfloat16 [4096, 128], replicated
- q_factor: float32 [1024, 128], P('tensor')
All inputs are finite; a program needn't handle non-finite values.
Results may differ from a plain program's by a relative error of at most 0.017.
Values may be sent and summed in bfloat16 or wider, within the bound.
No kernel may reach another device: no remote copies, remote signals or barrier semaphores. Data moves between devices by JAX's collectives and lax.ppermute only.
A program may use at most 64 MiB of HBM per device.

v0:
```python
import jax
import jax.numpy as jnp
from jax import lax
from jax.sharding import PartitionSpec as P


def orthonormal(p_three, gram):
    pieces = []
    for group in range(2):
        lower = jnp.linalg.cholesky(gram[group])
        pieces.append(
            lax.linalg.triangular_solve(
                lower, p_three[:, group, :], left_side=False, lower=True, transpose_a=True
            )
        )
    return jnp.stack(pieces, 1).reshape(p_three.shape[0], -1).astype(jnp.bfloat16)


def gram_of(p_three):
    return jnp.einsum("rgn,rgm->gnm", p_three, p_three, precision=lax.Precision.HIGHEST)


def local(grads, momentum, error, q_warm):
    momentum_out = (0.9 * momentum.astype(jnp.float32) + grads.astype(jnp.float32)).astype(
        jnp.bfloat16
    )
    corrected = (momentum_out.astype(jnp.float32) + error.astype(jnp.float32)).astype(jnp.bfloat16)
    block = corrected[0]
    rows = block.shape[1]
    local_cols = block.shape[2]
    rank = q_warm.shape[1] // 2
    q_three = q_warm.reshape(local_cols, 2, rank)
    p_raw = lax.psum(
        jnp.einsum("grk,kgn->rgn", block, q_three, preferred_element_type=jnp.float32).reshape(
            rows, 2 * rank
        ),
        ("dp", "tensor"),
    )
    p_whole = p_raw.reshape(rows, 2, rank)
    p_factor = orthonormal(p_whole, gram_of(p_whole))
    p_three = p_factor.reshape(rows, 2, rank)
    q_part = jnp.einsum("grk,rgn->kgn", block, p_three, preferred_element_type=jnp.float32).reshape(
        local_cols, 2 * rank
    )
    q_factor = lax.psum(q_part.astype(jnp.bfloat16), "dp").astype(jnp.float32) / lax.axis_size("dp")
    q_round = q_factor.astype(jnp.bfloat16).reshape(local_cols, 2, rank)
    approx = jnp.einsum("rgn,kgn->grk", p_three, q_round, preferred_element_type=jnp.float32)
    error_out = (corrected.astype(jnp.float32) - approx[None]).astype(jnp.bfloat16)
    return (momentum_out, error_out, p_factor, q_factor)


def solution(mesh):
    in_specs = (
        P("dp", None, None, "tensor"),
        P("dp", None, None, "tensor"),
        P("dp", None, None, "tensor"),
        P("tensor", None),
    )
    out_specs = (
        P("dp", None, None, "tensor"),
        P("dp", None, None, "tensor"),
        P(),
        P("tensor", None),
    )
    return jax.shard_map(local, mesh=mesh, in_specs=in_specs, out_specs=out_specs, check_vma=False)
```

profile of v0, /device:TPU:32, one launch (start us, length us, event | category | flops | bytes accessed | tf_op | source)
XLA Modules:
  0.0 461.1 jit_solution(17382312734773725870)
XLA Ops:
  7.2 0.0 all-reduce.2.cloned.1.call-start
  7.2 0.9 copy.16
  8.1 0.0 copy-start.1
  8.1 3.1 add_convert_fusion.1
  11.1 0.0 copy-start
  11.2 0.0 copy-done.1
  11.2 2.2 convolution_bitcast_fusion.1
  13.3 0.0 all-reduce.2.cloned.1.call-update
  13.4 262.1 %all-reduce.2.cloned.1.call-done = f32[4096,2,64]{0,2,1:T(8,128)} async-done(((f32[4096,2,64]{0,2,1:T(8,128)}), f32[4096,2,64]{0,2,1:T(8,128)}) %all-reduce.2.cloned.1.call-update) | async-done | bytes 2097168 | tf_op jit(solution)/shard_map/psum | solution.py:33
  275.5 4.3 fusion.15
  279.8 0.1 copy.18
  279.9 0.1 copy.20
  280.0 5.8 %cholesky.55 = f32[64,64]{1,0:T(8,128)S(1)} custom-call(f32[64,64]{1,0:T(8,128)S(1)} %get-tuple-element.17), custom_call_target="Cholesky" | custom-call | tf_op jit(solution)/shard_map/jit(cholesky)/cholesky | solution.py:10
  285.9 0.6 compare_reduce_fusion
  286.5 0.7 fusion.9
  287.2 4.9 %custom-call.7 = f32[1,64,64]{1,2,0:T(8,128)S(1)} custom-call(f32[1,64,64]{2,1,0:T(8,128)S(1)} %fusion.9), custom_call_target="InvertDiagBlocksLowerTriangular" | custom-call | tf_op jit(solution)/shard_map/triangular_solve/custom-call.0 | solution.py:12
  292.1 5.9 %cholesky.44 = f32[64,64]{1,0:T(8,128)S(1)} custom-call(f32[64,64]{1,0:T(8,128)S(1)} %get-tuple-element.16), custom_call_target="Cholesky" | custom-call | tf_op jit(solution)/shard_map/jit(cholesky)/cholesky | solution.py:10
  298.0 0.6 compare_reduce_fusion.1
  298.6 0.7 fusion.8
  299.3 4.9 %custom-call.6 = f32[1,64,64]{1,2,0:T(8,128)S(1)} custom-call(f32[1,64,64]{2,1,0:T(8,128)S(1)} %fusion.8), custom_call_target="InvertDiagBlocksLowerTriangular" | custom-call | tf_op jit(solution)/shard_map/triangular_solve/custom-call.0 | solution.py:12
  304.2 0.0 copy-start.2
  304.2 2.4 convolution_bitcast_fusion.2
  306.6 2.3 convolution_bitcast_fusion.3
  308.9 0.0 copy-done.2
  308.9 0.7 fusion.5
  309.6 1.1 maximum_convert_fusion
  310.7 0.1 copy.21
  310.8 136.4 %psum.15 = bf16[128,128]{1,0:T(8,128)(2,1)S(1)} all-reduce(bf16[128,128]{1,0:T(8,128)(2,1)S(1)} %copy.21), channel_id=1, replica_groups=mesh['dp'=32,'tensor'=8] {'dp'}, use_global_device_ids=true, to_apply=%region_3.6 | all-reduce | flops 16384 | bytes 65536 | tf_op jit(solution)/shard_map/psum | solution.py:45
  447.2 0.6 fusion.14
  447.8 0.1 copy.22
  447.9 4.1 fusion.1
  452.0 2.3 copy.23
  (5 shorter events, 0.1 us)
Async XLA Ops:
  7.2 268.3 %all-reduce.2.cloned.1.call-start = ((), (), s32[]{:S(2)}) async-start(), calls=%async_computation | async-start | bytes 4194304 | tf_op jit(solution)/shard_map/psum | solution.py:33
  8.1 3.1 copy-start.1
  11.1 436.8 %copy-start = (bf16[1,2,4096,128]{3,2,1,0:T(8,128)(2,1)}, bf16[1,2,4096,128]{3,2,1,0:T(8,128)(2,1)S(1)}, u32[]{:S(2)}) copy-start(bf16[1,2,4096,128]{3,2,1,0:T(8,128)(2,1)S(1)} %add_convert_fusion.1) | copy-start | bytes 6291460
  304.2 4.7 %copy-start.2 = (bf16[1,2,4096,128]{3,2,1,0:T(8,128)(2,1)S(1)}, bf16[1,2,4096,128]{3,2,1,0:T(8,128)(2,1)}, u32[]{:S(2)}) copy-start(bf16[1,2,4096,128]{3,2,1,0:T(8,128)(2,1)} %param.9) | copy-start | bytes 6291460
Sparse Core Ops, SparseCore 0:
  14.0 261.4 all-reduce.1
where the time goes:
time: 467 us; the launch traced here: 461 us
  waiting for transfers between devices  262 us (56%)
  blocking collectives  136 us (29%)
  other arithmetic  28.9 us (6%)
  matrix products  15.9 us (3%)
  between operations  14.2 us (3%)
    psum x1, waiting for transfers between devices, local(): lax.psum(jnp.einsum('grk,kgn->rgn', block, q_three, preferred_element_typ...  262 us
    psum x1, blocking collectives, local(): lax.psum(q_part.astype(jnp.bfloat16), 'dp').astype(jnp.float32)  136 us
    another operation x6, other arithmetic, orthonormal(): lower = jnp.linalg.cholesky(gram[group])  13.1 us
    another operation x4, other arithmetic, orthonormal(): lax.linalg.triangular_solve(lower, p_three[:, group, :], left_side=False,...  11.1 us
  transfers between devices with their start and end apart: 1, of which 1 were waited for; matrix products, arithmetic and copies ran while one was open for 0% of the time, Pallas kernels for 0%

commit v1 on v0

v1 whole, which is shorter than its diff:
```python
import jax
import jax.numpy as jnp
from jax import lax
from jax.experimental import pallas as pl
from jax.experimental.pallas import tpu as pltpu
from jax.sharding import Mesh
from jax.sharding import PartitionSpec as P

BF, F32 = jnp.bfloat16, jnp.float32
NZ, NX, NY, NC = 8, 4, 4, 2
ROWS, COLS, RANK2 = 4096, 128, 128
HALF = ROWS // NC
BLK = HALF // (NX * NY)
STEP = 512
NSTEP = HALF // STEP
MIB = 1 << 20


def dot(a, b, dims=((1,), (0,)), precision=None):
    return lax.dot_general(a, b, (dims, ((), ())), precision=precision, preferred_element_type=F32)


def left_lanes(shape):
    return lax.broadcasted_iota(jnp.int32, shape, len(shape) - 1) < RANK2 // 2


def front_body(half_ref, g_ref, m_ref, e_ref, q_ref, *rest):
    mo_ref, co_ref, p_ref = rest[-3:]
    q = q_ref[...]
    left = left_lanes(q.shape)
    total = None
    for group in range(2):
        mo = (0.9 * m_ref[0, group].astype(F32) + g_ref[0, group].astype(F32)).astype(BF)
        co = (mo.astype(F32) + e_ref[0, group].astype(F32)).astype(BF)
        mo_ref[0, group] = mo
        co_ref[group] = co
        term = dot(co, jnp.where(left if group == 0 else ~left, q, jnp.zeros_like(q)))
        total = term if total is None else total + term
    p_ref[...] = total.astype(p_ref.dtype)


def front(half, grads, momentum, error, q_warm, before, p_dtype):
    big = pl.BlockSpec((1, 2, STEP, COLS), lambda i, h: (0, 0, h[0] * NSTEP + i, 0))
    in_specs = [big, big, big, pl.BlockSpec((COLS, RANK2), lambda i, h: (0, 0))]
    args = [grads, momentum, error, q_warm]
    aliases = {}
    if before is not None:
        in_specs.append(pl.BlockSpec(memory_space=pl.ANY))
        args.append(before)
        aliases = {5: 0}
    return pl.pallas_call(
        front_body,
        grid_spec=pltpu.PrefetchScalarGridSpec(
            num_scalar_prefetch=1,
            grid=(NSTEP,),
            in_specs=in_specs,
            out_specs=[
                big,
                pl.BlockSpec((2, STEP, COLS), lambda i, h: (0, i, 0)),
                pl.BlockSpec((STEP, RANK2), lambda i, h: (i, 0)),
            ],
        ),
        out_shape=[
            jax.ShapeDtypeStruct(grads.shape, BF),
            jax.ShapeDtypeStruct((2, HALF, COLS), BF),
            jax.ShapeDtypeStruct((HALF, RANK2), p_dtype),
        ],
        input_output_aliases=aliases,
        compiler_params=pltpu.CompilerParams(vmem_limit_bytes=16 * MIB),
        cost_estimate=pl.CostEstimate(flops=2 * HALF * 256 * 128, bytes_accessed=6 * MIB, transcendentals=0),
    )(half, *args)


def sum_copies_body(x_ref, o_ref):
    total = x_ref[0].astype(F32)
    for k in range(1, x_ref.shape[0]):
        total = total + x_ref[k].astype(F32)
    total = total.astype(BF)
    for k in range(o_ref.shape[0]):
        o_ref[k] = total


def sum_copies(x, copies):
    return pl.pallas_call(
        sum_copies_body,
        out_shape=jax.ShapeDtypeStruct((copies, *x.shape[1:]), BF),
        compiler_params=pltpu.CompilerParams(vmem_limit_bytes=16 * MIB),
    )(x)


def products_body(p_ref, c_ref, *rest):
    u_ref, g_ref = rest[-2:]
    u0 = u1 = gram = None
    for i in range(NSTEP):
        rows = pl.ds(i * STEP, STEP)
        p = p_ref[rows]
        pt = p.T
        a, b, c = dot(pt[: RANK2 // 2], c_ref[0, rows]), dot(pt[RANK2 // 2 :], c_ref[1, rows]), dot(pt, p)
        u0, u1, gram = (a, b, c) if u0 is None else (u0 + a, u1 + b, gram + c)
    u = jnp.concatenate([u0, u1], axis=0)
    if len(rest) == 2:
        u_ref[...] = u
        g_ref[...] = gram
    else:
        u = (u + rest[0][...]).astype(BF)
        for k in range(NZ):
            u_ref[k] = u
        g_ref[...] = gram + rest[1][...]


def products(p, c, before):
    last = before is not None
    return pl.pallas_call(
        products_body,
        out_shape=[
            jax.ShapeDtypeStruct((NZ, RANK2, COLS) if last else (RANK2, COLS), BF if last else F32),
            jax.ShapeDtypeStruct((RANK2, RANK2), F32),
        ],
        compiler_params=pltpu.CompilerParams(vmem_limit_bytes=16 * MIB),
        cost_estimate=pl.CostEstimate(flops=2 * HALF * 256 * 128, bytes_accessed=2 * MIB, transcendentals=0),
    )(p, c, *(before if last else ()))


def inverse_body(g_ref, o_ref):
    n = RANK2 // 2
    gram = g_ref[...]
    row = lax.broadcasted_iota(jnp.int32, (n, 2 * n), 0)
    lane = lax.broadcasted_iota(jnp.int32, (n, 2 * n), 1)
    eye_left = jnp.where(row == lane, 1.0, 0.0)
    eye_right = jnp.where(row + n == lane, 1.0, 0.0)
    left = lane < n
    top = jnp.where(left, gram[:n], eye_right)
    swapped = pltpu.roll(gram[n:], n, 1)
    bottom = jnp.where(left, swapped, eye_right)
    both = [top, bottom]
    for k in range(n - 1):
        for s in range(2):
            a = both[s]
            pivot = a[k : k + 1, :]
            column = a[:, k : k + 1]
            factor = jnp.where(row[:, :1] > k, column / a[k : k + 1, k : k + 1], 0.0)
            both[s] = a - factor * pivot
    out = []
    for s in range(2):
        a = both[s]
        d = jnp.sum(a * eye_left, axis=1, keepdims=True)
        out.append(a * lax.rsqrt(d))
    o_ref[:n] = jnp.where(left, pltpu.roll(out[0], n, 1), 0.0)
    o_ref[n:] = jnp.where(left, 0.0, out[1])


def inverse(gram):
    return pl.pallas_call(
        inverse_body,
        out_shape=jax.ShapeDtypeStruct((RANK2, RANK2), F32),
        compiler_params=pltpu.CompilerParams(vmem_limit_bytes=16 * MIB),
        cost_estimate=pl.CostEstimate(flops=4 * 64**3, bytes_accessed=128 * 1024, transcendentals=128),
    )(gram)


def back_body(half_ref, po_ref, pt_ref, co_ref, ct_ref, l_ref, u_ref, e_ref, p_ref, q_ref, qt_ref, hi_ref, lo_ref):
    i = pl.program_id(0)

    @pl.when(i == 0)
    def _():
        inv = l_ref[...]
        qt = dot(inv, u_ref[...], precision=lax.Precision.HIGHEST) * (1.0 / (NZ * NX))
        q_ref[...] = qt.T
        qt_ref[...] = qt.astype(BF)
        hi = inv.astype(BF)
        hi_ref[...] = hi
        lo_ref[...] = (inv - hi.astype(F32)).astype(BF)

    def part(p_in, c_in):
        p = p_in[...]
        factor = dot(p, hi_ref[...], ((1,), (1,))) + dot(p, lo_ref[...], ((1,), (1,)))
        factor = factor.astype(BF)
        p_ref[...] = factor
        n = RANK2 // 2
        for group in range(2):
            approx = dot(factor[:, group * n : (group + 1) * n], qt_ref[group * n : (group + 1) * n])
            e_ref[0, group] = (c_in[group].astype(F32) - approx).astype(BF)

    @pl.when(i < NSTEP)
    def _():
        part(po_ref, co_ref)

    @pl.when(i >= NSTEP)
    def _():
        part(pt_ref, ct_ref)


def back(half, p_own, p_other, c_own, c_other, inv, u):
    def own(i):
        return jnp.minimum(i, NSTEP - 1)

    def other(i):
        return jnp.maximum(i - NSTEP, 0)

    def where(i, h):
        return jnp.where(i < NSTEP, h[0] * NSTEP + i, (1 - h[0]) * NSTEP + i - NSTEP)

    small = pl.BlockSpec((RANK2, RANK2), lambda i, h: (0, 0))
    return pl.pallas_call(
        back_body,
        grid_spec=pltpu.PrefetchScalarGridSpec(
            num_scalar_prefetch=1,
            grid=(2 * NSTEP,),
            in_specs=[
                pl.BlockSpec((STEP, RANK2), lambda i, h: (own(i), 0)),
                pl.BlockSpec((STEP, RANK2), lambda i, h: (other(i), 0)),
                pl.BlockSpec((2, STEP, COLS), lambda i, h: (0, own(i), 0)),
                pl.BlockSpec((2, STEP, COLS), lambda i, h: (0, other(i), 0)),
                small,
                small,
            ],
            out_specs=[
                pl.BlockSpec((1, 2, STEP, COLS), lambda i, h: (0, 0, where(i, h), 0)),
                pl.BlockSpec((STEP, RANK2), lambda i, h: (where(i, h), 0)),
                small,
            ],
            scratch_shapes=[pltpu.VMEM((RANK2, COLS), BF), pltpu.VMEM((RANK2, RANK2), BF), pltpu.VMEM((RANK2, RANK2), BF)],
        ),
        out_shape=[
            jax.ShapeDtypeStruct((1, 2, ROWS, COLS), BF),
            jax.ShapeDtypeStruct((ROWS, RANK2), BF),
            jax.ShapeDtypeStruct((COLS, RANK2), F32),
        ],
        compiler_params=pltpu.CompilerParams(vmem_limit_bytes=16 * MIB),
        cost_estimate=pl.CostEstimate(flops=6 * ROWS * 128 * 128, bytes_accessed=8 * MIB, transcendentals=0),
    )(half, p_own, p_other, c_own, c_other, inv, u)


def swap_cores(x):
    return lax.ppermute(x, "c", [(0, 1), (1, 0)])


def exchange(x, axes):
    return lax.all_to_all(x, axes, 0, 0)


def local(grads, momentum, error, q_warm):
    c = lax.axis_index("c").astype(jnp.int32)
    mine, theirs = c.reshape(1), (1 - c).reshape(1)

    with jax.named_scope("p_partial"):
        mo, c_other, p_send = front(theirs, grads, momentum, error, q_warm, None, BF)
        p_got = swap_cores(p_send)
        momentum_out, c_own, p_own = front(mine, grads, momentum, error, q_warm, mo, F32)
        chip = (p_own + p_got.astype(F32)).astype(BF)
    with jax.named_scope("p_sum"):
        parts = exchange(chip.reshape(NX * NY, BLK, RANK2), ("x", "y"))
        parts = exchange(sum_copies(parts, NZ), "z")
        p_mine = exchange(sum_copies(parts, NX * NY), ("x", "y")).reshape(HALF, RANK2)
        p_theirs = swap_cores(p_mine)
    with jax.named_scope("u_sum"):
        first = products(p_mine, c_own, None)
        copies, gram = products(p_theirs, c_other, first)
        parts = exchange(copies, "z")
        u = jnp.sum(parts.astype(F32), axis=0).astype(BF)
        got = [lax.ppermute(u, "x", [(i, i ^ k) for i in range(NX)]) for k in (1, 2, 3)]
        inv = inverse(gram)
        u, a, b, d = (t.astype(F32) for t in (u, *got))
        u = (u + a) + (b + d)
    with jax.named_scope("back"):
        error_out, p_factor, q_factor = back(mine, p_mine, p_theirs, c_own, c_other, inv, u)
    return momentum_out, error_out, p_factor, q_factor


def solution(mesh):
    fine = Mesh(mesh.devices.reshape(NZ, NX, NY, NC), ("z", "x", "y", "c"))
    dp, tensor = ("z", "x"), ("y", "c")
    big = P(dp, None, None, tensor)
    return jax.shard_map(
        local,
        mesh=fine,
        in_specs=(big, big, big, P(tensor, None)),
        out_specs=(big, big, P(), P(tensor, None)),
        check_vma=False,
    )
```

time: 467 us -> 96.4 us (0.21)
  waiting for transfers between devices: 262 us -> 1.43 us
  blocking collectives: 136 us -> 64.2 us
  other arithmetic: 28.9 us -> 0.2 us
  Pallas kernels: 0 us -> 17.5 us
  matrix products: 15.9 us -> 0 us
  between operations: 14.2 us -> 0.71 us
    psum x1 -> x0, waiting for transfers between devices: 262 us -> none  [local(): lax.psum(jnp.einsum('grk,kgn->rgn', block, q_three, preferred_element_typ...]
    psum x1 -> x0, blocking collectives: 136 us -> none  [local(): lax.psum(q_part.astype(jnp.bfloat16), 'dp').astype(jnp.float32)]
    all_to_all x0 -> x4, blocking collectives: none -> 64.2 us  [exchange(): return lax.all_to_all(x, axes, 0, 0)]
    another operation x10 -> x0, other arithmetic: 24.2 us -> none  [the longest x6 13.1 us: orthonormal(): lower = jnp.linalg.cholesky(gram[group])]
    pallas_call x0 -> x8, Pallas kernels: none -> 17.5 us  [the longest x1 5.98 us: back(): pl.pallas_call(back_body, grid_spec=pltpu.PrefetchScalarGridSpec(num_scal...]
    dot_general x4 -> x0, matrix products: 11.3 us -> none  [the longest x1 4.33 us: gram_of(): jnp.einsum('rgn,rgm->gnm', p_three, p_three, precision=lax.Precision.HIGH...]
  transfers between devices with their start and end apart: 1 -> 5, of which waited for: 1 -> 1; matrix products, arithmetic and copies ran while one was open for 0% -> 0% of each run, Pallas kernels for 0% -> 9%
where the time goes in v1:
time: 96.4 us; the launch traced here: 94.4 us
  blocking collectives  64.2 us (67%)
  Pallas kernels  17.5 us (18%)
  local copies, waits for them, and re-layouts  6.25 us (6%)
  starting transfers between devices  4.19 us (4%)
  waiting for transfers between devices  1.43 us (1%)
    all_to_all x4, blocking collectives, exchange(): return lax.all_to_all(x, axes, 0, 0)  64.2 us
    unnamed x14, local copies, waits for them, and re-layouts  6.25 us
    pallas_call x1, Pallas kernels, back(): pl.pallas_call(back_body, grid_spec=pltpu.PrefetchScalarGridSpec(num_scal...  5.98 us
    pallas_call x1, Pallas kernels, inverse(): pl.pallas_call(inverse_body, out_shape=jax.ShapeDtypeStruct((RANK2, RANK2...  5.41 us
    pallas_call x2, Pallas kernels, front(): pl.pallas_call(front_body, grid_spec=pltpu.PrefetchScalarGridSpec(num_sca...  5 us
    ppermute x3, starting transfers between devices, local(): lax.ppermute(u, 'x', [(i, i ^ k) for i in range(NX)])  4.18 us
  transfers between devices with their start and end apart: 5, of which 1 were waited for; matrix products, arithmetic and copies ran while one was open for 0% of the time, Pallas kernels for 9%

profile of v1, /device:TPU:32, one launch (start us, length us, event | category | flops | bytes accessed | tf_op | source)
XLA Modules:
  0.0 94.4 jit_solution(12202830352896913572)
XLA Ops:
  0.6 0.0 copy-start
  0.6 1.6 %copy-done = bf16[1,2,4096,128]{3,2,1,0:T(8,128)(2,1)S(1)} copy-done((bf16[1,2,4096,128]{3,2,1,0:T(8,128)(2,1)S(1)}, bf16[1,2,4096,128]{3,2,1,0:T(8,128)(2,1)}, u32[]{:S(2)}) %copy-start) | copy-done | bytes 2097176
  2.2 0.0 copy-start.2
  2.2 1.6 %copy-done.2 = bf16[1,2,4096,128]{3,2,1,0:T(8,128)(2,1)S(1)} copy-done((bf16[1,2,4096,128]{3,2,1,0:T(8,128)(2,1)S(1)}, bf16[1,2,4096,128]{3,2,1,0:T(8,128)(2,1)}, u32[]{:S(2)}) %copy-start.2) | copy-done | bytes 2097176
  3.8 1.6 %copy-done.4 = bf16[1,2,4096,128]{3,2,1,0:T(8,128)(2,1)S(1)} copy-done((bf16[1,2,4096,128]{3,2,1,0:T(8,128)(2,1)S(1)}, bf16[1,2,4096,128]{3,2,1,0:T(8,128)(2,1)}, u32[]{:S(2)}) %copy-start.4) | copy-done | bytes 2097176
  5.4 0.8 copy-done.6
  6.2 2.5 %p_partial.2 = (bf16[1,2,4096,128]{3,2,1,0:T(8,128)(2,1)}, bf16[2,2048,128]{2,1,0:T(8,128)(2,1)S(1)}, bf16[2048,128]{1,0:T(8,128)(2,1)S(1)}) custom-call(s32[1]{0:T(128)} %bitcast.1.half_ref, bf16[1,2,4096,128]{3,2,1,0:T(8,128)(2,1)S(1)} %copy-done, bf16[1,2,4096,128]{3,2,1,0:T(8,128)(2,1)S(1)} %copy-done.2, bf16[1,2,4096,128]{3,2,1,0:T(8,128)(2,1)S(1)} %copy-done.4, ...), custom_call_target="tpu_custom_call" | custom-call | flops 134217728 | bytes 6291456 | tf_op jit(solution)/shard_map/p_partial/pallas_call | solution.py:51
  8.7 0.0 collective-permute-start
  8.7 0.0 copy-done.1
  8.7 0.0 copy-done.3
  8.7 0.7 copy-done.5
  9.4 2.5 %p_partial.3 = (bf16[1,2,4096,128]{3,2,1,0:T(8,128)(2,1)}, bf16[2,2048,128]{2,1,0:T(8,128)(2,1)S(1)}, f32[2048,128]{1,0:T(8,128)S(1)}) custom-call(s32[1]{0:T(128)} %bitcast.half_ref, bf16[1,2,4096,128]{3,2,1,0:T(8,128)(2,1)S(1)} %copy-done.1, bf16[1,2,4096,128]{3,2,1,0:T(8,128)(2,1)S(1)} %copy-done.3, ...), custom_call_target="tpu_custom_call", output_to_operand_aliasing={{0}: (5, {})} | custom-call | flops 134217728 | bytes 6291456 | tf_op jit(solution)/shard_map/p_partial/pallas_call | solution.py:51
  11.9 0.0 collective-permute-done
  11.9 0.1 add_convert_fusion
  12.1 18.3 %all_to_all.20.x_ref = bf16[16,128,128]{2,1,0:T(8,128)(2,1)S(1)} all-to-all(bf16[16,128,128]{2,1,0:T(8,128)(2,1)S(1)} %bitcast.7), channel_id=1, replica_groups=mesh['z'=8,'x'=4,'y'=4,'c'=2] {'x','y'}, dimensions={0} | all-to-all | bytes 1048576 | tf_op jit(solution)/shard_map/p_sum/all_to_all | solution.py:239
  30.4 0.1 p_sum.2
  30.5 17.4 %all_to_all.21.x_ref = bf16[8,128,128]{2,1,0:T(8,128)(2,1)S(1)} all-to-all(bf16[8,128,128]{2,1,0:T(8,128)(2,1)S(1)} %p_sum.2), channel_id=1, replica_groups=mesh['z'=8,'x'=4,'y'=4,'c'=2] {'z'}, dimensions={0} | all-to-all | bytes 524288 | tf_op jit(solution)/shard_map/p_sum/all_to_all | solution.py:239
  47.8 0.1 p_sum.3
  47.9 13.6 %all_to_all.22 = bf16[16,128,128]{2,1,0:T(8,128)(2,1)S(1)} all-to-all(bf16[16,128,128]{2,1,0:T(8,128)(2,1)S(1)} %p_sum.3), channel_id=1, replica_groups=mesh['z'=8,'x'=4,'y'=4,'c'=2] {'x','y'}, dimensions={0} | all-to-all | bytes 1048576 | tf_op jit(solution)/shard_map/p_sum/all_to_all | solution.py:239
  61.5 0.0 collective-permute-start.1
  61.5 0.5 u_sum.3
  62.0 1.4 %collective-permute-done.1.p_ref.pt_ref = bf16[2048,128]{1,0:T(8,128)(2,1)S(1)} collective-permute-done((bf16[2048,128]{1,0:T(8,128)(2,1)S(1)}, bf16[2048,128]{1,0:T(8,128)(2,1)S(1)}, u32[]{:S(2)}, u32[]{:S(2)}) %collective-permute-start.1) | collective-permute-done | bytes 524320 | tf_op jit(solution)/shard_map/p_sum/ppermute | solution.py:235
  63.4 0.5 u_sum.4
  63.9 14.9 %all_to_all.23 = bf16[8,128,128]{2,1,0:T(8,128)(2,1)S(1)} all-to-all(bf16[8,128,128]{2,1,0:T(8,128)(2,1)S(1)} %get-tuple-element.26), channel_id=1, replica_groups=mesh['z'=8,'x'=4,'y'=4,'c'=2] {'z'}, dimensions={0} | all-to-all | bytes 524288 | tf_op jit(solution)/shard_map/u_sum/all_to_all | solution.py:239
  78.8 1.2 %collective-permute-start.4 = (bf16[128,128]{1,0:T(8,128)(2,1)S(1)}, bf16[128,128]{1,0:T(8,128)(2,1)S(1)}, u32[]{:S(2)}, u32[]{:S(2)}) collective-permute-start(bf16[128,128]{1,0:T(8,128)(2,1)S(1)} %reduce_sum.12), channel_id=1, source_target_pairs={{0,24},{8,16},{16,8},{24,0},{1,25},{9,17},{17,9},{25,1},{2,26},{10... | collective-permute-start | bytes 98312 | tf_op jit(solution)/shard_map/u_sum/ppermute | solution.py:261
  80.0 0.7 collective-permute-start.3
  80.7 2.3 %collective-permute-start.2 = (bf16[128,128]{1,0:T(8,128)(2,1)S(1)}, bf16[128,128]{1,0:T(8,128)(2,1)S(1)}, u32[]{:S(2)}, u32[]{:S(2)}) collective-permute-start(bf16[128,128]{1,0:T(8,128)(2,1)S(1)} %reduce_sum.12), channel_id=1, source_target_pairs={{0,8},{8,0},{16,24},{24,16},{1,9},{9,1},{17,25},{25,17},{2,10},{10... | collective-permute-start | bytes 98312 | tf_op jit(solution)/shard_map/u_sum/ppermute | solution.py:261
  83.0 5.4 %u_sum.5.l_ref = f32[128,128]{1,0:T(8,128)S(1)} custom-call(f32[128,128]{1,0:T(8,128)S(1)} %get-tuple-element.25.g_ref), custom_call_target="tpu_custom_call" | custom-call | flops 1048576 | bytes 131072 | tf_op jit(solution)/shard_map/u_sum/pallas_call | solution.py:153
  88.4 0.0 collective-permute-done.4
  88.4 0.0 collective-permute-done.3
  88.4 0.0 collective-permute-done.2
  88.5 6.0 %back.1 = (bf16[1,2,4096,128]{3,2,1,0:T(8,128)(2,1)}, bf16[4096,128]{1,0:T(8,128)(2,1)}, f32[128,128]{1,0:T(8,128)}) custom-call(s32[1]{0:T(128)} %bitcast.half_ref, bf16[2048,128]{1,0:T(8,128)(2,1)S(1)} %bitcast.6, bf16[2048,128]{1,0:T(8,128)(2,1)S(1)} %collective-permute-done.1.p_ref.pt_ref, bf16[2,2048,128]{2,1,0:T(8,128)(2,1)S(1)} %get-tuple-element.21.c_ref.co_ref, ...), custom_call_target="tpu_custom_call" | custom-call | flops 402653184 | bytes 8388608 | tf_op jit(solution)/shard_map/back/pallas_call | solution.py:204
  (7 shorter events, 0.1 us)
Async XLA Ops:
  0.6 1.6 %copy-start = (bf16[1,2,4096,128]{3,2,1,0:T(8,128)(2,1)S(1)}, bf16[1,2,4096,128]{3,2,1,0:T(8,128)(2,1)}, u32[]{:S(2)}) copy-start(bf16[1,2,4096,128]{3,2,1,0:T(8,128)(2,1)} %g_ref.3) | copy-start | bytes 6291460
  2.2 1.6 %copy-start.2 = (bf16[1,2,4096,128]{3,2,1,0:T(8,128)(2,1)S(1)}, bf16[1,2,4096,128]{3,2,1,0:T(8,128)(2,1)}, u32[]{:S(2)}) copy-start(bf16[1,2,4096,128]{3,2,1,0:T(8,128)(2,1)} %m_ref.3) | copy-start | bytes 6291460
  3.8 1.6 %copy-start.4 = (bf16[1,2,4096,128]{3,2,1,0:T(8,128)(2,1)S(1)}, bf16[1,2,4096,128]{3,2,1,0:T(8,128)(2,1)}, u32[]{:S(2)}) copy-start(bf16[1,2,4096,128]{3,2,1,0:T(8,128)(2,1)} %e_ref.3) | copy-start | bytes 6291460
  5.4 0.8 copy-start.6
  6.2 2.5 %copy-start.1 = (bf16[1,2,4096,128]{3,2,1,0:T(8,128)(2,1)S(1)}, bf16[1,2,4096,128]{3,2,1,0:T(8,128)(2,1)}, u32[]{:S(2)}) copy-start(bf16[1,2,4096,128]{3,2,1,0:T(8,128)(2,1)} %g_ref.3) | copy-start | bytes 6291460
  6.2 2.5 %copy-start.3 = (bf16[1,2,4096,128]{3,2,1,0:T(8,128)(2,1)S(1)}, bf16[1,2,4096,128]{3,2,1,0:T(8,128)(2,1)}, u32[]{:S(2)}) copy-start(bf16[1,2,4096,128]{3,2,1,0:T(8,128)(2,1)} %m_ref.3) | copy-start | bytes 6291460
  6.2 3.2 %copy-start.5 = (bf16[1,2,4096,128]{3,2,1,0:T(8,128)(2,1)S(1)}, bf16[1,2,4096,128]{3,2,1,0:T(8,128)(2,1)}, u32[]{:S(2)}) copy-start(bf16[1,2,4096,128]{3,2,1,0:T(8,128)(2,1)} %e_ref.3) | copy-start | bytes 6291460
  8.7 3.2 %collective-permute-start = (bf16[2048,128]{1,0:T(8,128)(2,1)S(1)}, bf16[2048,128]{1,0:T(8,128)(2,1)S(1)}, u32[]{:S(2)}, u32[]{:S(2)}) collective-permute-start(bf16[2048,128]{1,0:T(8,128)(2,1)S(1)} %get-tuple-element.20), channel_id=1, source_target_pairs={{0,1},{1,0},{2,3},{3,2},{4,5},{5,4},{6,7},{7,6},{8,9},{9,8},{10,11... | collective-permute-start | bytes 1572872 | tf_op jit(solution)/shard_map/p_partial/ppermute | solution.py:235
  61.5 1.9 %collective-permute-start.1 = (bf16[2048,128]{1,0:T(8,128)(2,1)S(1)}, bf16[2048,128]{1,0:T(8,128)(2,1)S(1)}, u32[]{:S(2)}, u32[]{:S(2)}) collective-permute-start(bf16[2048,128]{1,0:T(8,128)(2,1)S(1)} %bitcast.4), channel_id=1, source_target_pairs={{0,1},{1,0},{2,3},{3,2},{4,5},{5,4},{6,7},{7,6},{8,9},{9,8},{10,11... | collective-permute-start | bytes 1572872 | tf_op jit(solution)/shard_map/p_sum/ppermute | solution.py:235
  78.8 9.6 %collective-permute-start.4 = (bf16[128,128]{1,0:T(8,128)(2,1)S(1)}, bf16[128,128]{1,0:T(8,128)(2,1)S(1)}, u32[]{:S(2)}, u32[]{:S(2)}) collective-permute-start(bf16[128,128]{1,0:T(8,128)(2,1)S(1)} %reduce_sum.12), channel_id=1, source_target_pairs={{0,24},{8,16},{16,8},{24,0},{1,25},{9,17},{17,9},{25,1},{2,26},{10... | collective-permute-start | bytes 98312 | tf_op jit(solution)/shard_map/u_sum/ppermute | solution.py:261
  80.0 8.4 %collective-permute-start.3 = (bf16[128,128]{1,0:T(8,128)(2,1)S(1)}, bf16[128,128]{1,0:T(8,128)(2,1)S(1)}, u32[]{:S(2)}, u32[]{:S(2)}) collective-permute-start(bf16[128,128]{1,0:T(8,128)(2,1)S(1)} %reduce_sum.12), channel_id=1, source_target_pairs={{0,16},{8,24},{16,0},{24,8},{1,17},{9,25},{17,1},{25,9},{2,18},{10... | collective-permute-start | bytes 98312 | tf_op jit(solution)/shard_map/u_sum/ppermute | solution.py:261
  80.7 7.7 %collective-permute-start.2 = (bf16[128,128]{1,0:T(8,128)(2,1)S(1)}, bf16[128,128]{1,0:T(8,128)(2,1)S(1)}, u32[]{:S(2)}, u32[]{:S(2)}) collective-permute-start(bf16[128,128]{1,0:T(8,128)(2,1)S(1)} %reduce_sum.12), channel_id=1, source_target_pairs={{0,8},{8,0},{16,24},{24,16},{1,9},{9,1},{17,25},{25,17},{2,10},{10... | collective-permute-start | bytes 98312 | tf_op jit(solution)/shard_map/u_sum/ppermute | solution.py:261

commit v2 on v1

v2 whole, which is shorter than its diff:
```python
import jax
import jax.numpy as jnp
from jax import lax
from jax.experimental import pallas as pl
from jax.experimental.pallas import tpu as pltpu
from jax.sharding import Mesh
from jax.sharding import PartitionSpec as P

BF, F32 = jnp.bfloat16, jnp.float32
NZ, NX, NY, NC = 8, 4, 4, 2
ROWS, COLS, RANK2 = 4096, 128, 128
HALF = ROWS // NC
BLK = HALF // (NX * NY)
FRONT, PROD, BACK = 1024, 512, 512
PANEL = 8
MIB = 1 << 20


def dot(a, b, dims=((1,), (0,)), precision=None):
    return lax.dot_general(a, b, (dims, ((), ())), precision=precision, preferred_element_type=F32)


def left_lanes(shape):
    return lax.broadcasted_iota(jnp.int32, shape, len(shape) - 1) < RANK2 // 2


def front_body(half_ref, g_hbm, m_hbm, e_hbm, q_hbm, mo_ref, c_ref, p_ref, g_buf, m_buf, e_buf, q_buf, sem, q_sem):
    base = pl.multiple_of(half_ref[0] * HALF, HALF)

    def loads(k):
        here = pl.ds(pl.multiple_of(k * FRONT, FRONT), FRONT)
        there = pl.ds(pl.multiple_of(base + k * FRONT, FRONT), FRONT)
        return [
            pltpu.make_async_copy(hbm.at[0, :, there], buf.at[:, here], sem.at[i, k])
            for i, (hbm, buf) in enumerate(((m_hbm, m_buf), (g_hbm, g_buf), (e_hbm, e_buf)))
        ]

    load_q = pltpu.make_async_copy(q_hbm, q_buf, q_sem)
    load_q.start()
    for k in range(HALF // FRONT):
        for copy in loads(k):
            copy.start()
    load_q.wait()
    q = q_buf[...]
    left = left_lanes(q.shape)
    q_of = [jnp.where(left if group == 0 else ~left, q, jnp.zeros_like(q)) for group in range(2)]

    for k in range(HALF // FRONT):
        for copy in loads(k):
            copy.wait()
        rows = pl.ds(pl.multiple_of(k * FRONT, FRONT), FRONT)
        total = None
        for group in range(2):
            mo = (0.9 * m_buf[group, rows].astype(F32) + g_buf[group, rows].astype(F32)).astype(BF)
            co = (mo.astype(F32) + e_buf[group, rows].astype(F32)).astype(BF)
            mo_ref[group, rows] = mo
            c_ref[group, rows] = co
            term = dot(co, q_of[group])
            total = term if total is None else total + term
        p_ref[rows] = total.astype(p_ref.dtype)


def front(half, args, p_dtype):
    hbm, vmem = pl.BlockSpec(memory_space=pltpu.HBM), pl.BlockSpec(memory_space=pltpu.VMEM)
    return pl.pallas_call(
        front_body,
        in_specs=[pl.BlockSpec(memory_space=pltpu.SMEM)] + [hbm] * 4,
        out_specs=[vmem] * 3,
        out_shape=[pltpu.VMEM((2, HALF, COLS), BF), pltpu.VMEM((2, HALF, COLS), BF), pltpu.VMEM((HALF, RANK2), p_dtype)],
        scratch_shapes=[pltpu.VMEM((2, HALF, COLS), BF)] * 3
        + [pltpu.VMEM((COLS, RANK2), BF), pltpu.SemaphoreType.DMA((3, HALF // FRONT)), pltpu.SemaphoreType.DMA],
        compiler_params=pltpu.CompilerParams(vmem_limit_bytes=16 * MIB),
        cost_estimate=pl.CostEstimate(flops=2 * HALF * 256 * 128, bytes_accessed=4 * MIB, transcendentals=0),
    )(half, *(pltpu.with_memory_space_constraint(x, pltpu.HBM) for x in args))


def sum_copies_body(x_ref, o_ref):
    total = x_ref[0].astype(F32)
    for k in range(1, x_ref.shape[0]):
        total = total + x_ref[k].astype(F32)
    total = total.astype(BF)
    for k in range(o_ref.shape[0]):
        o_ref[k] = total


def sum_copies(x, copies):
    return pl.pallas_call(
        sum_copies_body,
        out_shape=jax.ShapeDtypeStruct((copies, *x.shape[1:]), BF),
        compiler_params=pltpu.CompilerParams(vmem_limit_bytes=16 * MIB),
    )(x)


def products_body(p_ref, c_ref, *rest):
    u_ref, g_ref = rest[-2:]
    n = RANK2 // 2
    u0 = u1 = gram = None
    for k in range(HALF // PROD):
        rows = pl.ds(k * PROD, PROD)
        p = p_ref[rows]
        pt = p.T
        a, b, c = dot(pt[:n], c_ref[0, rows]), dot(pt[n:], c_ref[1, rows]), dot(pt, p)
        u0, u1, gram = (a, b, c) if u0 is None else (u0 + a, u1 + b, gram + c)
    u = jnp.concatenate([u0, u1], axis=0)
    if len(rest) == 2:
        u_ref[...] = u
        g_ref[...] = gram
    else:
        u = (u + rest[0][...]).astype(BF)
        for k in range(NZ):
            u_ref[k] = u
        g_ref[...] = gram + rest[1][...]


def products(p, c, before):
    last = before is not None
    return pl.pallas_call(
        products_body,
        out_shape=[
            jax.ShapeDtypeStruct((NZ, RANK2, COLS) if last else (RANK2, COLS), BF if last else F32),
            jax.ShapeDtypeStruct((RANK2, RANK2), F32),
        ],
        compiler_params=pltpu.CompilerParams(vmem_limit_bytes=16 * MIB),
        cost_estimate=pl.CostEstimate(flops=2 * HALF * 256 * 128, bytes_accessed=2 * MIB, transcendentals=0),
    )(p, c, *(before if last else ()))


def inverse_rows(g_ref):
    n, t = RANK2 // 2, PANEL
    tiles = n // t
    lane = lax.broadcasted_iota(jnp.int32, (t, 2 * n), 1)
    sub = lax.broadcasted_iota(jnp.int32, (t, 2 * n), 0)
    left = lane < n

    def spread(x):
        return jnp.broadcast_to(x, (t, 2 * n))

    both, pivots = [], [[None] * tiles for _ in range(2)]
    for s in range(2):
        own = []
        for i in range(tiles):
            x = g_ref[s * n + t * i : s * n + t * i + t]
            x = pltpu.roll(x, n, 1) if s else x
            own.append(jnp.where(left, x, jnp.where(lane == sub + (t * i + n), 1.0, 0.0)))
        both.append(own)
    for top in range(tiles):
        columns = [
            [[spread(a[i][:, top * t + j : top * t + j + 1]) if i >= top else None for i in range(tiles)] for j in range(t)]
            for a in both
        ]
        for j in range(t):
            for s in range(2):
                c, a = columns[s], both[s]
                d = spread(c[j][top][j : j + 1])
                pivots[s][top] = d if j == 0 else jnp.where(sub == j, d, pivots[s][top])
                scale = 1.0 / d
                row = spread(a[top][j : j + 1])
                later = [spread(c[j][top][q : q + 1]) for q in range(j + 1, t)]
                for i in range(top, tiles):
                    factor = c[j][i] * scale
                    if i == top:
                        factor = jnp.where(sub > j, factor, 0.0)
                    for q, value in enumerate(later, j + 1):
                        c[q][i] = c[q][i] - factor * value
                    a[i] = a[i] - factor * row
    out = []
    for s in range(2):
        for i in range(tiles):
            y = both[s][i] * lax.rsqrt(pivots[s][i])
            out.append(jnp.where(left, 0.0, y) if s else jnp.where(left, pltpu.roll(y, n, 1), 0.0))
    return out


def factor_body(half_ref, g_ref, po_ref, pt_ref, mo_ref, mt_ref, m_hbm, p_hbm, f_ref, l_ref, w_ref, sem, m_sem):
    halves = [pl.multiple_of(h * HALF, HALF) for h in (half_ref[0], 1 - half_ref[0])]
    moves = [
        pltpu.make_async_copy(ref, m_hbm.at[0, :, pl.ds(halves[i], HALF)], m_sem.at[i]) for i, ref in enumerate((mo_ref, mt_ref))
    ]
    for copy in moves:
        copy.start()
    for i, rows in enumerate(inverse_rows(g_ref)):
        l_ref[i * PANEL : (i + 1) * PANEL] = rows
    inv_t = l_ref[...].T
    hi = inv_t.astype(BF)
    w_ref[:RANK2] = hi
    w_ref[RANK2:] = (inv_t - hi.astype(F32)).astype(BF)
    weights = w_ref[...]
    for which, p_ref in enumerate((po_ref, pt_ref)):
        moves.append(pltpu.make_async_copy(f_ref.at[pl.ds(which * HALF, HALF)], p_hbm.at[pl.ds(halves[which], HALF)], sem.at[which]))

        for k in range(HALF // BACK):
            p = p_ref[pl.ds(pl.multiple_of(k * BACK, BACK), BACK)]
            here = pl.ds(pl.multiple_of(which * HALF + k * BACK, BACK), BACK)
            f_ref[here] = dot(jnp.concatenate([p, p], axis=1), weights).astype(BF)

        moves[-1].start()
    for copy in moves:
        copy.wait()


def factor(half, gram, p_own, p_other, mo_own, mo_other):
    hbm, vmem = pl.BlockSpec(memory_space=pltpu.HBM), pl.BlockSpec(memory_space=pltpu.VMEM)
    return pl.pallas_call(
        factor_body,
        in_specs=[pl.BlockSpec(memory_space=pltpu.SMEM)] + [vmem] * 5,
        out_specs=[hbm, hbm, vmem, vmem],
        out_shape=[
            jax.ShapeDtypeStruct((1, 2, ROWS, COLS), BF),
            jax.ShapeDtypeStruct((ROWS, RANK2), BF),
            jax.ShapeDtypeStruct((ROWS, RANK2), BF),
            jax.ShapeDtypeStruct((RANK2, RANK2), F32),
        ],
        scratch_shapes=[pltpu.VMEM((2 * RANK2, RANK2), BF), pltpu.SemaphoreType.DMA((2,)), pltpu.SemaphoreType.DMA((2,))],
        compiler_params=pltpu.CompilerParams(vmem_limit_bytes=16 * MIB),
        cost_estimate=pl.CostEstimate(flops=4 * ROWS * 128 * 128, bytes_accessed=4 * MIB, transcendentals=128),
    )(half, gram, p_own, p_other, mo_own, mo_other)


def back_body(half_ref, f_ref, co_ref, ct_ref, l_ref, u_ref, a_ref, b_ref, d_ref, e_hbm, q_ref, e_buf, w_ref, sem):
    u, a, b, d = (t[...].astype(F32) for t in (u_ref, a_ref, b_ref, d_ref))
    qt = dot(l_ref[...], (u + a) + (b + d), precision=lax.Precision.HIGHEST) * (1.0 / (NZ * NX))
    q_ref[...] = qt.T
    qt = qt.astype(BF)
    top = lax.broadcasted_iota(jnp.int32, qt.shape, 0) < RANK2 // 2
    zero = jnp.zeros_like(qt)
    w_ref[...] = jnp.concatenate([jnp.where(top, qt, zero), jnp.where(top, zero, qt)], axis=1)
    weights = w_ref[...]

    def store(which, k):
        half = half_ref[0] if which == 0 else 1 - half_ref[0]
        here = pl.ds(pl.multiple_of(which * HALF + k * BACK, BACK), BACK)
        there = pl.ds(pl.multiple_of(half * HALF + k * BACK, BACK), BACK)
        return here, pltpu.make_async_copy(e_buf.at[:, here], e_hbm.at[0, :, there], sem.at[which, k])

    for which, c_ref in enumerate((co_ref, ct_ref)):

        for k in range(HALF // BACK):
            here, copy = store(which, k)
            approx = dot(f_ref[here], weights)
            for group in range(2):
                c = c_ref[group, pl.ds(pl.multiple_of(k * BACK, BACK), BACK)].astype(F32)
                e_buf[group, here] = (c - approx[:, group * COLS : (group + 1) * COLS]).astype(BF)
            copy.start()

    for which in range(2):

        for k in range(HALF // BACK):
            store(which, k)[1].wait()


def back(half, f, c_own, c_other, inv, us):
    vmem = pl.BlockSpec(memory_space=pltpu.VMEM)
    return pl.pallas_call(
        back_body,
        in_specs=[pl.BlockSpec(memory_space=pltpu.SMEM)] + [vmem] * 8,
        out_specs=[pl.BlockSpec(memory_space=pltpu.HBM), vmem],
        out_shape=[
            jax.ShapeDtypeStruct((1, 2, ROWS, COLS), BF),
            jax.ShapeDtypeStruct((COLS, RANK2), F32),
        ],
        scratch_shapes=[
            pltpu.VMEM((2, ROWS, COLS), BF),
            pltpu.VMEM((RANK2, 2 * COLS), BF),
            pltpu.SemaphoreType.DMA((2, HALF // BACK)),
        ],
        compiler_params=pltpu.CompilerParams(vmem_limit_bytes=16 * MIB),
        cost_estimate=pl.CostEstimate(flops=4 * ROWS * 128 * 128, bytes_accessed=6 * MIB, transcendentals=0),
    )(half, f, c_own, c_other, inv, *us)


def swap_cores(x):
    return lax.ppermute(x, "c", [(0, 1), (1, 0)])


def exchange(x, axes):
    return lax.all_to_all(x, axes, 0, 0)


def local(grads, momentum, error, q_warm):
    c = lax.axis_index("c").astype(jnp.int32)
    mine, theirs = c.reshape(1), (1 - c).reshape(1)

    with jax.named_scope("p_partial"):
        args = (grads, momentum, error, q_warm)
        mo_other, c_other, p_send = front(theirs, args, BF)
        p_got = swap_cores(p_send)
        mo_own, c_own, p_own = front(mine, args, F32)
        chip = (p_own + p_got.astype(F32)).astype(BF)
    with jax.named_scope("p_sum"):
        parts = exchange(chip.reshape(NX * NY, BLK, RANK2), ("x", "y"))
        parts = exchange(sum_copies(parts, NZ), "z")
        p_mine = exchange(sum_copies(parts, NX * NY), ("x", "y")).reshape(HALF, RANK2)
        p_theirs = swap_cores(p_mine)
    with jax.named_scope("u_sum"):
        first = products(p_mine, c_own, None)
        copies, gram = products(p_theirs, c_other, first)
        parts = exchange(copies, "z")
        u = sum_copies(parts, 1)[0]
        got = [lax.ppermute(u, "x", [(i, i ^ k) for i in range(NX)]) for k in (1, 2, 3)]
        momentum_out, p_factor, f, inv = factor(mine, gram, p_mine, p_theirs, mo_own, mo_other)
    with jax.named_scope("back"):
        error_out, q_factor = back(mine, f, c_own, c_other, inv, (u, *got))
    return momentum_out, error_out, p_factor, q_factor


def solution(mesh):
    fine = Mesh(mesh.devices.reshape(NZ, NX, NY, NC), ("z", "x", "y", "c"))
    dp, tensor = ("z", "x"), ("y", "c")
    big = P(dp, None, None, tensor)
    return jax.shard_map(
        local,
        mesh=fine,
        in_specs=(big, big, big, P(tensor, None)),
        out_specs=(big, big, P(), P(tensor, None)),
        check_vma=False,
    )
```

time: 96.4 us -> 87.2 us (0.905)
  the two profiles are of different devices: /device:TPU:32 before, /device:TPU:1 now
where the time goes in v2:
time: 87.2 us; the launch traced here: 86.9 us
  blocking collectives  60.9 us (70%)
  Pallas kernels  13.3 us (15%)
  starting transfers between devices  10.8 us (12%)
  waiting for transfers between devices  1.06 us (1%)
    all_to_all x4, blocking collectives, exchange(): return lax.all_to_all(x, axes, 0, 0)  60.9 us
    ppermute x2, starting transfers between devices, swap_cores(): return lax.ppermute(x, 'c', [(0, 1), (1, 0)])  7.5 us
    pallas_call x2, Pallas kernels, front(): pl.pallas_call(front_body, in_specs=[pl.BlockSpec(memory_space=pltpu.SMEM...  4.86 us
    pallas_call x1, Pallas kernels, factor(): pl.pallas_call(factor_body, in_specs=[pl.BlockSpec(memory_space=pltpu.SME...  4.76 us
    ppermute x3, starting transfers between devices, local(): lax.ppermute(u, 'x', [(i, i ^ k) for i in range(NX)])  3.34 us
    pallas_call x1, Pallas kernels, back(): pl.pallas_call(back_body, in_specs=[pl.BlockSpec(memory_space=pltpu.SMEM)...  2.55 us
  transfers between devices with their start and end apart: 5, of which 1 were waited for; matrix products, arithmetic and copies ran while one was open for 0% of the time, Pallas kernels for 9%

profile of v2, /device:TPU:1, one launch (start us, length us, event | category | flops | bytes accessed | tf_op | source)
XLA Modules:
  0.0 86.9 jit_solution(5334806456419898634)
XLA Ops:
  0.6 2.4 %p_partial.3 = (bf16[2,2048,128]{2,1,0:T(8,128)(2,1)S(1)}, bf16[2,2048,128]{2,1,0:T(8,128)(2,1)S(1)}, bf16[2048,128]{1,0:T(8,128)(2,1)S(1)}) custom-call(s32[1]{0:T(128)} %bitcast.1.half_ref, bf16[1,2,4096,128]{3,2,1,0:T(8,128)(2,1)} %g_hbm.3, bf16[1,2,4096,128]{3,2,1,0:T(8,128)(2,1)} %m_hbm.3, bf16[1,2,4096,128]{3,2,1,0:T(8,128)(2,1)} %e_hbm.3, ...), custom_call_target="tpu_custom_call" | custom-call | flops 134217728 | bytes 4194304 | tf_op jit(solution)/shard_map/p_partial/pallas_call | solution.py:65
  3.1 3.3 %collective-permute-start = (bf16[2048,128]{1,0:T(8,128)(2,1)S(1)}, bf16[2048,128]{1,0:T(8,128)(2,1)S(1)}, u32[]{:S(2)}, u32[]{:S(2)}) collective-permute-start(bf16[2048,128]{1,0:T(8,128)(2,1)S(1)} %get-tuple-element.21), channel_id=1, source_target_pairs={{0,1},{1,0},{2,3},{3,2},{4,5},{5,4},{6,7},{7,6},{8,9},{9,8},{10,11... | collective-permute-start | bytes 1572872 | tf_op jit(solution)/shard_map/p_partial/ppermute | solution.py:272
  6.4 2.4 %p_partial.2 = (bf16[2,2048,128]{2,1,0:T(8,128)(2,1)S(1)}, bf16[2,2048,128]{2,1,0:T(8,128)(2,1)S(1)}, f32[2048,128]{1,0:T(8,128)S(1)}) custom-call(s32[1]{0:T(128)} %bitcast.half_ref, bf16[1,2,4096,128]{3,2,1,0:T(8,128)(2,1)} %g_hbm.3, bf16[1,2,4096,128]{3,2,1,0:T(8,128)(2,1)} %m_hbm.3, bf16[1,2,4096,128]{3,2,1,0:T(8,128)(2,1)} %e_hbm.3, bf16[128,128]{1,0:T(8,128)(2,1)} %q_hbm.3), custom_call_target="tpu_custom_call" | custom-call | flops 134217728 | bytes 4194304 | tf_op jit(solution)/shard_map/p_partial/pallas_call | solution.py:65
  8.8 0.0 collective-permute-done
  8.8 0.1 add_convert_fusion
  9.0 15.0 %all_to_all.20.x_ref = bf16[16,128,128]{2,1,0:T(8,128)(2,1)S(1)} all-to-all(bf16[16,128,128]{2,1,0:T(8,128)(2,1)S(1)} %bitcast.12), channel_id=1, replica_groups=mesh['z'=8,'x'=4,'y'=4,'c'=2] {'x','y'}, dimensions={0} | all-to-all | bytes 1048576 | tf_op jit(solution)/shard_map/p_sum/all_to_all | solution.py:276
  23.9 0.1 p_sum.2
  24.0 17.4 %all_to_all.21.x_ref = bf16[8,128,128]{2,1,0:T(8,128)(2,1)S(1)} all-to-all(bf16[8,128,128]{2,1,0:T(8,128)(2,1)S(1)} %p_sum.2), channel_id=1, replica_groups=mesh['z'=8,'x'=4,'y'=4,'c'=2] {'z'}, dimensions={0} | all-to-all | bytes 524288 | tf_op jit(solution)/shard_map/p_sum/all_to_all | solution.py:276
  41.4 0.1 p_sum.3
  41.4 13.8 %all_to_all.22 = bf16[16,128,128]{2,1,0:T(8,128)(2,1)S(1)} all-to-all(bf16[16,128,128]{2,1,0:T(8,128)(2,1)S(1)} %p_sum.3), channel_id=1, replica_groups=mesh['z'=8,'x'=4,'y'=4,'c'=2] {'x','y'}, dimensions={0} | all-to-all | bytes 1048576 | tf_op jit(solution)/shard_map/p_sum/all_to_all | solution.py:276
  55.2 4.2 %collective-permute-start.1 = (bf16[2048,128]{1,0:T(8,128)(2,1)S(1)}, bf16[2048,128]{1,0:T(8,128)(2,1)S(1)}, u32[]{:S(2)}, u32[]{:S(2)}) collective-permute-start(bf16[2048,128]{1,0:T(8,128)(2,1)S(1)} %bitcast.5), channel_id=1, source_target_pairs={{0,1},{1,0},{2,3},{3,2},{4,5},{5,4},{6,7},{7,6},{8,9},{9,8},{10,11... | collective-permute-start | bytes 1572872 | tf_op jit(solution)/shard_map/p_sum/ppermute | solution.py:272
  59.4 0.5 u_sum.4
  59.9 1.1 %collective-permute-done.1.p_ref.pt_ref = bf16[2048,128]{1,0:T(8,128)(2,1)S(1)} collective-permute-done((bf16[2048,128]{1,0:T(8,128)(2,1)S(1)}, bf16[2048,128]{1,0:T(8,128)(2,1)S(1)}, u32[]{:S(2)}, u32[]{:S(2)}) %collective-permute-start.1) | collective-permute-done | bytes 524320 | tf_op jit(solution)/shard_map/p_sum/ppermute | solution.py:272
  60.9 0.5 u_sum.5
  61.4 14.8 %all_to_all.23.x_ref = bf16[8,128,128]{2,1,0:T(8,128)(2,1)S(1)} all-to-all(bf16[8,128,128]{2,1,0:T(8,128)(2,1)S(1)} %get-tuple-element.32), channel_id=1, replica_groups=mesh['z'=8,'x'=4,'y'=4,'c'=2] {'z'}, dimensions={0} | all-to-all | bytes 524288 | tf_op jit(solution)/shard_map/u_sum/all_to_all | solution.py:276
  76.2 0.9 %collective-permute-start.4 = (bf16[128,128]{1,0:T(8,128)(2,1)S(1)}, bf16[128,128]{1,0:T(8,128)(2,1)S(1)}, u32[]{:S(2)}, u32[]{:S(2)}) collective-permute-start(bf16[128,128]{1,0:T(8,128)(2,1)S(1)} %bitcast.8), channel_id=1, source_target_pairs={{0,24},{8,16},{16,8},{24,0},{1,25},{9,17},{17,9},{25,1},{2,26},{10... | collective-permute-start | bytes 98312 | tf_op jit(solution)/shard_map/u_sum/ppermute | solution.py:299
  77.2 0.4 collective-permute-start.3
  77.6 2.0 %collective-permute-start.2 = (bf16[128,128]{1,0:T(8,128)(2,1)S(1)}, bf16[128,128]{1,0:T(8,128)(2,1)S(1)}, u32[]{:S(2)}, u32[]{:S(2)}) collective-permute-start(bf16[128,128]{1,0:T(8,128)(2,1)S(1)} %bitcast.10), channel_id=1, source_target_pairs={{0,8},{8,0},{16,24},{24,16},{1,9},{9,1},{17,25},{25,17},{2,10},{10... | collective-permute-start | bytes 98312 | tf_op jit(solution)/shard_map/u_sum/ppermute | solution.py:299
  79.6 4.8 %u_sum.6 = (bf16[1,2,4096,128]{3,2,1,0:T(8,128)(2,1)}, bf16[4096,128]{1,0:T(8,128)(2,1)}, bf16[4096,128]{1,0:T(8,128)(2,1)S(1)}, f32[128,128]{1,0:T(8,128)S(1)}) custom-call(s32[1]{0:T(128)} %bitcast.half_ref, f32[128,128]{1,0:T(8,128)S(1)} %get-tuple-element.26.g_ref, bf16[2048,128]{1,0:T(8,128)(2,1)S(1)} %bitcast.7, ...), custom_call_target="tpu_custom_call" | custom-call | flops 268435456 | bytes 4194304 | tf_op jit(solution)/shard_map/u_sum/pallas_call | solution.py:203
  84.3 0.0 collective-permute-done.4.d_ref
  84.4 0.0 collective-permute-done.3.b_ref
  84.4 0.0 collective-permute-done.2.a_ref
  84.4 2.6 %back.1 = (bf16[1,2,4096,128]{3,2,1,0:T(8,128)(2,1)}, f32[128,128]{1,0:T(8,128)}) custom-call(s32[1]{0:T(128)} %bitcast.half_ref, bf16[4096,128]{1,0:T(8,128)(2,1)S(1)} %get-tuple-element.30.f_ref, bf16[2,2048,128]{2,1,0:T(8,128)(2,1)S(1)} %get-tuple-element.23.c_ref.co_ref, bf16[2,2048,128]{2,1,0:T(8,128)(2,1)S(1)} %get-tuple-element.22.c_ref.ct_ref, ...), custom_call_target="tpu_custom_call" | custom-call | flops 268435456 | bytes 6291456 | tf_op jit(solution)/shard_map/back/pallas_call | solution.py:253
  (1 shorter events, 0.0 us)
Async XLA Ops:
  3.1 5.8 %collective-permute-start = (bf16[2048,128]{1,0:T(8,128)(2,1)S(1)}, bf16[2048,128]{1,0:T(8,128)(2,1)S(1)}, u32[]{:S(2)}, u32[]{:S(2)}) collective-permute-start(bf16[2048,128]{1,0:T(8,128)(2,1)S(1)} %get-tuple-element.21), channel_id=1, source_target_pairs={{0,1},{1,0},{2,3},{3,2},{4,5},{5,4},{6,7},{7,6},{8,9},{9,8},{10,11... | collective-permute-start | bytes 1572872 | tf_op jit(solution)/shard_map/p_partial/ppermute | solution.py:272
  55.2 5.7 %collective-permute-start.1 = (bf16[2048,128]{1,0:T(8,128)(2,1)S(1)}, bf16[2048,128]{1,0:T(8,128)(2,1)S(1)}, u32[]{:S(2)}, u32[]{:S(2)}) collective-permute-start(bf16[2048,128]{1,0:T(8,128)(2,1)S(1)} %bitcast.5), channel_id=1, source_target_pairs={{0,1},{1,0},{2,3},{3,2},{4,5},{5,4},{6,7},{7,6},{8,9},{9,8},{10,11... | collective-permute-start | bytes 1572872 | tf_op jit(solution)/shard_map/p_sum/ppermute | solution.py:272
  76.2 8.1 %collective-permute-start.4 = (bf16[128,128]{1,0:T(8,128)(2,1)S(1)}, bf16[128,128]{1,0:T(8,128)(2,1)S(1)}, u32[]{:S(2)}, u32[]{:S(2)}) collective-permute-start(bf16[128,128]{1,0:T(8,128)(2,1)S(1)} %bitcast.8), channel_id=1, source_target_pairs={{0,24},{8,16},{16,8},{24,0},{1,25},{9,17},{17,9},{25,1},{2,26},{10... | collective-permute-start | bytes 98312 | tf_op jit(solution)/shard_map/u_sum/ppermute | solution.py:299
  77.2 7.2 %collective-permute-start.3 = (bf16[128,128]{1,0:T(8,128)(2,1)S(1)}, bf16[128,128]{1,0:T(8,128)(2,1)S(1)}, u32[]{:S(2)}, u32[]{:S(2)}) collective-permute-start(bf16[128,128]{1,0:T(8,128)(2,1)S(1)} %bitcast.9), channel_id=1, source_target_pairs={{0,16},{8,24},{16,0},{24,8},{1,17},{9,25},{17,1},{25,9},{2,18},{10... | collective-permute-start | bytes 98312 | tf_op jit(solution)/shard_map/u_sum/ppermute | solution.py:299
  77.6 6.8 %collective-permute-start.2 = (bf16[128,128]{1,0:T(8,128)(2,1)S(1)}, bf16[128,128]{1,0:T(8,128)(2,1)S(1)}, u32[]{:S(2)}, u32[]{:S(2)}) collective-permute-start(bf16[128,128]{1,0:T(8,128)(2,1)S(1)} %bitcast.10), channel_id=1, source_target_pairs={{0,8},{8,0},{16,24},{24,16},{1,9},{9,1},{17,25},{25,17},{2,10},{10... | collective-permute-start | bytes 98312 | tf_op jit(solution)/shard_map/u_sum/ppermute | solution.py:299

commit v3 on v2

--- a/solution.py
+++ b/solution.py
@@ -106,9 +106,7 @@
         u_ref[...] = u
         g_ref[...] = gram
     else:
-        u = (u + rest[0][...]).astype(BF)
-        for k in range(NZ):
-            u_ref[k] = u
+        u_ref[...] = (u + rest[0][...]).astype(BF)
         g_ref[...] = gram + rest[1][...]
 
 
@@ -117,7 +115,7 @@
     return pl.pallas_call(
         products_body,
         out_shape=[
-            jax.ShapeDtypeStruct((NZ, RANK2, COLS) if last else (RANK2, COLS), BF if last else F32),
+            jax.ShapeDtypeStruct((RANK2, COLS), BF if last else F32),
             jax.ShapeDtypeStruct((RANK2, RANK2), F32),
         ],
         compiler_params=pltpu.CompilerParams(vmem_limit_bytes=16 * MIB),
@@ -125,7 +123,7 @@
     )(p, c, *(before if last else ()))
 
 
-def inverse_rows(g_ref):
+def invert(g_ref, o_ref):
     n, t = RANK2 // 2, PANEL
     tiles = n // t
     lane = lax.broadcasted_iota(jnp.int32, (t, 2 * n), 1)
@@ -135,85 +133,97 @@
     def spread(x):
         return jnp.broadcast_to(x, (t, 2 * n))
 
-    both, pivots = [], [[None] * tiles for _ in range(2)]
+    both = []
     for s in range(2):
-        own = []
         for i in range(tiles):
             x = g_ref[s * n + t * i : s * n + t * i + t]
             x = pltpu.roll(x, n, 1) if s else x
-            own.append(jnp.where(left, x, jnp.where(lane == sub + (t * i + n), 1.0, 0.0)))
-        both.append(own)
+            both.append(jnp.where(left, x, jnp.where(lane == sub + (t * i + n), 1.0, 0.0)))
+
     for top in range(tiles):
-        columns = [
-            [[spread(a[i][:, top * t + j : top * t + j + 1]) if i >= top else None for i in range(tiles)] for j in range(t)]
-            for a in both
-        ]
-        for j in range(t):
-            for s in range(2):
-                c, a = columns[s], both[s]
-                d = spread(c[j][top][j : j + 1])
-                pivots[s][top] = d if j == 0 else jnp.where(sub == j, d, pivots[s][top])
+        first, live, out = top * t, tiles - top, []
+        for s in range(2):
+            a = list(both[s * live : (s + 1) * live])
+            forward = full = a[0]
+            c = [spread(full[:, first + j : first + j + 1]) for j in range(t)]
+            pivots = None
+            for j in range(t):
+                d = spread(c[j][j : j + 1])
+                pivots = d if j == 0 else jnp.where(sub == j, d, pivots)
                 scale = 1.0 / d
-                row = spread(a[top][j : j + 1])
-                later = [spread(c[j][top][q : q + 1]) for q in range(j + 1, t)]
-                for i in range(top, tiles):
-                    factor = c[j][i] * scale
-                    if i == top:
-                        factor = jnp.where(sub > j, factor, 0.0)
-                    for q, value in enumerate(later, j + 1):
-                        c[q][i] = c[q][i] - factor * value
-                    a[i] = a[i] - factor * row
-    out = []
-    for s in range(2):
-        for i in range(tiles):
-            y = both[s][i] * lax.rsqrt(pivots[s][i])
-            out.append(jnp.where(left, 0.0, y) if s else jnp.where(left, pltpu.roll(y, n, 1), 0.0))
-    return out
-
-
-def factor_body(half_ref, g_ref, po_ref, pt_ref, mo_ref, mt_ref, m_hbm, p_hbm, f_ref, l_ref, w_ref, sem, m_sem):
-    halves = [pl.multiple_of(h * HALF, HALF) for h in (half_ref[0], 1 - half_ref[0])]
-    moves = [
-        pltpu.make_async_copy(ref, m_hbm.at[0, :, pl.ds(halves[i], HALF)], m_sem.at[i]) for i, ref in enumerate((mo_ref, mt_ref))
-    ]
-    for copy in moves:
-        copy.start()
-    for i, rows in enumerate(inverse_rows(g_ref)):
-        l_ref[i * PANEL : (i + 1) * PANEL] = rows
+                factor = c[j] * scale
+                row = spread(forward[j : j + 1])
+                full = jnp.where(sub == j, row * scale, full - factor * row)
+                forward = forward - jnp.where(sub > j, factor, 0.0) * row
+                for q in range(j + 1, t):
+                    value = spread(c[j][q : q + 1])
+                    c[q] = jnp.where(sub == j, value * scale, c[q] - factor * value)
+            y = forward * lax.rsqrt(pivots)
+            o_ref[pl.ds(s * n + first, t)] = jnp.where(left, 0.0, y) if s else jnp.where(left, pltpu.roll(y, n, 1), 0.0)
+            solved = [spread(full[j : j + 1]) for j in range(t)]
+            for x in a[1:]:
+                columns = [spread(x[:, first + j : first + j + 1]) for j in range(t)]
+                for j in range(t):
+                    x = x - columns[j] * solved[j]
+                out.append(x)
+        both = out
+
+
+def inverse_body(half_ref, g_ref, mo_ref, mt_ref, o_ref, m_hbm, sem):
+    copies = []
+    for i, ref in enumerate((mo_ref, mt_ref)):
+        half = half_ref[0] if i == 0 else 1 - half_ref[0]
+        there = pl.ds(pl.multiple_of(half * HALF, HALF), HALF)
+        copies.append(pltpu.make_async_copy(ref, m_hbm.at[0, :, there], sem.at[i]))
+        copies[-1].start()
+    invert(g_ref, o_ref)
+    for copy in copies:
+        copy.wait()
+
+
+def inverse(half, gram, mo_own, mo_other):
+    vmem = pl.BlockSpec(memory_space=pltpu.VMEM)
+    return pl.pallas_call(
+        inverse_body,
+        in_specs=[pl.BlockSpec(memory_space=pltpu.SMEM), vmem, vmem, vmem],
+        out_specs=[vmem, pl.BlockSpec(memory_space=pltpu.HBM)],
+        out_shape=[jax.ShapeDtypeStruct((RANK2, RANK2), F32), jax.ShapeDtypeStruct((1, 2, ROWS, COLS), BF)],
+        scratch_shapes=[pltpu.SemaphoreType.DMA((2,))],
+        compiler_params=pltpu.CompilerParams(vmem_limit_bytes=16 * MIB),
+        cost_estimate=pl.CostEstimate(flops=64**3, bytes_accessed=6 * MIB, transcendentals=128),
+    )(half, gram, mo_own, mo_other)
+
+
+def factor_body(half_ref, l_ref, po_ref, pt_ref, p_hbm, f_ref, w_ref, sem):
     inv_t = l_ref[...].T
     hi = inv_t.astype(BF)
     w_ref[:RANK2] = hi
     w_ref[RANK2:] = (inv_t - hi.astype(F32)).astype(BF)
     weights = w_ref[...]
+    moves = []
     for which, p_ref in enumerate((po_ref, pt_ref)):
-        moves.append(pltpu.make_async_copy(f_ref.at[pl.ds(which * HALF, HALF)], p_hbm.at[pl.ds(halves[which], HALF)], sem.at[which]))
-
+        half = half_ref[0] if which == 0 else 1 - half_ref[0]
         for k in range(HALF // BACK):
-            p = p_ref[pl.ds(pl.multiple_of(k * BACK, BACK), BACK)]
-            here = pl.ds(pl.multiple_of(which * HALF + k * BACK, BACK), BACK)
-            f_ref[here] = dot(jnp.concatenate([p, p], axis=1), weights).astype(BF)
-
+            p = p_ref[pl.ds(k * BACK, BACK)]
+            f_ref[pl.ds(which * HALF + k * BACK, BACK)] = dot(jnp.concatenate([p, p], axis=1), weights).astype(BF)
+        there = pl.ds(pl.multiple_of(half * HALF, HALF), HALF)
+        moves.append(pltpu.make_async_copy(f_ref.at[pl.ds(which * HALF, HALF)], p_hbm.at[there], sem.at[which]))
         moves[-1].start()
     for copy in moves:
         copy.wait()
 
 
-def factor(half, gram, p_own, p_other, mo_own, mo_other):
+def factor(half, inv, p_own, p_other):
     hbm, vmem = pl.BlockSpec(memory_space=pltpu.HBM), pl.BlockSpec(memory_space=pltpu.VMEM)
     return pl.pallas_call(
         factor_body,
-        in_specs=[pl.BlockSpec(memory_space=pltpu.SMEM)] + [vmem] * 5,
-        out_specs=[hbm, hbm, vmem, vmem],
-        out_shape=[
-            jax.ShapeDtypeStruct((1, 2, ROWS, COLS), BF),
-            jax.ShapeDtypeStruct((ROWS, RANK2), BF),
-            jax.ShapeDtypeStruct((ROWS, RANK2), BF),
-            jax.ShapeDtypeStruct((RANK2, RANK2), F32),
-        ],
-        scratch_shapes=[pltpu.VMEM((2 * RANK2, RANK2), BF), pltpu.SemaphoreType.DMA((2,)), pltpu.SemaphoreType.DMA((2,))],
-        compiler_params=pltpu.CompilerParams(vmem_limit_bytes=16 * MIB),
-        cost_estimate=pl.CostEstimate(flops=4 * ROWS * 128 * 128, bytes_accessed=4 * MIB, transcendentals=128),
-    )(half, gram, p_own, p_other, mo_own, mo_other)
+        in_specs=[pl.BlockSpec(memory_space=pltpu.SMEM)] + [vmem] * 3,
+        out_specs=[hbm, vmem],
+        out_shape=[jax.ShapeDtypeStruct((ROWS, RANK2), BF), pltpu.VMEM((ROWS, RANK2), BF)],
+        scratch_shapes=[pltpu.VMEM((2 * RANK2, RANK2), BF), pltpu.SemaphoreType.DMA((2,))],
+        compiler_params=pltpu.CompilerParams(vmem_limit_bytes=16 * MIB),
+        cost_estimate=pl.CostEstimate(flops=4 * ROWS * 128 * 128, bytes_accessed=6 * MIB, transcendentals=0),
+    )(half, inv, p_own, p_other)
 
 
 def back_body(half_ref, f_ref, co_ref, ct_ref, l_ref, u_ref, a_ref, b_ref, d_ref, e_hbm, q_ref, e_buf, w_ref, sem):
@@ -270,6 +280,14 @@
 
 def swap_cores(x):
     return lax.ppermute(x, "c", [(0, 1), (1, 0)])
+
+
+def pair(x, axis, size, flip):
+    return lax.ppermute(x, axis, [(i, i ^ flip) for i in range(size)])
+
+
+def plus(a, b):
+    return (a.astype(F32) + b.astype(F32)).astype(BF)
 
 
 def exchange(x, axes):
@@ -293,11 +311,15 @@
         p_theirs = swap_cores(p_mine)
     with jax.named_scope("u_sum"):
         first = products(p_mine, c_own, None)
-        copies, gram = products(p_theirs, c_other, first)
-        parts = exchange(copies, "z")
-        u = sum_copies(parts, 1)[0]
-        got = [lax.ppermute(u, "x", [(i, i ^ k) for i in range(NX)]) for k in (1, 2, 3)]
-        momentum_out, p_factor, f, inv = factor(mine, gram, p_mine, p_theirs, mo_own, mo_other)
+        u, gram = products(p_theirs, c_other, first)
+        got = pair(u, "z", NZ, 1)
+        got, inv, momentum_out = lax.optimization_barrier((got, *inverse(mine, gram, mo_own, mo_other)))
+        u = plus(u, got)
+        got = pair(u, "z", NZ, 2)
+        got, p_factor, f = lax.optimization_barrier((got, *factor(mine, inv, p_mine, p_theirs)))
+        u = plus(u, got)
+        u = plus(u, pair(u, "z", NZ, 6))
+        got = [pair(u, "x", NX, k) for k in (1, 2, 3)]
     with jax.named_scope("back"):
         error_out, q_factor = back(mine, f, c_own, c_other, inv, (u, *got))
     return momentum_out, error_out, p_factor, q_factor

time: 87.2 us -> 85 us (0.975)
  the two profiles are of different devices: /device:TPU:1 before, /device:TPU:32 now
where the time goes in v3:
time: 85 us; the launch traced here: 84.4 us
  blocking collectives  50.7 us (60%)
  Pallas kernels  13.5 us (16%)
  waiting for transfers between devices  11.8 us (14%)
  starting transfers between devices  7.61 us (9%)
    all_to_all x3, blocking collectives, exchange(): return lax.all_to_all(x, axes, 0, 0)  50.7 us
    ppermute x6, waiting for transfers between devices, pair(): return lax.ppermute(x, axis, [(i, i ^ flip) for i in range(size)])  10.4 us
    ppermute x6, starting transfers between devices, pair(): return lax.ppermute(x, axis, [(i, i ^ flip) for i in range(size)])  7.51 us
    pallas_call x2, Pallas kernels, front(): pl.pallas_call(front_body, in_specs=[pl.BlockSpec(memory_space=pltpu.SMEM...  4.87 us
    pallas_call x1, Pallas kernels, inverse(): pl.pallas_call(inverse_body, in_specs=[pl.BlockSpec(memory_space=pltpu.SM...  3.31 us
    pallas_call x1, Pallas kernels, back(): pl.pallas_call(back_body, in_specs=[pl.BlockSpec(memory_space=pltpu.SMEM)...  2.56 us
  transfers between devices with their start and end apart: 8, of which 5 were waited for; matrix products, arithmetic and copies ran while one was open for 0% of the time, Pallas kernels for 9%

profile of v3, /device:TPU:32, one launch (start us, length us, event | category | flops | bytes accessed | tf_op | source)
XLA Modules:
  0.0 84.4 jit_solution(6437670107244882602)
XLA Ops:
  0.6 2.4 %p_partial.3 = (bf16[2,2048,128]{2,1,0:T(8,128)(2,1)S(1)}, bf16[2,2048,128]{2,1,0:T(8,128)(2,1)S(1)}, bf16[2048,128]{1,0:T(8,128)(2,1)S(1)}) custom-call(s32[1]{0:T(128)} %bitcast.1.half_ref, bf16[1,2,4096,128]{3,2,1,0:T(8,128)(2,1)} %g_hbm.3, bf16[1,2,4096,128]{3,2,1,0:T(8,128)(2,1)} %m_hbm.3, bf16[1,2,4096,128]{3,2,1,0:T(8,128)(2,1)} %e_hbm.3, ...), custom_call_target="tpu_custom_call" | custom-call | flops 134217728 | bytes 4194304 | tf_op jit(solution)/shard_map/p_partial/pallas_call | solution.py:65
  3.1 0.1 collective-permute-start
  3.2 2.4 %p_partial.2 = (bf16[2,2048,128]{2,1,0:T(8,128)(2,1)S(1)}, bf16[2,2048,128]{2,1,0:T(8,128)(2,1)S(1)}, f32[2048,128]{1,0:T(8,128)S(1)}) custom-call(s32[1]{0:T(128)} %bitcast.half_ref, bf16[1,2,4096,128]{3,2,1,0:T(8,128)(2,1)} %g_hbm.3, bf16[1,2,4096,128]{3,2,1,0:T(8,128)(2,1)} %m_hbm.3, bf16[1,2,4096,128]{3,2,1,0:T(8,128)(2,1)} %e_hbm.3, bf16[128,128]{1,0:T(8,128)(2,1)} %q_hbm.3), custom_call_target="tpu_custom_call" | custom-call | flops 134217728 | bytes 4194304 | tf_op jit(solution)/shard_map/p_partial/pallas_call | solution.py:65
  5.6 0.0 collective-permute-done
  5.6 0.1 add_convert_fusion
  5.7 19.0 %all_to_all.15.x_ref = bf16[16,128,128]{2,1,0:T(8,128)(2,1)S(1)} all-to-all(bf16[16,128,128]{2,1,0:T(8,128)(2,1)S(1)} %bitcast.7), channel_id=1, replica_groups=mesh['z'=8,'x'=4,'y'=4,'c'=2] {'x','y'}, dimensions={0} | all-to-all | bytes 1048576 | tf_op jit(solution)/shard_map/p_sum/all_to_all | solution.py:294
  24.7 0.1 p_sum.2
  24.8 17.4 %all_to_all.16.x_ref = bf16[8,128,128]{2,1,0:T(8,128)(2,1)S(1)} all-to-all(bf16[8,128,128]{2,1,0:T(8,128)(2,1)S(1)} %p_sum.2), channel_id=1, replica_groups=mesh['z'=8,'x'=4,'y'=4,'c'=2] {'z'}, dimensions={0} | all-to-all | bytes 524288 | tf_op jit(solution)/shard_map/p_sum/all_to_all | solution.py:294
  42.2 0.1 p_sum.3
  42.3 14.3 %all_to_all.17 = bf16[16,128,128]{2,1,0:T(8,128)(2,1)S(1)} all-to-all(bf16[16,128,128]{2,1,0:T(8,128)(2,1)S(1)} %p_sum.3), channel_id=1, replica_groups=mesh['z'=8,'x'=4,'y'=4,'c'=2] {'x','y'}, dimensions={0} | all-to-all | bytes 1048576 | tf_op jit(solution)/shard_map/p_sum/all_to_all | solution.py:294
  56.6 0.0 collective-permute-start.1
  56.6 0.5 u_sum.4
  57.0 1.4 %collective-permute-done.1.p_ref.pt_ref = bf16[2048,128]{1,0:T(8,128)(2,1)S(1)} collective-permute-done((bf16[2048,128]{1,0:T(8,128)(2,1)S(1)}, bf16[2048,128]{1,0:T(8,128)(2,1)S(1)}, u32[]{:S(2)}, u32[]{:S(2)}) %collective-permute-start.1) | collective-permute-done | bytes 524320 | tf_op jit(solution)/shard_map/p_sum/ppermute | solution.py:282
  58.5 0.5 u_sum.5
  59.0 1.5 %collective-permute-start.2 = (bf16[128,128]{1,0:T(8,128)(2,1)S(1)}, bf16[128,128]{1,0:T(8,128)(2,1)S(1)}, u32[]{:S(2)}, u32[]{:S(2)}) collective-permute-start(bf16[128,128]{1,0:T(8,128)(2,1)S(1)} %get-tuple-element.32), channel_id=1, source_target_pairs={{0,32},{32,0},{64,96},{96,64},{128,160},{160,128},{192,224},{224,1... | collective-permute-start | bytes 98312 | tf_op jit(solution)/shard_map/u_sum/ppermute | solution.py:286
  60.5 3.3 %u_sum.6 = (f32[128,128]{1,0:T(8,128)S(1)}, bf16[1,2,4096,128]{3,2,1,0:T(8,128)(2,1)}) custom-call(s32[1]{0:T(128)} %bitcast.half_ref, f32[128,128]{1,0:T(8,128)S(1)} %get-tuple-element.33.g_ref, bf16[2,2048,128]{2,1,0:T(8,128)(2,1)S(1)} %get-tuple-element.34.mo_ref, bf16[2,2048,128]{2,1,0:T(8,128)(2,1)S(1)} %get-tuple-element.35.mt_ref), custom_call_target="tpu_custom_call" | custom-call | flops 262144 | bytes 6291456 | tf_op jit(solution)/shard_map/u_sum/pallas_call | solution.py:186
  63.8 0.0 collective-permute-done.2
  63.8 0.2 collective-permute-start.3
  64.1 1.6 %u_sum.7 = (bf16[4096,128]{1,0:T(8,128)(2,1)}, bf16[4096,128]{1,0:T(8,128)(2,1)S(1)}) custom-call(s32[1]{0:T(128)} %bitcast.half_ref, f32[128,128]{1,0:T(8,128)S(1)} %get-tuple-element.40.l_ref, bf16[2048,128]{1,0:T(8,128)(2,1)S(1)} %bitcast.6, bf16[2048,128]{1,0:T(8,128)(2,1)S(1)} %collective-permute-done.1.p_ref.pt_ref), custom_call_target="tpu_custom_call" | custom-call | flops 268435456 | bytes 6291456 | tf_op jit(solution)/shard_map/u_sum/pallas_call | solution.py:218
  65.7 3.0 %collective-permute-done.3 = bf16[128,128]{1,0:T(8,128)(2,1)S(1)} collective-permute-done((bf16[128,128]{1,0:T(8,128)(2,1)S(1)}, bf16[128,128]{1,0:T(8,128)(2,1)S(1)}, u32[]{:S(2)}, u32[]{:S(2)}) %collective-permute-start.3) | collective-permute-done | bytes 32800 | tf_op jit(solution)/shard_map/u_sum/ppermute | solution.py:286
  68.8 1.5 %collective-permute-start.4 = (bf16[128,128]{1,0:T(8,128)(2,1)S(1)}, bf16[128,128]{1,0:T(8,128)(2,1)S(1)}, u32[]{:S(2)}, u32[]{:S(2)}) collective-permute-start(bf16[128,128]{1,0:T(8,128)(2,1)S(1)} %add_convert_fusion.2), channel_id=1, source_target_pairs={{0,192},{32,224},{64,128},{96,160},{128,64},{160,96},{192,0},{224,... | collective-permute-start | bytes 98312 | tf_op jit(solution)/shard_map/u_sum/ppermute | solution.py:286
  70.3 4.9 %collective-permute-done.4 = bf16[128,128]{1,0:T(8,128)(2,1)S(1)} collective-permute-done((bf16[128,128]{1,0:T(8,128)(2,1)S(1)}, bf16[128,128]{1,0:T(8,128)(2,1)S(1)}, u32[]{:S(2)}, u32[]{:S(2)}) %collective-permute-start.4) | collective-permute-done | bytes 32800 | tf_op jit(solution)/shard_map/u_sum/ppermute | solution.py:286
  75.2 1.2 %collective-permute-start.7 = (bf16[128,128]{1,0:T(8,128)(2,1)S(1)}, bf16[128,128]{1,0:T(8,128)(2,1)S(1)}, u32[]{:S(2)}, u32[]{:S(2)}) collective-permute-start(bf16[128,128]{1,0:T(8,128)(2,1)S(1)} %add_convert_fusion.1.u_ref), channel_id=1, source_target_pairs={{0,24},{8,16},{16,8},{24,0},{1,25},{9,17},{17,9},{25,1},{2,26},{10... | collective-permute-start | bytes 98312 | tf_op jit(solution)/shard_map/u_sum/ppermute | solution.py:286
  76.4 0.7 collective-permute-start.6
  77.1 2.3 %collective-permute-start.5 = (bf16[128,128]{1,0:T(8,128)(2,1)S(1)}, bf16[128,128]{1,0:T(8,128)(2,1)S(1)}, u32[]{:S(2)}, u32[]{:S(2)}) collective-permute-start(bf16[128,128]{1,0:T(8,128)(2,1)S(1)} %add_convert_fusion.1.u_ref), channel_id=1, source_target_pairs={{0,8},{8,0},{16,24},{24,16},{1,9},{9,1},{17,25},{25,17},{2,10},{10... | collective-permute-start | bytes 98312 | tf_op jit(solution)/shard_map/u_sum/ppermute | solution.py:286
  79.4 1.0 %collective-permute-done.7.d_ref = bf16[128,128]{1,0:T(8,128)(2,1)S(1)} collective-permute-done((bf16[128,128]{1,0:T(8,128)(2,1)S(1)}, bf16[128,128]{1,0:T(8,128)(2,1)S(1)}, u32[]{:S(2)}, u32[]{:S(2)}) %collective-permute-start.7) | collective-permute-done | bytes 32800 | tf_op jit(solution)/shard_map/u_sum/ppermute | solution.py:286
  80.5 1.4 %collective-permute-done.6.b_ref = bf16[128,128]{1,0:T(8,128)(2,1)S(1)} collective-permute-done((bf16[128,128]{1,0:T(8,128)(2,1)S(1)}, bf16[128,128]{1,0:T(8,128)(2,1)S(1)}, u32[]{:S(2)}, u32[]{:S(2)}) %collective-permute-start.6) | collective-permute-done | bytes 32800 | tf_op jit(solution)/shard_map/u_sum/ppermute | solution.py:286
  81.9 0.0 collective-permute-done.5.a_ref
  81.9 2.6 %back.1 = (bf16[1,2,4096,128]{3,2,1,0:T(8,128)(2,1)}, f32[128,128]{1,0:T(8,128)}) custom-call(s32[1]{0:T(128)} %bitcast.half_ref, bf16[4096,128]{1,0:T(8,128)(2,1)S(1)} %get-tuple-element.43.f_ref, bf16[2,2048,128]{2,1,0:T(8,128)(2,1)S(1)} %get-tuple-element.29.c_ref.co_ref, bf16[2,2048,128]{2,1,0:T(8,128)(2,1)S(1)} %get-tuple-element.28.c_ref.ct_ref, ...), custom_call_target="tpu_custom_call" | custom-call | flops 268435456 | bytes 6291456 | tf_op jit(solution)/shard_map/back/pallas_call | solution.py:263
  (3 shorter events, 0.0 us)
Async XLA Ops:
  3.1 2.5 %collective-permute-start = (bf16[2048,128]{1,0:T(8,128)(2,1)S(1)}, bf16[2048,128]{1,0:T(8,128)(2,1)S(1)}, u32[]{:S(2)}, u32[]{:S(2)}) collective-permute-start(bf16[2048,128]{1,0:T(8,128)(2,1)S(1)} %get-tuple-element.27), channel_id=1, source_target_pairs={{0,1},{1,0},{2,3},{3,2},{4,5},{5,4},{6,7},{7,6},{8,9},{9,8},{10,11... | collective-permute-start | bytes 1572872 | tf_op jit(solution)/shard_map/p_partial/ppermute | solution.py:282
  56.6 1.9 %collective-permute-start.1 = (bf16[2048,128]{1,0:T(8,128)(2,1)S(1)}, bf16[2048,128]{1,0:T(8,128)(2,1)S(1)}, u32[]{:S(2)}, u32[]{:S(2)}) collective-permute-start(bf16[2048,128]{1,0:T(8,128)(2,1)S(1)} %bitcast.4), channel_id=1, source_target_pairs={{0,1},{1,0},{2,3},{3,2},{4,5},{5,4},{6,7},{7,6},{8,9},{9,8},{10,11... | collective-permute-start | bytes 1572872 | tf_op jit(solution)/shard_map/p_sum/ppermute | solution.py:282
  59.0 4.9 %collective-permute-start.2 = (bf16[128,128]{1,0:T(8,128)(2,1)S(1)}, bf16[128,128]{1,0:T(8,128)(2,1)S(1)}, u32[]{:S(2)}, u32[]{:S(2)}) collective-permute-start(bf16[128,128]{1,0:T(8,128)(2,1)S(1)} %get-tuple-element.32), channel_id=1, source_target_pairs={{0,32},{32,0},{64,96},{96,64},{128,160},{160,128},{192,224},{224,1... | collective-permute-start | bytes 98312 | tf_op jit(solution)/shard_map/u_sum/ppermute | solution.py:286
  63.8 4.9 %collective-permute-start.3 = (bf16[128,128]{1,0:T(8,128)(2,1)S(1)}, bf16[128,128]{1,0:T(8,128)(2,1)S(1)}, u32[]{:S(2)}, u32[]{:S(2)}) collective-permute-start(bf16[128,128]{1,0:T(8,128)(2,1)S(1)} %add_convert_fusion.3), channel_id=1, source_target_pairs={{0,64},{32,96},{64,0},{96,32},{128,192},{160,224},{192,128},{224,1... | collective-permute-start | bytes 98312 | tf_op jit(solution)/shard_map/u_sum/ppermute | solution.py:286
  68.8 6.5 %collective-permute-start.4 = (bf16[128,128]{1,0:T(8,128)(2,1)S(1)}, bf16[128,128]{1,0:T(8,128)(2,1)S(1)}, u32[]{:S(2)}, u32[]{:S(2)}) collective-permute-start(bf16[128,128]{1,0:T(8,128)(2,1)S(1)} %add_convert_fusion.2), channel_id=1, source_target_pairs={{0,192},{32,224},{64,128},{96,160},{128,64},{160,96},{192,0},{224,... | collective-permute-start | bytes 98312 | tf_op jit(solution)/shard_map/u_sum/ppermute | solution.py:286
  75.2 5.2 %collective-permute-start.7 = (bf16[128,128]{1,0:T(8,128)(2,1)S(1)}, bf16[128,128]{1,0:T(8,128)(2,1)S(1)}, u32[]{:S(2)}, u32[]{:S(2)}) collective-permute-start(bf16[128,128]{1,0:T(8,128)(2,1)S(1)} %add_convert_fusion.1.u_ref), channel_id=1, source_target_pairs={{0,24},{8,16},{16,8},{24,0},{1,25},{9,17},{17,9},{25,1},{2,26},{10... | collective-permute-start | bytes 98312 | tf_op jit(solution)/shard_map/u_sum/ppermute | solution.py:286
  76.4 5.4 %collective-permute-start.6 = (bf16[128,128]{1,0:T(8,128)(2,1)S(1)}, bf16[128,128]{1,0:T(8,128)(2,1)S(1)}, u32[]{:S(2)}, u32[]{:S(2)}) collective-permute-start(bf16[128,128]{1,0:T(8,128)(2,1)S(1)} %add_convert_fusion.1.u_ref), channel_id=1, source_target_pairs={{0,16},{8,24},{16,0},{24,8},{1,17},{9,25},{17,1},{25,9},{2,18},{10... | collective-permute-start | bytes 98312 | tf_op jit(solution)/shard_map/u_sum/ppermute | solution.py:286
  77.1 4.7 %collective-permute-start.5 = (bf16[128,128]{1,0:T(8,128)(2,1)S(1)}, bf16[128,128]{1,0:T(8,128)(2,1)S(1)}, u32[]{:S(2)}, u32[]{:S(2)}) collective-permute-start(bf16[128,128]{1,0:T(8,128)(2,1)S(1)} %add_convert_fusion.1.u_ref), channel_id=1, source_target_pairs={{0,8},{8,0},{16,24},{24,16},{1,9},{9,1},{17,25},{25,17},{2,10},{10... | collective-permute-start | bytes 98312 | tf_op jit(solution)/shard_map/u_sum/ppermute | solution.py:286

commit v4 on v3

--- a/solution.py
+++ b/solution.py
@@ -11,7 +11,7 @@
 ROWS, COLS, RANK2 = 4096, 128, 128
 HALF = ROWS // NC
 BLK = HALF // (NX * NY)
-FRONT, PROD, BACK = 1024, 512, 512
+FRONT, PROD, BACK = 1024, 512, 256
 PANEL = 8
 MIB = 1 << 20
 
@@ -226,36 +226,36 @@
     )(half, inv, p_own, p_other)
 
 
+def split(x):
+    hi = x.astype(BF)
+    return hi, (x - hi.astype(F32)).astype(BF)
+
+
 def back_body(half_ref, f_ref, co_ref, ct_ref, l_ref, u_ref, a_ref, b_ref, d_ref, e_hbm, q_ref, e_buf, w_ref, sem):
     u, a, b, d = (t[...].astype(F32) for t in (u_ref, a_ref, b_ref, d_ref))
-    qt = dot(l_ref[...], (u + a) + (b + d), precision=lax.Precision.HIGHEST) * (1.0 / (NZ * NX))
-    q_ref[...] = qt.T
+    (ih, il), (uh, ul) = split(l_ref[...]), split(((u + a) + (b + d)) * (1.0 / (NZ * NX)))
+    qt = dot(jnp.concatenate([ih, il], axis=1), jnp.concatenate([uh, uh], axis=0)) + dot(ih, ul)
+    q_ref[...] = qt
     qt = qt.astype(BF)
     top = lax.broadcasted_iota(jnp.int32, qt.shape, 0) < RANK2 // 2
     zero = jnp.zeros_like(qt)
     w_ref[...] = jnp.concatenate([jnp.where(top, qt, zero), jnp.where(top, zero, qt)], axis=1)
     weights = w_ref[...]
-
-    def store(which, k):
+    copies = []
+    for which, c_ref in enumerate((co_ref, ct_ref)):
         half = half_ref[0] if which == 0 else 1 - half_ref[0]
-        here = pl.ds(pl.multiple_of(which * HALF + k * BACK, BACK), BACK)
-        there = pl.ds(pl.multiple_of(half * HALF + k * BACK, BACK), BACK)
-        return here, pltpu.make_async_copy(e_buf.at[:, here], e_hbm.at[0, :, there], sem.at[which, k])
-
-    for which, c_ref in enumerate((co_ref, ct_ref)):
-
         for k in range(HALF // BACK):
-            here, copy = store(which, k)
+            here = pl.ds(which * HALF + k * BACK, BACK)
+            there = pl.ds(pl.multiple_of(half * HALF + k * BACK, BACK), BACK)
             approx = dot(f_ref[here], weights)
             for group in range(2):
-                c = c_ref[group, pl.ds(pl.multiple_of(k * BACK, BACK), BACK)].astype(F32)
+                c = c_ref[group, pl.ds(k * BACK, BACK)].astype(F32)
                 e_buf[group, here] = (c - approx[:, group * COLS : (group + 1) * COLS]).astype(BF)
-            copy.start()
-
-    for which in range(2):
-
-        for k in range(HALF // BACK):
-            store(which, k)[1].wait()
+            copies.append(pltpu.make_async_copy(e_buf.at[:, here], e_hbm.at[0, :, there], sem.at[which, k]))
+            copies[-1].start()
+    q_ref[...] = q_ref[...].T
+    for copy in copies:
+        copy.wait()
 
 
 def back(half, f, c_own, c_other, inv, us):
@@ -312,13 +312,16 @@
     with jax.named_scope("u_sum"):
         first = products(p_mine, c_own, None)
         u, gram = products(p_theirs, c_other, first)
-        got = pair(u, "z", NZ, 1)
+        def tree(u, got):
+            u, a, b, d = (t.astype(F32) for t in (u, *got))
+            return ((u + a) + (b + d)).astype(BF)
+
+        got = [pair(u, "z", NZ, k) for k in (1, 2, 3)]
         got, inv, momentum_out = lax.optimization_barrier((got, *inverse(mine, gram, mo_own, mo_other)))
-        u = plus(u, got)
-        got = pair(u, "z", NZ, 2)
+        u = tree(u, got)
+        got = pair(u, "z", NZ, 6)
         got, p_factor, f = lax.optimization_barrier((got, *factor(mine, inv, p_mine, p_theirs)))
         u = plus(u, got)
-        u = plus(u, pair(u, "z", NZ, 6))
         got = [pair(u, "x", NX, k) for k in (1, 2, 3)]
     with jax.named_scope("back"):
         error_out, q_factor = back(mine, f, c_own, c_other, inv, (u, *got))

time: 85 us -> 83.5 us (0.982); the launches traced: 84.4 us -> 82 us
  waiting for transfers between devices: 11.8 us -> 8.43 us
  starting transfers between devices: 7.61 us -> 8.69 us
    ppermute x6 -> x7, waiting for transfers between devices: 10.4 us -> 7.01 us  [pair(): return lax.ppermute(x, axis, [(i, i ^ flip) for i in range(size)])]
    ppermute x6 -> x7, starting transfers between devices: 7.51 us -> 8.59 us  [pair(): return lax.ppermute(x, axis, [(i, i ^ flip) for i in range(size)])]
  transfers between devices with their start and end apart: 8 -> 9, of which waited for: 5 -> 5; matrix products, arithmetic and copies ran while one was open for 0% -> 0% of each run, Pallas kernels for 9% -> 10%
where the time goes in v4:
time: 83.5 us; the launch traced here: 82 us
  blocking collectives  50.7 us (61%)
  Pallas kernels  13.3 us (16%)
  starting transfers between devices  8.69 us (10%)
  waiting for transfers between devices  8.43 us (10%)
    all_to_all x3, blocking collectives, exchange(): return lax.all_to_all(x, axes, 0, 0)  50.7 us
    ppermute x7, starting transfers between devices, pair(): return lax.ppermute(x, axis, [(i, i ^ flip) for i in range(size)])  8.59 us
    ppermute x7, waiting for transfers between devices, pair(): return lax.ppermute(x, axis, [(i, i ^ flip) for i in range(size)])  7.01 us
    pallas_call x2, Pallas kernels, front(): pl.pallas_call(front_body, in_specs=[pl.BlockSpec(memory_space=pltpu.SMEM...  4.87 us
    pallas_call x1, Pallas kernels, inverse(): pl.pallas_call(inverse_body, in_specs=[pl.BlockSpec(memory_space=pltpu.SM...  3.31 us
    pallas_call x1, Pallas kernels, back(): pl.pallas_call(back_body, in_specs=[pl.BlockSpec(memory_space=pltpu.SMEM)...  2.45 us
  transfers between devices with their start and end apart: 9, of which 5 were waited for; matrix products, arithmetic and copies ran while one was open for 0% of the time, Pallas kernels for 10%

profile of v4, /device:TPU:32, one launch (start us, length us, event | category | flops | bytes accessed | tf_op | source)
XLA Modules:
  0.0 82.0 jit_solution(2529321300662259095)
XLA Ops:
  0.6 2.4 %p_partial.3 = (bf16[2,2048,128]{2,1,0:T(8,128)(2,1)S(1)}, bf16[2,2048,128]{2,1,0:T(8,128)(2,1)S(1)}, bf16[2048,128]{1,0:T(8,128)(2,1)S(1)}) custom-call(s32[1]{0:T(128)} %bitcast.1.half_ref, bf16[1,2,4096,128]{3,2,1,0:T(8,128)(2,1)} %g_hbm.3, bf16[1,2,4096,128]{3,2,1,0:T(8,128)(2,1)} %m_hbm.3, bf16[1,2,4096,128]{3,2,1,0:T(8,128)(2,1)} %e_hbm.3, ...), custom_call_target="tpu_custom_call" | custom-call | flops 134217728 | bytes 4194304 | tf_op jit(solution)/shard_map/p_partial/pallas_call | solution.py:65
  3.1 0.1 collective-permute-start
  3.2 2.4 %p_partial.2 = (bf16[2,2048,128]{2,1,0:T(8,128)(2,1)S(1)}, bf16[2,2048,128]{2,1,0:T(8,128)(2,1)S(1)}, f32[2048,128]{1,0:T(8,128)S(1)}) custom-call(s32[1]{0:T(128)} %bitcast.half_ref, bf16[1,2,4096,128]{3,2,1,0:T(8,128)(2,1)} %g_hbm.3, bf16[1,2,4096,128]{3,2,1,0:T(8,128)(2,1)} %m_hbm.3, bf16[1,2,4096,128]{3,2,1,0:T(8,128)(2,1)} %e_hbm.3, bf16[128,128]{1,0:T(8,128)(2,1)} %q_hbm.3), custom_call_target="tpu_custom_call" | custom-call | flops 134217728 | bytes 4194304 | tf_op jit(solution)/shard_map/p_partial/pallas_call | solution.py:65
  5.6 0.0 collective-permute-done
  5.6 0.1 add_convert_fusion
  5.7 19.0 %all_to_all.15.x_ref = bf16[16,128,128]{2,1,0:T(8,128)(2,1)S(1)} all-to-all(bf16[16,128,128]{2,1,0:T(8,128)(2,1)S(1)} %bitcast.7), channel_id=1, replica_groups=mesh['z'=8,'x'=4,'y'=4,'c'=2] {'x','y'}, dimensions={0} | all-to-all | bytes 1048576 | tf_op jit(solution)/shard_map/p_sum/all_to_all | solution.py:294
  24.7 0.1 p_sum.2
  24.8 17.4 %all_to_all.16.x_ref = bf16[8,128,128]{2,1,0:T(8,128)(2,1)S(1)} all-to-all(bf16[8,128,128]{2,1,0:T(8,128)(2,1)S(1)} %p_sum.2), channel_id=1, replica_groups=mesh['z'=8,'x'=4,'y'=4,'c'=2] {'z'}, dimensions={0} | all-to-all | bytes 524288 | tf_op jit(solution)/shard_map/p_sum/all_to_all | solution.py:294
  42.2 0.1 p_sum.3
  42.3 14.3 %all_to_all.17 = bf16[16,128,128]{2,1,0:T(8,128)(2,1)S(1)} all-to-all(bf16[16,128,128]{2,1,0:T(8,128)(2,1)S(1)} %p_sum.3), channel_id=1, replica_groups=mesh['z'=8,'x'=4,'y'=4,'c'=2] {'x','y'}, dimensions={0} | all-to-all | bytes 1048576 | tf_op jit(solution)/shard_map/p_sum/all_to_all | solution.py:294
  56.6 0.0 collective-permute-start.1
  56.6 0.5 u_sum.4
  57.0 1.4 %collective-permute-done.1.p_ref.pt_ref = bf16[2048,128]{1,0:T(8,128)(2,1)S(1)} collective-permute-done((bf16[2048,128]{1,0:T(8,128)(2,1)S(1)}, bf16[2048,128]{1,0:T(8,128)(2,1)S(1)}, u32[]{:S(2)}, u32[]{:S(2)}) %collective-permute-start.1) | collective-permute-done | bytes 524320 | tf_op jit(solution)/shard_map/p_sum/ppermute | solution.py:282
  58.5 0.5 u_sum.5
  59.0 0.2 collective-permute-start.4
  59.2 3.7 %collective-permute-start.3 = (bf16[128,128]{1,0:T(8,128)(2,1)S(1)}, bf16[128,128]{1,0:T(8,128)(2,1)S(1)}, u32[]{:S(2)}, u32[]{:S(2)}) collective-permute-start(bf16[128,128]{1,0:T(8,128)(2,1)S(1)} %get-tuple-element.34), channel_id=1, source_target_pairs={{0,64},{32,96},{64,0},{96,32},{128,192},{160,224},{192,128},{224,1... | collective-permute-start | bytes 98312 | tf_op jit(solution)/shard_map/u_sum/ppermute | solution.py:286
  62.9 0.0 collective-permute-start.2
  62.9 3.3 %u_sum.6 = (f32[128,128]{1,0:T(8,128)S(1)}, bf16[1,2,4096,128]{3,2,1,0:T(8,128)(2,1)}) custom-call(s32[1]{0:T(128)} %bitcast.half_ref, f32[128,128]{1,0:T(8,128)S(1)} %get-tuple-element.35.g_ref, bf16[2,2048,128]{2,1,0:T(8,128)(2,1)S(1)} %get-tuple-element.36.mo_ref, bf16[2,2048,128]{2,1,0:T(8,128)(2,1)S(1)} %get-tuple-element.37.mt_ref), custom_call_target="tpu_custom_call" | custom-call | flops 262144 | bytes 6291456 | tf_op jit(solution)/shard_map/u_sum/pallas_call | solution.py:186
  66.2 0.0 collective-permute-done.4
  66.2 0.0 collective-permute-done.3
  66.2 0.6 collective-permute-done.2
  66.8 0.5 collective-permute-start.5
  67.3 1.6 %u_sum.7 = (bf16[4096,128]{1,0:T(8,128)(2,1)}, bf16[4096,128]{1,0:T(8,128)(2,1)S(1)}) custom-call(s32[1]{0:T(128)} %bitcast.half_ref, f32[128,128]{1,0:T(8,128)S(1)} %get-tuple-element.44.l_ref, bf16[2048,128]{1,0:T(8,128)(2,1)S(1)} %bitcast.6, bf16[2048,128]{1,0:T(8,128)(2,1)S(1)} %collective-permute-done.1.p_ref.pt_ref), custom_call_target="tpu_custom_call" | custom-call | flops 268435456 | bytes 6291456 | tf_op jit(solution)/shard_map/u_sum/pallas_call | solution.py:218
  68.9 4.0 %collective-permute-done.5 = bf16[128,128]{1,0:T(8,128)(2,1)S(1)} collective-permute-done((bf16[128,128]{1,0:T(8,128)(2,1)S(1)}, bf16[128,128]{1,0:T(8,128)(2,1)S(1)}, u32[]{:S(2)}, u32[]{:S(2)}) %collective-permute-start.5) | collective-permute-done | bytes 32800 | tf_op jit(solution)/shard_map/u_sum/ppermute | solution.py:286
  72.9 1.2 %collective-permute-start.8 = (bf16[128,128]{1,0:T(8,128)(2,1)S(1)}, bf16[128,128]{1,0:T(8,128)(2,1)S(1)}, u32[]{:S(2)}, u32[]{:S(2)}) collective-permute-start(bf16[128,128]{1,0:T(8,128)(2,1)S(1)} %add_convert_fusion.1.u_ref), channel_id=1, source_target_pairs={{0,24},{8,16},{16,8},{24,0},{1,25},{9,17},{17,9},{25,1},{2,26},{10... | collective-permute-start | bytes 98312 | tf_op jit(solution)/shard_map/u_sum/ppermute | solution.py:286
  74.1 0.7 collective-permute-start.7
  74.8 2.3 %collective-permute-start.6 = (bf16[128,128]{1,0:T(8,128)(2,1)S(1)}, bf16[128,128]{1,0:T(8,128)(2,1)S(1)}, u32[]{:S(2)}, u32[]{:S(2)}) collective-permute-start(bf16[128,128]{1,0:T(8,128)(2,1)S(1)} %add_convert_fusion.1.u_ref), channel_id=1, source_target_pairs={{0,8},{8,0},{16,24},{24,16},{1,9},{9,1},{17,25},{25,17},{2,10},{10... | collective-permute-start | bytes 98312 | tf_op jit(solution)/shard_map/u_sum/ppermute | solution.py:286
  77.1 1.0 %collective-permute-done.8.d_ref = bf16[128,128]{1,0:T(8,128)(2,1)S(1)} collective-permute-done((bf16[128,128]{1,0:T(8,128)(2,1)S(1)}, bf16[128,128]{1,0:T(8,128)(2,1)S(1)}, u32[]{:S(2)}, u32[]{:S(2)}) %collective-permute-start.8) | collective-permute-done | bytes 32800 | tf_op jit(solution)/shard_map/u_sum/ppermute | solution.py:286
  78.1 1.4 %collective-permute-done.7.b_ref = bf16[128,128]{1,0:T(8,128)(2,1)S(1)} collective-permute-done((bf16[128,128]{1,0:T(8,128)(2,1)S(1)}, bf16[128,128]{1,0:T(8,128)(2,1)S(1)}, u32[]{:S(2)}, u32[]{:S(2)}) %collective-permute-start.7) | collective-permute-done | bytes 32800 | tf_op jit(solution)/shard_map/u_sum/ppermute | solution.py:286
  79.5 0.0 collective-permute-done.6.a_ref
  79.5 2.5 %back.1 = (bf16[1,2,4096,128]{3,2,1,0:T(8,128)(2,1)}, f32[128,128]{1,0:T(8,128)}) custom-call(s32[1]{0:T(128)} %bitcast.half_ref, bf16[4096,128]{1,0:T(8,128)(2,1)S(1)} %get-tuple-element.47.f_ref, bf16[2,2048,128]{2,1,0:T(8,128)(2,1)S(1)} %get-tuple-element.31.c_ref.co_ref, bf16[2,2048,128]{2,1,0:T(8,128)(2,1)S(1)} %get-tuple-element.30.c_ref.ct_ref, ...), custom_call_target="tpu_custom_call" | custom-call | flops 268435456 | bytes 6291456 | tf_op jit(solution)/shard_map/back/pallas_call | solution.py:263
  (2 shorter events, 0.0 us)
Async XLA Ops:
  3.1 2.5 %collective-permute-start = (bf16[2048,128]{1,0:T(8,128)(2,1)S(1)}, bf16[2048,128]{1,0:T(8,128)(2,1)S(1)}, u32[]{:S(2)}, u32[]{:S(2)}) collective-permute-start(bf16[2048,128]{1,0:T(8,128)(2,1)S(1)} %get-tuple-element.29), channel_id=1, source_target_pairs={{0,1},{1,0},{2,3},{3,2},{4,5},{5,4},{6,7},{7,6},{8,9},{9,8},{10,11... | collective-permute-start | bytes 1572872 | tf_op jit(solution)/shard_map/p_partial/ppermute | solution.py:282
  56.6 1.9 %collective-permute-start.1 = (bf16[2048,128]{1,0:T(8,128)(2,1)S(1)}, bf16[2048,128]{1,0:T(8,128)(2,1)S(1)}, u32[]{:S(2)}, u32[]{:S(2)}) collective-permute-start(bf16[2048,128]{1,0:T(8,128)(2,1)S(1)} %bitcast.4), channel_id=1, source_target_pairs={{0,1},{1,0},{2,3},{3,2},{4,5},{5,4},{6,7},{7,6},{8,9},{9,8},{10,11... | collective-permute-start | bytes 1572872 | tf_op jit(solution)/shard_map/p_sum/ppermute | solution.py:282
  59.0 7.2 %collective-permute-start.4 = (bf16[128,128]{1,0:T(8,128)(2,1)S(1)}, bf16[128,128]{1,0:T(8,128)(2,1)S(1)}, u32[]{:S(2)}, u32[]{:S(2)}) collective-permute-start(bf16[128,128]{1,0:T(8,128)(2,1)S(1)} %get-tuple-element.34), channel_id=1, source_target_pairs={{0,96},{32,64},{64,32},{96,0},{128,224},{160,192},{192,160},{224,1... | collective-permute-start | bytes 98312 | tf_op jit(solution)/shard_map/u_sum/ppermute | solution.py:286
  59.2 7.0 %collective-permute-start.3 = (bf16[128,128]{1,0:T(8,128)(2,1)S(1)}, bf16[128,128]{1,0:T(8,128)(2,1)S(1)}, u32[]{:S(2)}, u32[]{:S(2)}) collective-permute-start(bf16[128,128]{1,0:T(8,128)(2,1)S(1)} %get-tuple-element.34), channel_id=1, source_target_pairs={{0,64},{32,96},{64,0},{96,32},{128,192},{160,224},{192,128},{224,1... | collective-permute-start | bytes 98312 | tf_op jit(solution)/shard_map/u_sum/ppermute | solution.py:286
  62.9 3.9 %collective-permute-start.2 = (bf16[128,128]{1,0:T(8,128)(2,1)S(1)}, bf16[128,128]{1,0:T(8,128)(2,1)S(1)}, u32[]{:S(2)}, u32[]{:S(2)}) collective-permute-start(bf16[128,128]{1,0:T(8,128)(2,1)S(1)} %get-tuple-element.34), channel_id=1, source_target_pairs={{0,32},{32,0},{64,96},{96,64},{128,160},{160,128},{192,224},{224,1... | collective-permute-start | bytes 98312 | tf_op jit(solution)/shard_map/u_sum/ppermute | solution.py:286
  66.8 6.1 %collective-permute-start.5 = (bf16[128,128]{1,0:T(8,128)(2,1)S(1)}, bf16[128,128]{1,0:T(8,128)(2,1)S(1)}, u32[]{:S(2)}, u32[]{:S(2)}) collective-permute-start(bf16[128,128]{1,0:T(8,128)(2,1)S(1)} %add_convert_fusion.2), channel_id=1, source_target_pairs={{0,192},{32,224},{64,128},{96,160},{128,64},{160,96},{192,0},{224,... | collective-permute-start | bytes 98312 | tf_op jit(solution)/shard_map/u_sum/ppermute | solution.py:286
  72.9 5.2 %collective-permute-start.8 = (bf16[128,128]{1,0:T(8,128)(2,1)S(1)}, bf16[128,128]{1,0:T(8,128)(2,1)S(1)}, u32[]{:S(2)}, u32[]{:S(2)}) collective-permute-start(bf16[128,128]{1,0:T(8,128)(2,1)S(1)} %add_convert_fusion.1.u_ref), channel_id=1, source_target_pairs={{0,24},{8,16},{16,8},{24,0},{1,25},{9,17},{17,9},{25,1},{2,26},{10... | collective-permute-start | bytes 98312 | tf_op jit(solution)/shard_map/u_sum/ppermute | solution.py:286
  74.1 5.4 %collective-permute-start.7 = (bf16[128,128]{1,0:T(8,128)(2,1)S(1)}, bf16[128,128]{1,0:T(8,128)(2,1)S(1)}, u32[]{:S(2)}, u32[]{:S(2)}) collective-permute-start(bf16[128,128]{1,0:T(8,128)(2,1)S(1)} %add_convert_fusion.1.u_ref), channel_id=1, source_target_pairs={{0,16},{8,24},{16,0},{24,8},{1,17},{9,25},{17,1},{25,9},{2,18},{10... | collective-permute-start | bytes 98312 | tf_op jit(solution)/shard_map/u_sum/ppermute | solution.py:286
  74.8 4.7 %collective-permute-start.6 = (bf16[128,128]{1,0:T(8,128)(2,1)S(1)}, bf16[128,128]{1,0:T(8,128)(2,1)S(1)}, u32[]{:S(2)}, u32[]{:S(2)}) collective-permute-start(bf16[128,128]{1,0:T(8,128)(2,1)S(1)} %add_convert_fusion.1.u_ref), channel_id=1, source_target_pairs={{0,8},{8,0},{16,24},{24,16},{1,9},{9,1},{17,25},{25,17},{2,10},{10... | collective-permute-start | bytes 98312 | tf_op jit(solution)/shard_map/u_sum/ppermute | solution.py:286

commit v5 on v4

--- a/solution.py
+++ b/solution.py
@@ -316,12 +316,12 @@
             u, a, b, d = (t.astype(F32) for t in (u, *got))
             return ((u + a) + (b + d)).astype(BF)
 
+        got = pair(u, "z", NZ, 6)
+        got, inv, momentum_out = lax.optimization_barrier((got, *inverse(mine, gram, mo_own, mo_other)))
+        u = plus(u, got)
         got = [pair(u, "z", NZ, k) for k in (1, 2, 3)]
-        got, inv, momentum_out = lax.optimization_barrier((got, *inverse(mine, gram, mo_own, mo_other)))
+        got, p_factor, f = lax.optimization_barrier((got, *factor(mine, inv, p_mine, p_theirs)))
         u = tree(u, got)
-        got = pair(u, "z", NZ, 6)
-        got, p_factor, f = lax.optimization_barrier((got, *factor(mine, inv, p_mine, p_theirs)))
-        u = plus(u, got)
         got = [pair(u, "x", NX, k) for k in (1, 2, 3)]
     with jax.named_scope("back"):
         error_out, q_factor = back(mine, f, c_own, c_other, inv, (u, *got))

time: 83.5 us -> 82.2 us (0.984); the launches traced: 82 us -> 82 us
  transfers between devices with their start and end apart: 9 -> 9, of which waited for: 5 -> 6; matrix products, arithmetic and copies ran while one was open for 0% -> 0% of each run, Pallas kernels for 10% -> 10%
where the time goes in v5:
time: 82.2 us; the launch traced here: 82 us
  blocking collectives  50.7 us (62%)
  Pallas kernels  13.3 us (16%)
  waiting for transfers between devices  8.78 us (11%)
  starting transfers between devices  8.35 us (10%)
    all_to_all x3, blocking collectives, exchange(): return lax.all_to_all(x, axes, 0, 0)  50.7 us
    ppermute x7, starting transfers between devices, pair(): return lax.ppermute(x, axis, [(i, i ^ flip) for i in range(size)])  8.25 us
    ppermute x7, waiting for transfers between devices, pair(): return lax.ppermute(x, axis, [(i, i ^ flip) for i in range(size)])  7.36 us
    pallas_call x2, Pallas kernels, front(): pl.pallas_call(front_body, in_specs=[pl.BlockSpec(memory_space=pltpu.SMEM...  4.87 us
    pallas_call x1, Pallas kernels, inverse(): pl.pallas_call(inverse_body, in_specs=[pl.BlockSpec(memory_space=pltpu.SM...  3.31 us
    pallas_call x1, Pallas kernels, back(): pl.pallas_call(back_body, in_specs=[pl.BlockSpec(memory_space=pltpu.SMEM)...  2.45 us
  transfers between devices with their start and end apart: 9, of which 6 were waited for; matrix products, arithmetic and copies ran while one was open for 0% of the time, Pallas kernels for 10%

profile of v5, /device:TPU:32, one launch (start us, length us, event | category | flops | bytes accessed | tf_op | source)
XLA Modules:
  0.0 82.0 jit_solution(10713104974329580186)
XLA Ops:
  0.6 2.4 %p_partial.3 = (bf16[2,2048,128]{2,1,0:T(8,128)(2,1)S(1)}, bf16[2,2048,128]{2,1,0:T(8,128)(2,1)S(1)}, bf16[2048,128]{1,0:T(8,128)(2,1)S(1)}) custom-call(s32[1]{0:T(128)} %bitcast.1.half_ref, bf16[1,2,4096,128]{3,2,1,0:T(8,128)(2,1)} %g_hbm.3, bf16[1,2,4096,128]{3,2,1,0:T(8,128)(2,1)} %m_hbm.3, bf16[1,2,4096,128]{3,2,1,0:T(8,128)(2,1)} %e_hbm.3, ...), custom_call_target="tpu_custom_call" | custom-call | flops 134217728 | bytes 4194304 | tf_op jit(solution)/shard_map/p_partial/pallas_call | solution.py:65
  3.1 0.1 collective-permute-start
  3.2 2.4 %p_partial.2 = (bf16[2,2048,128]{2,1,0:T(8,128)(2,1)S(1)}, bf16[2,2048,128]{2,1,0:T(8,128)(2,1)S(1)}, f32[2048,128]{1,0:T(8,128)S(1)}) custom-call(s32[1]{0:T(128)} %bitcast.half_ref, bf16[1,2,4096,128]{3,2,1,0:T(8,128)(2,1)} %g_hbm.3, bf16[1,2,4096,128]{3,2,1,0:T(8,128)(2,1)} %m_hbm.3, bf16[1,2,4096,128]{3,2,1,0:T(8,128)(2,1)} %e_hbm.3, bf16[128,128]{1,0:T(8,128)(2,1)} %q_hbm.3), custom_call_target="tpu_custom_call" | custom-call | flops 134217728 | bytes 4194304 | tf_op jit(solution)/shard_map/p_partial/pallas_call | solution.py:65
  5.6 0.0 collective-permute-done
  5.6 0.1 add_convert_fusion
  5.7 19.0 %all_to_all.15.x_ref = bf16[16,128,128]{2,1,0:T(8,128)(2,1)S(1)} all-to-all(bf16[16,128,128]{2,1,0:T(8,128)(2,1)S(1)} %bitcast.7), channel_id=1, replica_groups=mesh['z'=8,'x'=4,'y'=4,'c'=2] {'x','y'}, dimensions={0} | all-to-all | bytes 1048576 | tf_op jit(solution)/shard_map/p_sum/all_to_all | solution.py:294
  24.7 0.1 p_sum.2
  24.8 17.4 %all_to_all.16.x_ref = bf16[8,128,128]{2,1,0:T(8,128)(2,1)S(1)} all-to-all(bf16[8,128,128]{2,1,0:T(8,128)(2,1)S(1)} %p_sum.2), channel_id=1, replica_groups=mesh['z'=8,'x'=4,'y'=4,'c'=2] {'z'}, dimensions={0} | all-to-all | bytes 524288 | tf_op jit(solution)/shard_map/p_sum/all_to_all | solution.py:294
  42.2 0.1 p_sum.3
  42.3 14.3 %all_to_all.17 = bf16[16,128,128]{2,1,0:T(8,128)(2,1)S(1)} all-to-all(bf16[16,128,128]{2,1,0:T(8,128)(2,1)S(1)} %p_sum.3), channel_id=1, replica_groups=mesh['z'=8,'x'=4,'y'=4,'c'=2] {'x','y'}, dimensions={0} | all-to-all | bytes 1048576 | tf_op jit(solution)/shard_map/p_sum/all_to_all | solution.py:294
  56.6 0.0 collective-permute-start.1
  56.6 0.5 u_sum.4
  57.0 1.4 %collective-permute-done.1.p_ref.pt_ref = bf16[2048,128]{1,0:T(8,128)(2,1)S(1)} collective-permute-done((bf16[2048,128]{1,0:T(8,128)(2,1)S(1)}, bf16[2048,128]{1,0:T(8,128)(2,1)S(1)}, u32[]{:S(2)}, u32[]{:S(2)}) %collective-permute-start.1) | collective-permute-done | bytes 524320 | tf_op jit(solution)/shard_map/p_sum/ppermute | solution.py:282
  58.5 0.5 u_sum.5
  59.0 0.5 collective-permute-start.2
  59.4 3.3 %u_sum.6 = (f32[128,128]{1,0:T(8,128)S(1)}, bf16[1,2,4096,128]{3,2,1,0:T(8,128)(2,1)}) custom-call(s32[1]{0:T(128)} %bitcast.half_ref, f32[128,128]{1,0:T(8,128)S(1)} %get-tuple-element.35.g_ref, bf16[2,2048,128]{2,1,0:T(8,128)(2,1)S(1)} %get-tuple-element.36.mo_ref, bf16[2,2048,128]{2,1,0:T(8,128)(2,1)S(1)} %get-tuple-element.37.mt_ref), custom_call_target="tpu_custom_call" | custom-call | flops 262144 | bytes 6291456 | tf_op jit(solution)/shard_map/u_sum/pallas_call | solution.py:186
  62.8 2.7 %collective-permute-done.2 = bf16[128,128]{1,0:T(8,128)(2,1)S(1)} collective-permute-done((bf16[128,128]{1,0:T(8,128)(2,1)S(1)}, bf16[128,128]{1,0:T(8,128)(2,1)S(1)}, u32[]{:S(2)}, u32[]{:S(2)}) %collective-permute-start.2) | collective-permute-done | bytes 32800 | tf_op jit(solution)/shard_map/u_sum/ppermute | solution.py:286
  65.4 0.2 collective-permute-start.5
  65.7 3.3 %collective-permute-start.4 = (bf16[128,128]{1,0:T(8,128)(2,1)S(1)}, bf16[128,128]{1,0:T(8,128)(2,1)S(1)}, u32[]{:S(2)}, u32[]{:S(2)}) collective-permute-start(bf16[128,128]{1,0:T(8,128)(2,1)S(1)} %add_convert_fusion.2), channel_id=1, source_target_pairs={{0,64},{32,96},{64,0},{96,32},{128,192},{160,224},{192,128},{224,1... | collective-permute-start | bytes 98312 | tf_op jit(solution)/shard_map/u_sum/ppermute | solution.py:286
  69.0 0.0 collective-permute-start.3
  69.0 1.6 %u_sum.7 = (bf16[4096,128]{1,0:T(8,128)(2,1)}, bf16[4096,128]{1,0:T(8,128)(2,1)S(1)}) custom-call(s32[1]{0:T(128)} %bitcast.half_ref, f32[128,128]{1,0:T(8,128)S(1)} %get-tuple-element.42.l_ref, bf16[2048,128]{1,0:T(8,128)(2,1)S(1)} %bitcast.6, bf16[2048,128]{1,0:T(8,128)(2,1)S(1)} %collective-permute-done.1.p_ref.pt_ref), custom_call_target="tpu_custom_call" | custom-call | flops 268435456 | bytes 6291456 | tf_op jit(solution)/shard_map/u_sum/pallas_call | solution.py:218
  70.6 0.0 collective-permute-done.5
  70.6 0.6 collective-permute-done.4
  71.2 1.7 %collective-permute-done.3 = bf16[128,128]{1,0:T(8,128)(2,1)S(1)} collective-permute-done((bf16[128,128]{1,0:T(8,128)(2,1)S(1)}, bf16[128,128]{1,0:T(8,128)(2,1)S(1)}, u32[]{:S(2)}, u32[]{:S(2)}) %collective-permute-start.3) | collective-permute-done | bytes 32800 | tf_op jit(solution)/shard_map/u_sum/ppermute | solution.py:286
  72.9 1.2 %collective-permute-start.8 = (bf16[128,128]{1,0:T(8,128)(2,1)S(1)}, bf16[128,128]{1,0:T(8,128)(2,1)S(1)}, u32[]{:S(2)}, u32[]{:S(2)}) collective-permute-start(bf16[128,128]{1,0:T(8,128)(2,1)S(1)} %add_convert_fusion.1.u_ref), channel_id=1, source_target_pairs={{0,24},{8,16},{16,8},{24,0},{1,25},{9,17},{17,9},{25,1},{2,26},{10... | collective-permute-start | bytes 98312 | tf_op jit(solution)/shard_map/u_sum/ppermute | solution.py:286
  74.1 0.7 collective-permute-start.7
  74.8 2.3 %collective-permute-start.6 = (bf16[128,128]{1,0:T(8,128)(2,1)S(1)}, bf16[128,128]{1,0:T(8,128)(2,1)S(1)}, u32[]{:S(2)}, u32[]{:S(2)}) collective-permute-start(bf16[128,128]{1,0:T(8,128)(2,1)S(1)} %add_convert_fusion.1.u_ref), channel_id=1, source_target_pairs={{0,8},{8,0},{16,24},{24,16},{1,9},{9,1},{17,25},{25,17},{2,10},{10... | collective-permute-start | bytes 98312 | tf_op jit(solution)/shard_map/u_sum/ppermute | solution.py:286
  77.1 1.0 %collective-permute-done.8.d_ref = bf16[128,128]{1,0:T(8,128)(2,1)S(1)} collective-permute-done((bf16[128,128]{1,0:T(8,128)(2,1)S(1)}, bf16[128,128]{1,0:T(8,128)(2,1)S(1)}, u32[]{:S(2)}, u32[]{:S(2)}) %collective-permute-start.8) | collective-permute-done | bytes 32800 | tf_op jit(solution)/shard_map/u_sum/ppermute | solution.py:286
  78.1 1.4 %collective-permute-done.7.b_ref = bf16[128,128]{1,0:T(8,128)(2,1)S(1)} collective-permute-done((bf16[128,128]{1,0:T(8,128)(2,1)S(1)}, bf16[128,128]{1,0:T(8,128)(2,1)S(1)}, u32[]{:S(2)}, u32[]{:S(2)}) %collective-permute-start.7) | collective-permute-done | bytes 32800 | tf_op jit(solution)/shard_map/u_sum/ppermute | solution.py:286
  79.5 0.0 collective-permute-done.6.a_ref
  79.5 2.5 %back.1 = (bf16[1,2,4096,128]{3,2,1,0:T(8,128)(2,1)}, f32[128,128]{1,0:T(8,128)}) custom-call(s32[1]{0:T(128)} %bitcast.half_ref, bf16[4096,128]{1,0:T(8,128)(2,1)S(1)} %get-tuple-element.45.f_ref, bf16[2,2048,128]{2,1,0:T(8,128)(2,1)S(1)} %get-tuple-element.31.c_ref.co_ref, bf16[2,2048,128]{2,1,0:T(8,128)(2,1)S(1)} %get-tuple-element.30.c_ref.ct_ref, ...), custom_call_target="tpu_custom_call" | custom-call | flops 268435456 | bytes 6291456 | tf_op jit(solution)/shard_map/back/pallas_call | solution.py:263
  (2 shorter events, 0.0 us)
Async XLA Ops:
  3.1 2.5 %collective-permute-start = (bf16[2048,128]{1,0:T(8,128)(2,1)S(1)}, bf16[2048,128]{1,0:T(8,128)(2,1)S(1)}, u32[]{:S(2)}, u32[]{:S(2)}) collective-permute-start(bf16[2048,128]{1,0:T(8,128)(2,1)S(1)} %get-tuple-element.29), channel_id=1, source_target_pairs={{0,1},{1,0},{2,3},{3,2},{4,5},{5,4},{6,7},{7,6},{8,9},{9,8},{10,11... | collective-permute-start | bytes 1572872 | tf_op jit(solution)/shard_map/p_partial/ppermute | solution.py:282
  56.6 1.9 %collective-permute-start.1 = (bf16[2048,128]{1,0:T(8,128)(2,1)S(1)}, bf16[2048,128]{1,0:T(8,128)(2,1)S(1)}, u32[]{:S(2)}, u32[]{:S(2)}) collective-permute-start(bf16[2048,128]{1,0:T(8,128)(2,1)S(1)} %bitcast.4), channel_id=1, source_target_pairs={{0,1},{1,0},{2,3},{3,2},{4,5},{5,4},{6,7},{7,6},{8,9},{9,8},{10,11... | collective-permute-start | bytes 1572872 | tf_op jit(solution)/shard_map/p_sum/ppermute | solution.py:282
  59.0 6.5 %collective-permute-start.2 = (bf16[128,128]{1,0:T(8,128)(2,1)S(1)}, bf16[128,128]{1,0:T(8,128)(2,1)S(1)}, u32[]{:S(2)}, u32[]{:S(2)}) collective-permute-start(bf16[128,128]{1,0:T(8,128)(2,1)S(1)} %get-tuple-element.34), channel_id=1, source_target_pairs={{0,192},{32,224},{64,128},{96,160},{128,64},{160,96},{192,0},{224,... | collective-permute-start | bytes 98312 | tf_op jit(solution)/shard_map/u_sum/ppermute | solution.py:286
  65.4 5.2 %collective-permute-start.5 = (bf16[128,128]{1,0:T(8,128)(2,1)S(1)}, bf16[128,128]{1,0:T(8,128)(2,1)S(1)}, u32[]{:S(2)}, u32[]{:S(2)}) collective-permute-start(bf16[128,128]{1,0:T(8,128)(2,1)S(1)} %add_convert_fusion.2), channel_id=1, source_target_pairs={{0,96},{32,64},{64,32},{96,0},{128,224},{160,192},{192,160},{224,1... | collective-permute-start | bytes 98312 | tf_op jit(solution)/shard_map/u_sum/ppermute | solution.py:286
  65.7 5.6 %collective-permute-start.4 = (bf16[128,128]{1,0:T(8,128)(2,1)S(1)}, bf16[128,128]{1,0:T(8,128)(2,1)S(1)}, u32[]{:S(2)}, u32[]{:S(2)}) collective-permute-start(bf16[128,128]{1,0:T(8,128)(2,1)S(1)} %add_convert_fusion.2), channel_id=1, source_target_pairs={{0,64},{32,96},{64,0},{96,32},{128,192},{160,224},{192,128},{224,1... | collective-permute-start | bytes 98312 | tf_op jit(solution)/shard_map/u_sum/ppermute | solution.py:286
  69.0 3.9 %collective-permute-start.3 = (bf16[128,128]{1,0:T(8,128)(2,1)S(1)}, bf16[128,128]{1,0:T(8,128)(2,1)S(1)}, u32[]{:S(2)}, u32[]{:S(2)}) collective-permute-start(bf16[128,128]{1,0:T(8,128)(2,1)S(1)} %add_convert_fusion.2), channel_id=1, source_target_pairs={{0,32},{32,0},{64,96},{96,64},{128,160},{160,128},{192,224},{224,1... | collective-permute-start | bytes 98312 | tf_op jit(solution)/shard_map/u_sum/ppermute | solution.py:286
  72.9 5.2 %collective-permute-start.8 = (bf16[128,128]{1,0:T(8,128)(2,1)S(1)}, bf16[128,128]{1,0:T(8,128)(2,1)S(1)}, u32[]{:S(2)}, u32[]{:S(2)}) collective-permute-start(bf16[128,128]{1,0:T(8,128)(2,1)S(1)} %add_convert_fusion.1.u_ref), channel_id=1, source_target_pairs={{0,24},{8,16},{16,8},{24,0},{1,25},{9,17},{17,9},{25,1},{2,26},{10... | collective-permute-start | bytes 98312 | tf_op jit(solution)/shard_map/u_sum/ppermute | solution.py:286
  74.1 5.4 %collective-permute-start.7 = (bf16[128,128]{1,0:T(8,128)(2,1)S(1)}, bf16[128,128]{1,0:T(8,128)(2,1)S(1)}, u32[]{:S(2)}, u32[]{:S(2)}) collective-permute-start(bf16[128,128]{1,0:T(8,128)(2,1)S(1)} %add_convert_fusion.1.u_ref), channel_id=1, source_target_pairs={{0,16},{8,24},{16,0},{24,8},{1,17},{9,25},{17,1},{25,9},{2,18},{10... | collective-permute-start | bytes 98312 | tf_op jit(solution)/shard_map/u_sum/ppermute | solution.py:286
  74.8 4.7 %collective-permute-start.6 = (bf16[128,128]{1,0:T(8,128)(2,1)S(1)}, bf16[128,128]{1,0:T(8,128)(2,1)S(1)}, u32[]{:S(2)}, u32[]{:S(2)}) collective-permute-start(bf16[128,128]{1,0:T(8,128)(2,1)S(1)} %add_convert_fusion.1.u_ref), channel_id=1, source_target_pairs={{0,8},{8,0},{16,24},{24,16},{1,9},{9,1},{17,25},{25,17},{2,10},{10... | collective-permute-start | bytes 98312 | tf_op jit(solution)/shard_map/u_sum/ppermute | solution.py:286

commit v6 on v5

--- a/solution.py
+++ b/solution.py
@@ -75,10 +75,10 @@
 
 
 def sum_copies_body(x_ref, o_ref):
-    total = x_ref[0].astype(F32)
-    for k in range(1, x_ref.shape[0]):
-        total = total + x_ref[k].astype(F32)
-    total = total.astype(BF)
+    terms = [x_ref[k].astype(F32) for k in range(x_ref.shape[0])]
+    while len(terms) > 1:
+        terms = [a + b for a, b in zip(terms[::2], terms[1::2])]
+    total = terms[0].astype(BF)
     for k in range(o_ref.shape[0]):
         o_ref[k] = total
 
@@ -306,7 +306,9 @@
         chip = (p_own + p_got.astype(F32)).astype(BF)
     with jax.named_scope("p_sum"):
         parts = exchange(chip.reshape(NX * NY, BLK, RANK2), ("x", "y"))
-        parts = exchange(sum_copies(parts, NZ), "z")
+        part = sum_copies(parts, 1)[0]
+        part = plus(part, pair(part, "z", NZ, 6))
+        parts = jnp.stack([part] + [pair(part, "z", NZ, k) for k in (1, 2, 3)])
         p_mine = exchange(sum_copies(parts, NX * NY), ("x", "y")).reshape(HALF, RANK2)
         p_theirs = swap_cores(p_mine)
     with jax.named_scope("u_sum"):

time: 82.2 us -> 80 us (0.973)
  blocking collectives: 50.7 us -> 32.4 us
  starting transfers between devices: 8.35 us -> 21 us
  waiting for transfers between devices: 8.78 us -> 11.8 us
    all_to_all x3 -> x2, blocking collectives: 50.7 us -> 32.4 us  [exchange(): return lax.all_to_all(x, axes, 0, 0)]
    ppermute x7 -> x11, starting transfers between devices: 8.25 us -> 20.9 us  [pair(): return lax.ppermute(x, axis, [(i, i ^ flip) for i in range(size)])]
    ppermute x7 -> x11, waiting for transfers between devices: 7.36 us -> 10.4 us  [pair(): return lax.ppermute(x, axis, [(i, i ^ flip) for i in range(size)])]
  transfers between devices with their start and end apart: 9 -> 13, of which waited for: 6 -> 9; matrix products, arithmetic and copies ran while one was open for 0% -> 0% of each run, Pallas kernels for 10% -> 10%
where the time goes in v6:
time: 80 us; the launch traced here: 79.5 us
  blocking collectives  32.4 us (40%)
  starting transfers between devices  21 us (26%)
  Pallas kernels  13.3 us (17%)
  waiting for transfers between devices  11.8 us (15%)
    all_to_all x2, blocking collectives, exchange(): return lax.all_to_all(x, axes, 0, 0)  32.4 us
    ppermute x11, starting transfers between devices, pair(): return lax.ppermute(x, axis, [(i, i ^ flip) for i in range(size)])  20.9 us
    ppermute x11, waiting for transfers between devices, pair(): return lax.ppermute(x, axis, [(i, i ^ flip) for i in range(size)])  10.4 us
    pallas_call x2, Pallas kernels, front(): pl.pallas_call(front_body, in_specs=[pl.BlockSpec(memory_space=pltpu.SMEM...  4.87 us
    pallas_call x1, Pallas kernels, inverse(): pl.pallas_call(inverse_body, in_specs=[pl.BlockSpec(memory_space=pltpu.SM...  3.31 us
    pallas_call x1, Pallas kernels, back(): pl.pallas_call(back_body, in_specs=[pl.BlockSpec(memory_space=pltpu.SMEM)...  2.45 us
    pallas_call x1, Pallas kernels, factor(): pl.pallas_call(factor_body, in_specs=[pl.BlockSpec(memory_space=pltpu.SME...  1.61 us
  transfers between devices with their start and end apart: 13, of which 9 were waited for; matrix products, arithmetic and copies ran while one was open for 0% of the time, Pallas kernels for 10%

profile of v6, /device:TPU:32, one launch (start us, length us, event | category | flops | bytes accessed | tf_op | source)
XLA Modules:
  0.0 79.5 jit_solution(7325242925050062329)
XLA Ops:
  0.6 2.4 %p_partial.3 = (bf16[2,2048,128]{2,1,0:T(8,128)(2,1)S(1)}, bf16[2,2048,128]{2,1,0:T(8,128)(2,1)S(1)}, bf16[2048,128]{1,0:T(8,128)(2,1)S(1)}) custom-call(s32[1]{0:T(128)} %bitcast.1.half_ref, bf16[1,2,4096,128]{3,2,1,0:T(8,128)(2,1)} %g_hbm.3, bf16[1,2,4096,128]{3,2,1,0:T(8,128)(2,1)} %m_hbm.3, bf16[1,2,4096,128]{3,2,1,0:T(8,128)(2,1)} %e_hbm.3, ...), custom_call_target="tpu_custom_call" | custom-call | flops 134217728 | bytes 4194304 | tf_op jit(solution)/shard_map/p_partial/pallas_call | solution.py:65
  3.1 0.1 collective-permute-start
  3.2 2.4 %p_partial.2 = (bf16[2,2048,128]{2,1,0:T(8,128)(2,1)S(1)}, bf16[2,2048,128]{2,1,0:T(8,128)(2,1)S(1)}, f32[2048,128]{1,0:T(8,128)S(1)}) custom-call(s32[1]{0:T(128)} %bitcast.half_ref, bf16[1,2,4096,128]{3,2,1,0:T(8,128)(2,1)} %g_hbm.3, bf16[1,2,4096,128]{3,2,1,0:T(8,128)(2,1)} %m_hbm.3, bf16[1,2,4096,128]{3,2,1,0:T(8,128)(2,1)} %e_hbm.3, bf16[128,128]{1,0:T(8,128)(2,1)} %q_hbm.3), custom_call_target="tpu_custom_call" | custom-call | flops 134217728 | bytes 4194304 | tf_op jit(solution)/shard_map/p_partial/pallas_call | solution.py:65
  5.6 0.0 collective-permute-done
  5.6 0.1 add_convert_fusion
  5.7 19.0 %all_to_all.10.x_ref = bf16[16,128,128]{2,1,0:T(8,128)(2,1)S(1)} all-to-all(bf16[16,128,128]{2,1,0:T(8,128)(2,1)S(1)} %bitcast.14), channel_id=1, replica_groups=mesh['z'=8,'x'=4,'y'=4,'c'=2] {'x','y'}, dimensions={0} | all-to-all | bytes 1048576 | tf_op jit(solution)/shard_map/p_sum/all_to_all | solution.py:294
  24.7 0.1 p_sum.2
  24.8 5.5 %collective-permute-start.1 = (bf16[128,128]{1,0:T(8,128)(2,1)S(1)}, bf16[128,128]{1,0:T(8,128)(2,1)S(1)}, u32[]{:S(2)}, u32[]{:S(2)}) collective-permute-start(bf16[128,128]{1,0:T(8,128)(2,1)S(1)} %bitcast.13), channel_id=1, source_target_pairs={{0,192},{32,224},{64,128},{96,160},{128,64},{160,96},{192,0},{224,... | collective-permute-start | bytes 98312 | tf_op jit(solution)/shard_map/p_sum/ppermute | solution.py:286
  30.3 1.9 %collective-permute-done.1 = bf16[128,128]{1,0:T(8,128)(2,1)S(1)} collective-permute-done((bf16[128,128]{1,0:T(8,128)(2,1)S(1)}, bf16[128,128]{1,0:T(8,128)(2,1)S(1)}, u32[]{:S(2)}, u32[]{:S(2)}) %collective-permute-start.1) | collective-permute-done | bytes 32800 | tf_op jit(solution)/shard_map/p_sum/ppermute | solution.py:286
  32.2 1.1 %collective-permute-start.4 = (bf16[128,128]{1,0:T(8,128)(2,1)S(1)}, bf16[128,128]{1,0:T(8,128)(2,1)S(1)}, u32[]{:S(2)}, u32[]{:S(2)}) collective-permute-start(bf16[128,128]{1,0:T(8,128)(2,1)S(1)} %add_convert_fusion.3), channel_id=1, source_target_pairs={{0,96},{32,64},{64,32},{96,0},{128,224},{160,192},{192,160},{224,1... | collective-permute-start | bytes 98312 | tf_op jit(solution)/shard_map/p_sum/ppermute | solution.py:286
  33.3 2.4 %collective-permute-start.3 = (bf16[128,128]{1,0:T(8,128)(2,1)S(1)}, bf16[128,128]{1,0:T(8,128)(2,1)S(1)}, u32[]{:S(2)}, u32[]{:S(2)}) collective-permute-start(bf16[128,128]{1,0:T(8,128)(2,1)S(1)} %add_convert_fusion.3), channel_id=1, source_target_pairs={{0,64},{32,96},{64,0},{96,32},{128,192},{160,224},{192,128},{224,1... | collective-permute-start | bytes 98312 | tf_op jit(solution)/shard_map/p_sum/ppermute | solution.py:286
  35.7 0.1 collective-permute-start.2
  35.8 0.4 collective-permute-done.4
  36.2 1.9 %collective-permute-done.3 = bf16[128,128]{1,0:T(8,128)(2,1)S(1)} collective-permute-done((bf16[128,128]{1,0:T(8,128)(2,1)S(1)}, bf16[128,128]{1,0:T(8,128)(2,1)S(1)}, u32[]{:S(2)}, u32[]{:S(2)}) %collective-permute-start.3) | collective-permute-done | bytes 32800 | tf_op jit(solution)/shard_map/p_sum/ppermute | solution.py:286
  38.1 1.5 %collective-permute-done.2 = bf16[128,128]{1,0:T(8,128)(2,1)S(1)} collective-permute-done((bf16[128,128]{1,0:T(8,128)(2,1)S(1)}, bf16[128,128]{1,0:T(8,128)(2,1)S(1)}, u32[]{:S(2)}, u32[]{:S(2)}) %collective-permute-start.2) | collective-permute-done | bytes 32800 | tf_op jit(solution)/shard_map/p_sum/ppermute | solution.py:286
  39.6 13.4 %all_to_all.11 = bf16[16,128,128]{2,1,0:T(8,128)(2,1)S(1)} all-to-all(bf16[16,128,128]{2,1,0:T(8,128)(2,1)S(1)} %p_sum.3), channel_id=1, replica_groups=mesh['z'=8,'x'=4,'y'=4,'c'=2] {'x','y'}, dimensions={0} | all-to-all | bytes 1048576 | tf_op jit(solution)/shard_map/p_sum/all_to_all | solution.py:294
  53.0 0.5 u_sum.4
  53.5 1.4 %collective-permute-done.5.p_ref.pt_ref = bf16[2048,128]{1,0:T(8,128)(2,1)S(1)} collective-permute-done((bf16[2048,128]{1,0:T(8,128)(2,1)S(1)}, bf16[2048,128]{1,0:T(8,128)(2,1)S(1)}, u32[]{:S(2)}, u32[]{:S(2)}) %collective-permute-start.5) | collective-permute-done | bytes 524320 | tf_op jit(solution)/shard_map/p_sum/ppermute | solution.py:282
  54.9 0.5 u_sum.5
  55.4 3.7 %collective-permute-start.6 = (bf16[128,128]{1,0:T(8,128)(2,1)S(1)}, bf16[128,128]{1,0:T(8,128)(2,1)S(1)}, u32[]{:S(2)}, u32[]{:S(2)}) collective-permute-start(bf16[128,128]{1,0:T(8,128)(2,1)S(1)} %get-tuple-element.34), channel_id=1, source_target_pairs={{0,192},{32,224},{64,128},{96,160},{128,64},{160,96},{192,0},{224,... | collective-permute-start | bytes 98312 | tf_op jit(solution)/shard_map/u_sum/ppermute | solution.py:286
  59.1 3.3 %u_sum.6 = (f32[128,128]{1,0:T(8,128)S(1)}, bf16[1,2,4096,128]{3,2,1,0:T(8,128)(2,1)}) custom-call(s32[1]{0:T(128)} %bitcast.half_ref, f32[128,128]{1,0:T(8,128)S(1)} %get-tuple-element.35.g_ref, bf16[2,2048,128]{2,1,0:T(8,128)(2,1)S(1)} %get-tuple-element.36.mo_ref, bf16[2,2048,128]{2,1,0:T(8,128)(2,1)S(1)} %get-tuple-element.37.mt_ref), custom_call_target="tpu_custom_call" | custom-call | flops 262144 | bytes 6291456 | tf_op jit(solution)/shard_map/u_sum/pallas_call | solution.py:186
  62.5 1.1 %collective-permute-start.9 = (bf16[128,128]{1,0:T(8,128)(2,1)S(1)}, bf16[128,128]{1,0:T(8,128)(2,1)S(1)}, u32[]{:S(2)}, u32[]{:S(2)}) collective-permute-start(bf16[128,128]{1,0:T(8,128)(2,1)S(1)} %add_convert_fusion.2), channel_id=1, source_target_pairs={{0,96},{32,64},{64,32},{96,0},{128,224},{160,192},{192,160},{224,1... | collective-permute-start | bytes 98312 | tf_op jit(solution)/shard_map/u_sum/ppermute | solution.py:286
  63.5 2.9 %collective-permute-start.8 = (bf16[128,128]{1,0:T(8,128)(2,1)S(1)}, bf16[128,128]{1,0:T(8,128)(2,1)S(1)}, u32[]{:S(2)}, u32[]{:S(2)}) collective-permute-start(bf16[128,128]{1,0:T(8,128)(2,1)S(1)} %add_convert_fusion.2), channel_id=1, source_target_pairs={{0,64},{32,96},{64,0},{96,32},{128,192},{160,224},{192,128},{224,1... | collective-permute-start | bytes 98312 | tf_op jit(solution)/shard_map/u_sum/ppermute | solution.py:286
  66.5 1.6 %u_sum.7 = (bf16[4096,128]{1,0:T(8,128)(2,1)}, bf16[4096,128]{1,0:T(8,128)(2,1)S(1)}) custom-call(s32[1]{0:T(128)} %bitcast.half_ref, f32[128,128]{1,0:T(8,128)S(1)} %get-tuple-element.42.l_ref, bf16[2048,128]{1,0:T(8,128)(2,1)S(1)} %bitcast.12, bf16[2048,128]{1,0:T(8,128)(2,1)S(1)} %collective-permute-done.5.p_ref.pt_ref), custom_call_target="tpu_custom_call" | custom-call | flops 268435456 | bytes 6291456 | tf_op jit(solution)/shard_map/u_sum/pallas_call | solution.py:218
  68.1 0.6 collective-permute-done.8
  68.7 1.7 %collective-permute-done.7 = bf16[128,128]{1,0:T(8,128)(2,1)S(1)} collective-permute-done((bf16[128,128]{1,0:T(8,128)(2,1)S(1)}, bf16[128,128]{1,0:T(8,128)(2,1)S(1)}, u32[]{:S(2)}, u32[]{:S(2)}) %collective-permute-start.7) | collective-permute-done | bytes 32800 | tf_op jit(solution)/shard_map/u_sum/ppermute | solution.py:286
  70.4 1.2 %collective-permute-start.12 = (bf16[128,128]{1,0:T(8,128)(2,1)S(1)}, bf16[128,128]{1,0:T(8,128)(2,1)S(1)}, u32[]{:S(2)}, u32[]{:S(2)}) collective-permute-start(bf16[128,128]{1,0:T(8,128)(2,1)S(1)} %add_convert_fusion.1.u_ref), channel_id=1, source_target_pairs={{0,24},{8,16},{16,8},{24,0},{1,25},{9,17},{17,9},{25,1},{2,26},{10... | collective-permute-start | bytes 98312 | tf_op jit(solution)/shard_map/u_sum/ppermute | solution.py:286
  71.6 0.7 collective-permute-start.11
  72.3 2.3 %collective-permute-start.10 = (bf16[128,128]{1,0:T(8,128)(2,1)S(1)}, bf16[128,128]{1,0:T(8,128)(2,1)S(1)}, u32[]{:S(2)}, u32[]{:S(2)}) collective-permute-start(bf16[128,128]{1,0:T(8,128)(2,1)S(1)} %add_convert_fusion.1.u_ref), channel_id=1, source_target_pairs={{0,8},{8,0},{16,24},{24,16},{1,9},{9,1},{17,25},{25,17},{2,10},{10... | collective-permute-start | bytes 98312 | tf_op jit(solution)/shard_map/u_sum/ppermute | solution.py:286
  74.6 1.0 %collective-permute-done.12.d_ref = bf16[128,128]{1,0:T(8,128)(2,1)S(1)} collective-permute-done((bf16[128,128]{1,0:T(8,128)(2,1)S(1)}, bf16[128,128]{1,0:T(8,128)(2,1)S(1)}, u32[]{:S(2)}, u32[]{:S(2)}) %collective-permute-start.12) | collective-permute-done | bytes 32800 | tf_op jit(solution)/shard_map/u_sum/ppermute | solution.py:286
  75.6 1.4 %collective-permute-done.11.b_ref = bf16[128,128]{1,0:T(8,128)(2,1)S(1)} collective-permute-done((bf16[128,128]{1,0:T(8,128)(2,1)S(1)}, bf16[128,128]{1,0:T(8,128)(2,1)S(1)}, u32[]{:S(2)}, u32[]{:S(2)}) %collective-permute-start.11) | collective-permute-done | bytes 32800 | tf_op jit(solution)/shard_map/u_sum/ppermute | solution.py:286
  77.0 2.5 %back.1 = (bf16[1,2,4096,128]{3,2,1,0:T(8,128)(2,1)}, f32[128,128]{1,0:T(8,128)}) custom-call(s32[1]{0:T(128)} %bitcast.half_ref, bf16[4096,128]{1,0:T(8,128)(2,1)S(1)} %get-tuple-element.45.f_ref, bf16[2,2048,128]{2,1,0:T(8,128)(2,1)S(1)} %get-tuple-element.31.c_ref.co_ref, bf16[2,2048,128]{2,1,0:T(8,128)(2,1)S(1)} %get-tuple-element.30.c_ref.ct_ref, ...), custom_call_target="tpu_custom_call" | custom-call | flops 268435456 | bytes 6291456 | tf_op jit(solution)/shard_map/back/pallas_call | solution.py:263
  (10 shorter events, 0.1 us)
Async XLA Ops:
  3.1 2.5 %collective-permute-start = (bf16[2048,128]{1,0:T(8,128)(2,1)S(1)}, bf16[2048,128]{1,0:T(8,128)(2,1)S(1)}, u32[]{:S(2)}, u32[]{:S(2)}) collective-permute-start(bf16[2048,128]{1,0:T(8,128)(2,1)S(1)} %get-tuple-element.29), channel_id=1, source_target_pairs={{0,1},{1,0},{2,3},{3,2},{4,5},{5,4},{6,7},{7,6},{8,9},{9,8},{10,11... | collective-permute-start | bytes 1572872 | tf_op jit(solution)/shard_map/p_partial/ppermute | solution.py:282
  24.8 7.4 %collective-permute-start.1 = (bf16[128,128]{1,0:T(8,128)(2,1)S(1)}, bf16[128,128]{1,0:T(8,128)(2,1)S(1)}, u32[]{:S(2)}, u32[]{:S(2)}) collective-permute-start(bf16[128,128]{1,0:T(8,128)(2,1)S(1)} %bitcast.13), channel_id=1, source_target_pairs={{0,192},{32,224},{64,128},{96,160},{128,64},{160,96},{192,0},{224,... | collective-permute-start | bytes 98312 | tf_op jit(solution)/shard_map/p_sum/ppermute | solution.py:286
  32.2 4.0 %collective-permute-start.4 = (bf16[128,128]{1,0:T(8,128)(2,1)S(1)}, bf16[128,128]{1,0:T(8,128)(2,1)S(1)}, u32[]{:S(2)}, u32[]{:S(2)}) collective-permute-start(bf16[128,128]{1,0:T(8,128)(2,1)S(1)} %add_convert_fusion.3), channel_id=1, source_target_pairs={{0,96},{32,64},{64,32},{96,0},{128,224},{160,192},{192,160},{224,1... | collective-permute-start | bytes 98312 | tf_op jit(solution)/shard_map/p_sum/ppermute | solution.py:286
  33.3 4.8 %collective-permute-start.3 = (bf16[128,128]{1,0:T(8,128)(2,1)S(1)}, bf16[128,128]{1,0:T(8,128)(2,1)S(1)}, u32[]{:S(2)}, u32[]{:S(2)}) collective-permute-start(bf16[128,128]{1,0:T(8,128)(2,1)S(1)} %add_convert_fusion.3), channel_id=1, source_target_pairs={{0,64},{32,96},{64,0},{96,32},{128,192},{160,224},{192,128},{224,1... | collective-permute-start | bytes 98312 | tf_op jit(solution)/shard_map/p_sum/ppermute | solution.py:286
  35.7 3.9 %collective-permute-start.2 = (bf16[128,128]{1,0:T(8,128)(2,1)S(1)}, bf16[128,128]{1,0:T(8,128)(2,1)S(1)}, u32[]{:S(2)}, u32[]{:S(2)}) collective-permute-start(bf16[128,128]{1,0:T(8,128)(2,1)S(1)} %add_convert_fusion.3), channel_id=1, source_target_pairs={{0,32},{32,0},{64,96},{96,64},{128,160},{160,128},{192,224},{224,1... | collective-permute-start | bytes 98312 | tf_op jit(solution)/shard_map/p_sum/ppermute | solution.py:286
  53.0 1.9 %collective-permute-start.5 = (bf16[2048,128]{1,0:T(8,128)(2,1)S(1)}, bf16[2048,128]{1,0:T(8,128)(2,1)S(1)}, u32[]{:S(2)}, u32[]{:S(2)}) collective-permute-start(bf16[2048,128]{1,0:T(8,128)(2,1)S(1)} %bitcast.10), channel_id=1, source_target_pairs={{0,1},{1,0},{2,3},{3,2},{4,5},{5,4},{6,7},{7,6},{8,9},{9,8},{10,11... | collective-permute-start | bytes 1572872 | tf_op jit(solution)/shard_map/p_sum/ppermute | solution.py:282
  55.4 7.0 %collective-permute-start.6 = (bf16[128,128]{1,0:T(8,128)(2,1)S(1)}, bf16[128,128]{1,0:T(8,128)(2,1)S(1)}, u32[]{:S(2)}, u32[]{:S(2)}) collective-permute-start(bf16[128,128]{1,0:T(8,128)(2,1)S(1)} %get-tuple-element.34), channel_id=1, source_target_pairs={{0,192},{32,224},{64,128},{96,160},{128,64},{160,96},{192,0},{224,... | collective-permute-start | bytes 98312 | tf_op jit(solution)/shard_map/u_sum/ppermute | solution.py:286
  62.5 5.6 %collective-permute-start.9 = (bf16[128,128]{1,0:T(8,128)(2,1)S(1)}, bf16[128,128]{1,0:T(8,128)(2,1)S(1)}, u32[]{:S(2)}, u32[]{:S(2)}) collective-permute-start(bf16[128,128]{1,0:T(8,128)(2,1)S(1)} %add_convert_fusion.2), channel_id=1, source_target_pairs={{0,96},{32,64},{64,32},{96,0},{128,224},{160,192},{192,160},{224,1... | collective-permute-start | bytes 98312 | tf_op jit(solution)/shard_map/u_sum/ppermute | solution.py:286
  63.5 5.2 %collective-permute-start.8 = (bf16[128,128]{1,0:T(8,128)(2,1)S(1)}, bf16[128,128]{1,0:T(8,128)(2,1)S(1)}, u32[]{:S(2)}, u32[]{:S(2)}) collective-permute-start(bf16[128,128]{1,0:T(8,128)(2,1)S(1)} %add_convert_fusion.2), channel_id=1, source_target_pairs={{0,64},{32,96},{64,0},{96,32},{128,192},{160,224},{192,128},{224,1... | collective-permute-start | bytes 98312 | tf_op jit(solution)/shard_map/u_sum/ppermute | solution.py:286
  66.5 3.9 %collective-permute-start.7 = (bf16[128,128]{1,0:T(8,128)(2,1)S(1)}, bf16[128,128]{1,0:T(8,128)(2,1)S(1)}, u32[]{:S(2)}, u32[]{:S(2)}) collective-permute-start(bf16[128,128]{1,0:T(8,128)(2,1)S(1)} %add_convert_fusion.2), channel_id=1, source_target_pairs={{0,32},{32,0},{64,96},{96,64},{128,160},{160,128},{192,224},{224,1... | collective-permute-start | bytes 98312 | tf_op jit(solution)/shard_map/u_sum/ppermute | solution.py:286
  70.4 5.2 %collective-permute-start.12 = (bf16[128,128]{1,0:T(8,128)(2,1)S(1)}, bf16[128,128]{1,0:T(8,128)(2,1)S(1)}, u32[]{:S(2)}, u32[]{:S(2)}) collective-permute-start(bf16[128,128]{1,0:T(8,128)(2,1)S(1)} %add_convert_fusion.1.u_ref), channel_id=1, source_target_pairs={{0,24},{8,16},{16,8},{24,0},{1,25},{9,17},{17,9},{25,1},{2,26},{10... | collective-permute-start | bytes 98312 | tf_op jit(solution)/shard_map/u_sum/ppermute | solution.py:286
  71.6 5.4 %collective-permute-start.11 = (bf16[128,128]{1,0:T(8,128)(2,1)S(1)}, bf16[128,128]{1,0:T(8,128)(2,1)S(1)}, u32[]{:S(2)}, u32[]{:S(2)}) collective-permute-start(bf16[128,128]{1,0:T(8,128)(2,1)S(1)} %add_convert_fusion.1.u_ref), channel_id=1, source_target_pairs={{0,16},{8,24},{16,0},{24,8},{1,17},{9,25},{17,1},{25,9},{2,18},{10... | collective-permute-start | bytes 98312 | tf_op jit(solution)/shard_map/u_sum/ppermute | solution.py:286
  72.3 4.7 %collective-permute-start.10 = (bf16[128,128]{1,0:T(8,128)(2,1)S(1)}, bf16[128,128]{1,0:T(8,128)(2,1)S(1)}, u32[]{:S(2)}, u32[]{:S(2)}) collective-permute-start(bf16[128,128]{1,0:T(8,128)(2,1)S(1)} %add_convert_fusion.1.u_ref), channel_id=1, source_target_pairs={{0,8},{8,0},{16,24},{24,16},{1,9},{9,1},{17,25},{25,17},{2,10},{10... | collective-permute-start | bytes 98312 | tf_op jit(solution)/shard_map/u_sum/ppermute | solution.py:286

commit v7 on v6

--- a/solution.py
+++ b/solution.py
@@ -169,29 +169,37 @@
         both = out
 
 
-def inverse_body(half_ref, g_ref, mo_ref, mt_ref, o_ref, m_hbm, sem):
+def inverse(gram):
+    return pl.pallas_call(
+        invert,
+        out_shape=jax.ShapeDtypeStruct((RANK2, RANK2), F32),
+        compiler_params=pltpu.CompilerParams(vmem_limit_bytes=16 * MIB),
+        cost_estimate=pl.CostEstimate(flops=64**3, bytes_accessed=6 * MIB, transcendentals=128),
+    )(gram)
+
+
+def store_body(half_ref, own_ref, other_ref, m_hbm, sem):
     copies = []
-    for i, ref in enumerate((mo_ref, mt_ref)):
+    for i, ref in enumerate((own_ref, other_ref)):
         half = half_ref[0] if i == 0 else 1 - half_ref[0]
         there = pl.ds(pl.multiple_of(half * HALF, HALF), HALF)
         copies.append(pltpu.make_async_copy(ref, m_hbm.at[0, :, there], sem.at[i]))
         copies[-1].start()
-    invert(g_ref, o_ref)
     for copy in copies:
         copy.wait()
 
 
-def inverse(half, gram, mo_own, mo_other):
+def store(half, own, other):
     vmem = pl.BlockSpec(memory_space=pltpu.VMEM)
     return pl.pallas_call(
-        inverse_body,
-        in_specs=[pl.BlockSpec(memory_space=pltpu.SMEM), vmem, vmem, vmem],
-        out_specs=[vmem, pl.BlockSpec(memory_space=pltpu.HBM)],
-        out_shape=[jax.ShapeDtypeStruct((RANK2, RANK2), F32), jax.ShapeDtypeStruct((1, 2, ROWS, COLS), BF)],
+        store_body,
+        in_specs=[pl.BlockSpec(memory_space=pltpu.SMEM), vmem, vmem],
+        out_specs=pl.BlockSpec(memory_space=pltpu.HBM),
+        out_shape=jax.ShapeDtypeStruct((1, 2, ROWS, COLS), BF),
         scratch_shapes=[pltpu.SemaphoreType.DMA((2,))],
         compiler_params=pltpu.CompilerParams(vmem_limit_bytes=16 * MIB),
-        cost_estimate=pl.CostEstimate(flops=64**3, bytes_accessed=6 * MIB, transcendentals=128),
-    )(half, gram, mo_own, mo_other)
+        cost_estimate=pl.CostEstimate(flops=0, bytes_accessed=4 * MIB, transcendentals=0),
+    )(half, own, other)
 
 
 def factor_body(half_ref, l_ref, po_ref, pt_ref, p_hbm, f_ref, w_ref, sem):
@@ -308,7 +316,9 @@
         parts = exchange(chip.reshape(NX * NY, BLK, RANK2), ("x", "y"))
         part = sum_copies(parts, 1)[0]
         part = plus(part, pair(part, "z", NZ, 6))
-        parts = jnp.stack([part] + [pair(part, "z", NZ, k) for k in (1, 2, 3)])
+        got = [pair(part, "z", NZ, k) for k in (1, 2, 3)]
+        got, momentum_out = lax.optimization_barrier((got, store(mine, mo_own, mo_other)))
+        parts = jnp.stack([part] + got)
         p_mine = exchange(sum_copies(parts, NX * NY), ("x", "y")).reshape(HALF, RANK2)
         p_theirs = swap_cores(p_mine)
     with jax.named_scope("u_sum"):
@@ -319,7 +329,7 @@
             return ((u + a) + (b + d)).astype(BF)
 
         got = pair(u, "z", NZ, 6)
-        got, inv, momentum_out = lax.optimization_barrier((got, *inverse(mine, gram, mo_own, mo_other)))
+        got, inv = lax.optimization_barrier((got, inverse(gram)))
         u = plus(u, got)
         got = [pair(u, "z", NZ, k) for k in (1, 2, 3)]
         got, p_factor, f = lax.optimization_barrier((got, *factor(mine, inv, p_mine, p_theirs)))

time: 80 us -> 79.1 us (0.989)
  waiting for transfers between devices: 11.8 us -> 11 us
    ppermute x11, waiting for transfers between devices: 10.4 us -> 9.53 us  [pair(): return lax.ppermute(x, axis, [(i, i ^ flip) for i in range(size)])]
    pallas_call x1 -> x2, Pallas kernels: 3.31 us -> 3.43 us  [the longest x1 2.1 us: inverse(): pl.pallas_call(invert, out_shape=jax.ShapeDtypeStruct((RANK2, RANK2), F32...]
where the time goes in v7:
time: 79.1 us; the launch traced here: 78.3 us
  blocking collectives  32.4 us (41%)
  starting transfers between devices  20.6 us (26%)
  Pallas kernels  13.4 us (17%)
  waiting for transfers between devices  11 us (14%)
    all_to_all x2, blocking collectives, exchange(): return lax.all_to_all(x, axes, 0, 0)  32.4 us
    ppermute x11, starting transfers between devices, pair(): return lax.ppermute(x, axis, [(i, i ^ flip) for i in range(size)])  20.5 us
    ppermute x11, waiting for transfers between devices, pair(): return lax.ppermute(x, axis, [(i, i ^ flip) for i in range(size)])  9.53 us
    pallas_call x2, Pallas kernels, front(): pl.pallas_call(front_body, in_specs=[pl.BlockSpec(memory_space=pltpu.SMEM...  4.87 us
    pallas_call x1, Pallas kernels, back(): pl.pallas_call(back_body, in_specs=[pl.BlockSpec(memory_space=pltpu.SMEM)...  2.46 us
    pallas_call x1, Pallas kernels, inverse(): pl.pallas_call(invert, out_shape=jax.ShapeDtypeStruct((RANK2, RANK2), F32...  2.1 us
    pallas_call x1, Pallas kernels, factor(): pl.pallas_call(factor_body, in_specs=[pl.BlockSpec(memory_space=pltpu.SME...  1.61 us
  transfers between devices with their start and end apart: 13, of which 9 were waited for; matrix products, arithmetic and copies ran while one was open for 0% of the time, Pallas kernels for 10%

profile of v7, /device:TPU:32, one launch (start us, length us, event | category | flops | bytes accessed | tf_op | source)
XLA Modules:
  0.0 78.3 jit_solution(1150470195066174174)
XLA Ops:
  0.6 2.4 %p_partial.3 = (bf16[2,2048,128]{2,1,0:T(8,128)(2,1)S(1)}, bf16[2,2048,128]{2,1,0:T(8,128)(2,1)S(1)}, bf16[2048,128]{1,0:T(8,128)(2,1)S(1)}) custom-call(s32[1]{0:T(128)} %bitcast.1.half_ref, bf16[1,2,4096,128]{3,2,1,0:T(8,128)(2,1)} %g_hbm.3, bf16[1,2,4096,128]{3,2,1,0:T(8,128)(2,1)} %m_hbm.3, bf16[1,2,4096,128]{3,2,1,0:T(8,128)(2,1)} %e_hbm.3, ...), custom_call_target="tpu_custom_call" | custom-call | flops 134217728 | bytes 4194304 | tf_op jit(solution)/shard_map/p_partial/pallas_call | solution.py:65
  3.1 0.1 collective-permute-start
  3.2 2.4 %p_partial.2 = (bf16[2,2048,128]{2,1,0:T(8,128)(2,1)S(1)}, bf16[2,2048,128]{2,1,0:T(8,128)(2,1)S(1)}, f32[2048,128]{1,0:T(8,128)S(1)}) custom-call(s32[1]{0:T(128)} %bitcast.half_ref, bf16[1,2,4096,128]{3,2,1,0:T(8,128)(2,1)} %g_hbm.3, bf16[1,2,4096,128]{3,2,1,0:T(8,128)(2,1)} %m_hbm.3, bf16[1,2,4096,128]{3,2,1,0:T(8,128)(2,1)} %e_hbm.3, bf16[128,128]{1,0:T(8,128)(2,1)} %q_hbm.3), custom_call_target="tpu_custom_call" | custom-call | flops 134217728 | bytes 4194304 | tf_op jit(solution)/shard_map/p_partial/pallas_call | solution.py:65
  5.6 0.1 add_convert_fusion
  5.7 19.0 %all_to_all.10.x_ref = bf16[16,128,128]{2,1,0:T(8,128)(2,1)S(1)} all-to-all(bf16[16,128,128]{2,1,0:T(8,128)(2,1)S(1)} %bitcast.14), channel_id=1, replica_groups=mesh['z'=8,'x'=4,'y'=4,'c'=2] {'x','y'}, dimensions={0} | all-to-all | bytes 1048576 | tf_op jit(solution)/shard_map/p_sum/all_to_all | solution.py:302
  24.8 5.5 %collective-permute-start.1 = (bf16[128,128]{1,0:T(8,128)(2,1)S(1)}, bf16[128,128]{1,0:T(8,128)(2,1)S(1)}, u32[]{:S(2)}, u32[]{:S(2)}) collective-permute-start(bf16[128,128]{1,0:T(8,128)(2,1)S(1)} %bitcast.13), channel_id=1, source_target_pairs={{0,192},{32,224},{64,128},{96,160},{128,64},{160,96},{192,0},{224,... | collective-permute-start | bytes 98312 | tf_op jit(solution)/shard_map/p_sum/ppermute | solution.py:294
  30.3 1.9 %collective-permute-done.1 = bf16[128,128]{1,0:T(8,128)(2,1)S(1)} collective-permute-done((bf16[128,128]{1,0:T(8,128)(2,1)S(1)}, bf16[128,128]{1,0:T(8,128)(2,1)S(1)}, u32[]{:S(2)}, u32[]{:S(2)}) %collective-permute-start.1) | collective-permute-done | bytes 32800 | tf_op jit(solution)/shard_map/p_sum/ppermute | solution.py:294
  32.2 1.1 %collective-permute-start.4 = (bf16[128,128]{1,0:T(8,128)(2,1)S(1)}, bf16[128,128]{1,0:T(8,128)(2,1)S(1)}, u32[]{:S(2)}, u32[]{:S(2)}) collective-permute-start(bf16[128,128]{1,0:T(8,128)(2,1)S(1)} %add_convert_fusion.3), channel_id=1, source_target_pairs={{0,96},{32,64},{64,32},{96,0},{128,224},{160,192},{192,160},{224,1... | collective-permute-start | bytes 98312 | tf_op jit(solution)/shard_map/p_sum/ppermute | solution.py:294
  33.3 2.4 %collective-permute-start.3 = (bf16[128,128]{1,0:T(8,128)(2,1)S(1)}, bf16[128,128]{1,0:T(8,128)(2,1)S(1)}, u32[]{:S(2)}, u32[]{:S(2)}) collective-permute-start(bf16[128,128]{1,0:T(8,128)(2,1)S(1)} %add_convert_fusion.3), channel_id=1, source_target_pairs={{0,64},{32,96},{64,0},{96,32},{128,192},{160,224},{192,128},{224,1... | collective-permute-start | bytes 98312 | tf_op jit(solution)/shard_map/p_sum/ppermute | solution.py:294
  35.7 0.1 collective-permute-start.2
  35.8 1.3 %p_sum.4 = bf16[1,2,4096,128]{3,2,1,0:T(8,128)(2,1)} custom-call(s32[1]{0:T(128)} %bitcast.half_ref, bf16[2,2048,128]{2,1,0:T(8,128)(2,1)S(1)} %get-tuple-element.31.own_ref, bf16[2,2048,128]{2,1,0:T(8,128)(2,1)S(1)} %get-tuple-element.32.other_ref), custom_call_target="tpu_custom_call" | custom-call | bytes 4194304 | tf_op jit(solution)/shard_map/p_sum/pallas_call | solution.py:194
  37.1 1.0 %collective-permute-done.3 = bf16[128,128]{1,0:T(8,128)(2,1)S(1)} collective-permute-done((bf16[128,128]{1,0:T(8,128)(2,1)S(1)}, bf16[128,128]{1,0:T(8,128)(2,1)S(1)}, u32[]{:S(2)}, u32[]{:S(2)}) %collective-permute-start.3) | collective-permute-done | bytes 32800 | tf_op jit(solution)/shard_map/p_sum/ppermute | solution.py:294
  38.1 1.5 %collective-permute-done.2 = bf16[128,128]{1,0:T(8,128)(2,1)S(1)} collective-permute-done((bf16[128,128]{1,0:T(8,128)(2,1)S(1)}, bf16[128,128]{1,0:T(8,128)(2,1)S(1)}, u32[]{:S(2)}, u32[]{:S(2)}) %collective-permute-start.2) | collective-permute-done | bytes 32800 | tf_op jit(solution)/shard_map/p_sum/ppermute | solution.py:294
  39.6 13.4 %all_to_all.11 = bf16[16,128,128]{2,1,0:T(8,128)(2,1)S(1)} all-to-all(bf16[16,128,128]{2,1,0:T(8,128)(2,1)S(1)} %p_sum.5), channel_id=1, replica_groups=mesh['z'=8,'x'=4,'y'=4,'c'=2] {'x','y'}, dimensions={0} | all-to-all | bytes 1048576 | tf_op jit(solution)/shard_map/p_sum/all_to_all | solution.py:302
  53.0 0.5 u_sum.4
  53.5 1.4 %collective-permute-done.5.p_ref.pt_ref = bf16[2048,128]{1,0:T(8,128)(2,1)S(1)} collective-permute-done((bf16[2048,128]{1,0:T(8,128)(2,1)S(1)}, bf16[2048,128]{1,0:T(8,128)(2,1)S(1)}, u32[]{:S(2)}, u32[]{:S(2)}) %collective-permute-start.5) | collective-permute-done | bytes 524320 | tf_op jit(solution)/shard_map/p_sum/ppermute | solution.py:290
  54.9 0.5 u_sum.5
  55.4 3.7 %collective-permute-start.6 = (bf16[128,128]{1,0:T(8,128)(2,1)S(1)}, bf16[128,128]{1,0:T(8,128)(2,1)S(1)}, u32[]{:S(2)}, u32[]{:S(2)}) collective-permute-start(bf16[128,128]{1,0:T(8,128)(2,1)S(1)} %get-tuple-element.41), channel_id=1, source_target_pairs={{0,192},{32,224},{64,128},{96,160},{128,64},{160,96},{192,0},{224,... | collective-permute-start | bytes 98312 | tf_op jit(solution)/shard_map/u_sum/ppermute | solution.py:294
  59.1 2.1 %u_sum.6.l_ref = f32[128,128]{1,0:T(8,128)S(1)} custom-call(f32[128,128]{1,0:T(8,128)S(1)} %get-tuple-element.42.g_ref), custom_call_target="tpu_custom_call" | custom-call | flops 262144 | bytes 6291456 | tf_op jit(solution)/shard_map/u_sum/pallas_call | solution.py:173
  61.2 0.9 %collective-permute-done.6 = bf16[128,128]{1,0:T(8,128)(2,1)S(1)} collective-permute-done((bf16[128,128]{1,0:T(8,128)(2,1)S(1)}, bf16[128,128]{1,0:T(8,128)(2,1)S(1)}, u32[]{:S(2)}, u32[]{:S(2)}) %collective-permute-start.6) | collective-permute-done | bytes 32800 | tf_op jit(solution)/shard_map/u_sum/ppermute | solution.py:294
  62.2 1.3 %collective-permute-start.9 = (bf16[128,128]{1,0:T(8,128)(2,1)S(1)}, bf16[128,128]{1,0:T(8,128)(2,1)S(1)}, u32[]{:S(2)}, u32[]{:S(2)}) collective-permute-start(bf16[128,128]{1,0:T(8,128)(2,1)S(1)} %add_convert_fusion.2), channel_id=1, source_target_pairs={{0,96},{32,64},{64,32},{96,0},{128,224},{160,192},{192,160},{224,1... | collective-permute-start | bytes 98312 | tf_op jit(solution)/shard_map/u_sum/ppermute | solution.py:294
  63.5 1.8 %collective-permute-start.8 = (bf16[128,128]{1,0:T(8,128)(2,1)S(1)}, bf16[128,128]{1,0:T(8,128)(2,1)S(1)}, u32[]{:S(2)}, u32[]{:S(2)}) collective-permute-start(bf16[128,128]{1,0:T(8,128)(2,1)S(1)} %add_convert_fusion.2), channel_id=1, source_target_pairs={{0,64},{32,96},{64,0},{96,32},{128,192},{160,224},{192,128},{224,1... | collective-permute-start | bytes 98312 | tf_op jit(solution)/shard_map/u_sum/ppermute | solution.py:294
  65.2 0.5 collective-permute-start.7
  65.7 1.6 %u_sum.7 = (bf16[4096,128]{1,0:T(8,128)(2,1)}, bf16[4096,128]{1,0:T(8,128)(2,1)S(1)}) custom-call(s32[1]{0:T(128)} %bitcast.half_ref, f32[128,128]{1,0:T(8,128)S(1)} %u_sum.6.l_ref, bf16[2048,128]{1,0:T(8,128)(2,1)S(1)} %bitcast.12, bf16[2048,128]{1,0:T(8,128)(2,1)S(1)} %collective-permute-done.5.p_ref.pt_ref), custom_call_target="tpu_custom_call" | custom-call | flops 268435456 | bytes 6291456 | tf_op jit(solution)/shard_map/u_sum/pallas_call | solution.py:226
  67.4 1.0 %collective-permute-done.8 = bf16[128,128]{1,0:T(8,128)(2,1)S(1)} collective-permute-done((bf16[128,128]{1,0:T(8,128)(2,1)S(1)}, bf16[128,128]{1,0:T(8,128)(2,1)S(1)}, u32[]{:S(2)}, u32[]{:S(2)}) %collective-permute-start.8) | collective-permute-done | bytes 32800 | tf_op jit(solution)/shard_map/u_sum/ppermute | solution.py:294
  68.4 0.8 %collective-permute-done.7 = bf16[128,128]{1,0:T(8,128)(2,1)S(1)} collective-permute-done((bf16[128,128]{1,0:T(8,128)(2,1)S(1)}, bf16[128,128]{1,0:T(8,128)(2,1)S(1)}, u32[]{:S(2)}, u32[]{:S(2)}) %collective-permute-start.7) | collective-permute-done | bytes 32800 | tf_op jit(solution)/shard_map/u_sum/ppermute | solution.py:294
  69.2 1.2 %collective-permute-start.12 = (bf16[128,128]{1,0:T(8,128)(2,1)S(1)}, bf16[128,128]{1,0:T(8,128)(2,1)S(1)}, u32[]{:S(2)}, u32[]{:S(2)}) collective-permute-start(bf16[128,128]{1,0:T(8,128)(2,1)S(1)} %add_convert_fusion.1.u_ref), channel_id=1, source_target_pairs={{0,24},{8,16},{16,8},{24,0},{1,25},{9,17},{17,9},{25,1},{2,26},{10... | collective-permute-start | bytes 98312 | tf_op jit(solution)/shard_map/u_sum/ppermute | solution.py:294
  70.4 0.7 collective-permute-start.11
  71.1 2.3 %collective-permute-start.10 = (bf16[128,128]{1,0:T(8,128)(2,1)S(1)}, bf16[128,128]{1,0:T(8,128)(2,1)S(1)}, u32[]{:S(2)}, u32[]{:S(2)}) collective-permute-start(bf16[128,128]{1,0:T(8,128)(2,1)S(1)} %add_convert_fusion.1.u_ref), channel_id=1, source_target_pairs={{0,8},{8,0},{16,24},{24,16},{1,9},{9,1},{17,25},{25,17},{2,10},{10... | collective-permute-start | bytes 98312 | tf_op jit(solution)/shard_map/u_sum/ppermute | solution.py:294
  73.4 1.0 %collective-permute-done.12.d_ref = bf16[128,128]{1,0:T(8,128)(2,1)S(1)} collective-permute-done((bf16[128,128]{1,0:T(8,128)(2,1)S(1)}, bf16[128,128]{1,0:T(8,128)(2,1)S(1)}, u32[]{:S(2)}, u32[]{:S(2)}) %collective-permute-start.12) | collective-permute-done | bytes 32800 | tf_op jit(solution)/shard_map/u_sum/ppermute | solution.py:294
  74.4 1.4 %collective-permute-done.11.b_ref = bf16[128,128]{1,0:T(8,128)(2,1)S(1)} collective-permute-done((bf16[128,128]{1,0:T(8,128)(2,1)S(1)}, bf16[128,128]{1,0:T(8,128)(2,1)S(1)}, u32[]{:S(2)}, u32[]{:S(2)}) %collective-permute-start.11) | collective-permute-done | bytes 32800 | tf_op jit(solution)/shard_map/u_sum/ppermute | solution.py:294
  75.8 2.5 %back.1 = (bf16[1,2,4096,128]{3,2,1,0:T(8,128)(2,1)}, f32[128,128]{1,0:T(8,128)}) custom-call(s32[1]{0:T(128)} %bitcast.half_ref, bf16[4096,128]{1,0:T(8,128)(2,1)S(1)} %get-tuple-element.47.f_ref, bf16[2,2048,128]{2,1,0:T(8,128)(2,1)S(1)} %get-tuple-element.38.c_ref.co_ref, bf16[2,2048,128]{2,1,0:T(8,128)(2,1)S(1)} %get-tuple-element.37.c_ref.ct_ref, ...), custom_call_target="tpu_custom_call" | custom-call | flops 268435456 | bytes 6291456 | tf_op jit(solution)/shard_map/back/pallas_call | solution.py:271
  (11 shorter events, 0.2 us)
Async XLA Ops:
  3.1 2.5 %collective-permute-start = (bf16[2048,128]{1,0:T(8,128)(2,1)S(1)}, bf16[2048,128]{1,0:T(8,128)(2,1)S(1)}, u32[]{:S(2)}, u32[]{:S(2)}) collective-permute-start(bf16[2048,128]{1,0:T(8,128)(2,1)S(1)} %get-tuple-element.30), channel_id=1, source_target_pairs={{0,1},{1,0},{2,3},{3,2},{4,5},{5,4},{6,7},{7,6},{8,9},{9,8},{10,11... | collective-permute-start | bytes 1572872 | tf_op jit(solution)/shard_map/p_partial/ppermute | solution.py:290
  24.8 7.4 %collective-permute-start.1 = (bf16[128,128]{1,0:T(8,128)(2,1)S(1)}, bf16[128,128]{1,0:T(8,128)(2,1)S(1)}, u32[]{:S(2)}, u32[]{:S(2)}) collective-permute-start(bf16[128,128]{1,0:T(8,128)(2,1)S(1)} %bitcast.13), channel_id=1, source_target_pairs={{0,192},{32,224},{64,128},{96,160},{128,64},{160,96},{192,0},{224,... | collective-permute-start | bytes 98312 | tf_op jit(solution)/shard_map/p_sum/ppermute | solution.py:294
  32.2 4.9 %collective-permute-start.4 = (bf16[128,128]{1,0:T(8,128)(2,1)S(1)}, bf16[128,128]{1,0:T(8,128)(2,1)S(1)}, u32[]{:S(2)}, u32[]{:S(2)}) collective-permute-start(bf16[128,128]{1,0:T(8,128)(2,1)S(1)} %add_convert_fusion.3), channel_id=1, source_target_pairs={{0,96},{32,64},{64,32},{96,0},{128,224},{160,192},{192,160},{224,1... | collective-permute-start | bytes 98312 | tf_op jit(solution)/shard_map/p_sum/ppermute | solution.py:294
  33.3 4.8 %collective-permute-start.3 = (bf16[128,128]{1,0:T(8,128)(2,1)S(1)}, bf16[128,128]{1,0:T(8,128)(2,1)S(1)}, u32[]{:S(2)}, u32[]{:S(2)}) collective-permute-start(bf16[128,128]{1,0:T(8,128)(2,1)S(1)} %add_convert_fusion.3), channel_id=1, source_target_pairs={{0,64},{32,96},{64,0},{96,32},{128,192},{160,224},{192,128},{224,1... | collective-permute-start | bytes 98312 | tf_op jit(solution)/shard_map/p_sum/ppermute | solution.py:294
  35.7 3.9 %collective-permute-start.2 = (bf16[128,128]{1,0:T(8,128)(2,1)S(1)}, bf16[128,128]{1,0:T(8,128)(2,1)S(1)}, u32[]{:S(2)}, u32[]{:S(2)}) collective-permute-start(bf16[128,128]{1,0:T(8,128)(2,1)S(1)} %add_convert_fusion.3), channel_id=1, source_target_pairs={{0,32},{32,0},{64,96},{96,64},{128,160},{160,128},{192,224},{224,1... | collective-permute-start | bytes 98312 | tf_op jit(solution)/shard_map/p_sum/ppermute | solution.py:294
  53.0 1.9 %collective-permute-start.5 = (bf16[2048,128]{1,0:T(8,128)(2,1)S(1)}, bf16[2048,128]{1,0:T(8,128)(2,1)S(1)}, u32[]{:S(2)}, u32[]{:S(2)}) collective-permute-start(bf16[2048,128]{1,0:T(8,128)(2,1)S(1)} %bitcast.10), channel_id=1, source_target_pairs={{0,1},{1,0},{2,3},{3,2},{4,5},{5,4},{6,7},{7,6},{8,9},{9,8},{10,11... | collective-permute-start | bytes 1572872 | tf_op jit(solution)/shard_map/p_sum/ppermute | solution.py:290
  55.4 6.7 %collective-permute-start.6 = (bf16[128,128]{1,0:T(8,128)(2,1)S(1)}, bf16[128,128]{1,0:T(8,128)(2,1)S(1)}, u32[]{:S(2)}, u32[]{:S(2)}) collective-permute-start(bf16[128,128]{1,0:T(8,128)(2,1)S(1)} %get-tuple-element.41), channel_id=1, source_target_pairs={{0,192},{32,224},{64,128},{96,160},{128,64},{160,96},{192,0},{224,... | collective-permute-start | bytes 98312 | tf_op jit(solution)/shard_map/u_sum/ppermute | solution.py:294
  62.2 5.2 %collective-permute-start.9 = (bf16[128,128]{1,0:T(8,128)(2,1)S(1)}, bf16[128,128]{1,0:T(8,128)(2,1)S(1)}, u32[]{:S(2)}, u32[]{:S(2)}) collective-permute-start(bf16[128,128]{1,0:T(8,128)(2,1)S(1)} %add_convert_fusion.2), channel_id=1, source_target_pairs={{0,96},{32,64},{64,32},{96,0},{128,224},{160,192},{192,160},{224,1... | collective-permute-start | bytes 98312 | tf_op jit(solution)/shard_map/u_sum/ppermute | solution.py:294
  63.5 4.9 %collective-permute-start.8 = (bf16[128,128]{1,0:T(8,128)(2,1)S(1)}, bf16[128,128]{1,0:T(8,128)(2,1)S(1)}, u32[]{:S(2)}, u32[]{:S(2)}) collective-permute-start(bf16[128,128]{1,0:T(8,128)(2,1)S(1)} %add_convert_fusion.2), channel_id=1, source_target_pairs={{0,64},{32,96},{64,0},{96,32},{128,192},{160,224},{192,128},{224,1... | collective-permute-start | bytes 98312 | tf_op jit(solution)/shard_map/u_sum/ppermute | solution.py:294
  65.2 3.9 %collective-permute-start.7 = (bf16[128,128]{1,0:T(8,128)(2,1)S(1)}, bf16[128,128]{1,0:T(8,128)(2,1)S(1)}, u32[]{:S(2)}, u32[]{:S(2)}) collective-permute-start(bf16[128,128]{1,0:T(8,128)(2,1)S(1)} %add_convert_fusion.2), channel_id=1, source_target_pairs={{0,32},{32,0},{64,96},{96,64},{128,160},{160,128},{192,224},{224,1... | collective-permute-start | bytes 98312 | tf_op jit(solution)/shard_map/u_sum/ppermute | solution.py:294
  69.2 5.2 %collective-permute-start.12 = (bf16[128,128]{1,0:T(8,128)(2,1)S(1)}, bf16[128,128]{1,0:T(8,128)(2,1)S(1)}, u32[]{:S(2)}, u32[]{:S(2)}) collective-permute-start(bf16[128,128]{1,0:T(8,128)(2,1)S(1)} %add_convert_fusion.1.u_ref), channel_id=1, source_target_pairs={{0,24},{8,16},{16,8},{24,0},{1,25},{9,17},{17,9},{25,1},{2,26},{10... | collective-permute-start | bytes 98312 | tf_op jit(solution)/shard_map/u_sum/ppermute | solution.py:294
  70.4 5.4 %collective-permute-start.11 = (bf16[128,128]{1,0:T(8,128)(2,1)S(1)}, bf16[128,128]{1,0:T(8,128)(2,1)S(1)}, u32[]{:S(2)}, u32[]{:S(2)}) collective-permute-start(bf16[128,128]{1,0:T(8,128)(2,1)S(1)} %add_convert_fusion.1.u_ref), channel_id=1, source_target_pairs={{0,16},{8,24},{16,0},{24,8},{1,17},{9,25},{17,1},{25,9},{2,18},{10... | collective-permute-start | bytes 98312 | tf_op jit(solution)/shard_map/u_sum/ppermute | solution.py:294
  71.1 4.7 %collective-permute-start.10 = (bf16[128,128]{1,0:T(8,128)(2,1)S(1)}, bf16[128,128]{1,0:T(8,128)(2,1)S(1)}, u32[]{:S(2)}, u32[]{:S(2)}) collective-permute-start(bf16[128,128]{1,0:T(8,128)(2,1)S(1)} %add_convert_fusion.1.u_ref), channel_id=1, source_target_pairs={{0,8},{8,0},{16,24},{24,16},{1,9},{9,1},{17,25},{25,17},{2,10},{10... | collective-permute-start | bytes 98312 | tf_op jit(solution)/shard_map/u_sum/ppermute | solution.py:294

commit v8 on v7

--- a/solution.py
+++ b/solution.py
@@ -24,54 +24,70 @@
     return lax.broadcasted_iota(jnp.int32, shape, len(shape) - 1) < RANK2 // 2
 
 
-def front_body(half_ref, g_hbm, m_hbm, e_hbm, q_hbm, mo_ref, c_ref, p_ref, g_buf, m_buf, e_buf, q_buf, sem, q_sem):
+def front_body(half_ref, g_hbm, m_hbm, e_hbm, q_hbm, *rest):
+    first = len(rest) == 13
+    ahead, rest = (rest[3:6], rest[:3] + rest[6:]) if first else (rest[:3], rest[3:])
+    mo_ref, c_ref, p_ref, g_buf, m_buf, e_buf, q_buf, sem, q_sem, *more = rest
     base = pl.multiple_of(half_ref[0] * HALF, HALF)
+    hbm, buf = (m_hbm, g_hbm, e_hbm), (m_buf, g_buf, e_buf)
 
     def loads(k):
-        here = pl.ds(pl.multiple_of(k * FRONT, FRONT), FRONT)
+        here = pl.ds(k * FRONT, FRONT)
         there = pl.ds(pl.multiple_of(base + k * FRONT, FRONT), FRONT)
-        return [
-            pltpu.make_async_copy(hbm.at[0, :, there], buf.at[:, here], sem.at[i, k])
-            for i, (hbm, buf) in enumerate(((m_hbm, m_buf), (g_hbm, g_buf), (e_hbm, e_buf)))
-        ]
+        return [pltpu.make_async_copy(hbm[i].at[0, :, there], buf[i].at[:, here], sem.at[i, k]) for i in range(3)]
 
     load_q = pltpu.make_async_copy(q_hbm, q_buf, q_sem)
     load_q.start()
-    for k in range(HALF // FRONT):
+    chunks = range(HALF // FRONT)
+    mine = chunks if first else chunks[1:]
+    for k in mine:
         for copy in loads(k):
             copy.start()
+    extra = []
+    if first:
+        there = pl.ds(pl.multiple_of(HALF - base, HALF), FRONT)
+        extra = [pltpu.make_async_copy(hbm[i].at[0, :, there], ahead[i], more[0].at[i]) for i in range(3)]
+    for copy in extra:
+        copy.start()
     load_q.wait()
     q = q_buf[...]
     left = left_lanes(q.shape)
     q_of = [jnp.where(left if group == 0 else ~left, q, jnp.zeros_like(q)) for group in range(2)]
-
-    for k in range(HALF // FRONT):
-        for copy in loads(k):
-            copy.wait()
-        rows = pl.ds(pl.multiple_of(k * FRONT, FRONT), FRONT)
+    for k in chunks:
+        rows = pl.ds(k * FRONT, FRONT)
+        if k in mine:
+            for copy in loads(k):
+                copy.wait()
         total = None
         for group in range(2):
-            mo = (0.9 * m_buf[group, rows].astype(F32) + g_buf[group, rows].astype(F32)).astype(BF)
-            co = (mo.astype(F32) + e_buf[group, rows].astype(F32)).astype(BF)
+            m, g, e = (x[group, rows].astype(F32) for x in (buf if k in mine else ahead))
+            mo = (0.9 * m + g).astype(BF)
+            co = (mo.astype(F32) + e).astype(BF)
             mo_ref[group, rows] = mo
             c_ref[group, rows] = co
             term = dot(co, q_of[group])
             total = term if total is None else total + term
         p_ref[rows] = total.astype(p_ref.dtype)
-
-
-def front(half, args, p_dtype):
+    for copy in extra:
+        copy.wait()
+
+
+def front(half, args, ahead):
     hbm, vmem = pl.BlockSpec(memory_space=pltpu.HBM), pl.BlockSpec(memory_space=pltpu.VMEM)
+    first = ahead is None
+    part = pltpu.VMEM((2, HALF, COLS), BF)
     return pl.pallas_call(
         front_body,
-        in_specs=[pl.BlockSpec(memory_space=pltpu.SMEM)] + [hbm] * 4,
-        out_specs=[vmem] * 3,
-        out_shape=[pltpu.VMEM((2, HALF, COLS), BF), pltpu.VMEM((2, HALF, COLS), BF), pltpu.VMEM((HALF, RANK2), p_dtype)],
+        in_specs=[pl.BlockSpec(memory_space=pltpu.SMEM)] + [hbm] * 4 + [vmem] * (0 if first else 3),
+        out_specs=[vmem] * (6 if first else 3),
+        out_shape=[part, part, pltpu.VMEM((HALF, RANK2), BF if first else F32)]
+        + [pltpu.VMEM((2, FRONT, COLS), BF)] * (3 if first else 0),
         scratch_shapes=[pltpu.VMEM((2, HALF, COLS), BF)] * 3
-        + [pltpu.VMEM((COLS, RANK2), BF), pltpu.SemaphoreType.DMA((3, HALF // FRONT)), pltpu.SemaphoreType.DMA],
+        + [pltpu.VMEM((COLS, RANK2), BF), pltpu.SemaphoreType.DMA((3, HALF // FRONT)), pltpu.SemaphoreType.DMA]
+        + [pltpu.SemaphoreType.DMA((3,))] * first,
         compiler_params=pltpu.CompilerParams(vmem_limit_bytes=16 * MIB),
         cost_estimate=pl.CostEstimate(flops=2 * HALF * 256 * 128, bytes_accessed=4 * MIB, transcendentals=0),
-    )(half, *(pltpu.with_memory_space_constraint(x, pltpu.HBM) for x in args))
+    )(half, *(pltpu.with_memory_space_constraint(x, pltpu.HBM) for x in args), *(ahead or ()))
 
 
 def sum_copies_body(x_ref, o_ref):
@@ -308,18 +324,18 @@
 
     with jax.named_scope("p_partial"):
         args = (grads, momentum, error, q_warm)
-        mo_other, c_other, p_send = front(theirs, args, BF)
+        mo_other, c_other, p_send, *ahead = front(theirs, args, None)
         p_got = swap_cores(p_send)
-        mo_own, c_own, p_own = front(mine, args, F32)
+        mo_own, c_own, p_own = front(mine, args, ahead)
         chip = (p_own + p_got.astype(F32)).astype(BF)
     with jax.named_scope("p_sum"):
-        parts = exchange(chip.reshape(NX * NY, BLK, RANK2), ("x", "y"))
+        parts = exchange(chip.reshape(NX * NY, BLK, RANK2), ("y", "x"))
         part = sum_copies(parts, 1)[0]
         part = plus(part, pair(part, "z", NZ, 6))
         got = [pair(part, "z", NZ, k) for k in (1, 2, 3)]
         got, momentum_out = lax.optimization_barrier((got, store(mine, mo_own, mo_other)))
         parts = jnp.stack([part] + got)
-        p_mine = exchange(sum_copies(parts, NX * NY), ("x", "y")).reshape(HALF, RANK2)
+        p_mine = exchange(sum_copies(parts, NX * NY), ("y", "x")).reshape(HALF, RANK2)
         p_theirs = swap_cores(p_mine)
     with jax.named_scope("u_sum"):
         first = products(p_mine, c_own, None)

time: 79.1 us -> 78.7 us (level)
  transfers between devices with their start and end apart: 13 -> 13, of which waited for: 9 -> 10; matrix products, arithmetic and copies ran while one was open for 0% -> 0% of each run, Pallas kernels for 10% -> 10%
where the time goes in v8:
time: 78.7 us; the launch traced here: 77.8 us
  blocking collectives  32 us (41%)
  starting transfers between devices  20.6 us (26%)
  Pallas kernels  13.3 us (17%)
  waiting for transfers between devices  11 us (14%)
    all_to_all x2, blocking collectives, exchange(): return lax.all_to_all(x, axes, 0, 0)  32 us
    ppermute x11, starting transfers between devices, pair(): return lax.ppermute(x, axis, [(i, i ^ flip) for i in range(size)])  20.5 us
    ppermute x11, waiting for transfers between devices, pair(): return lax.ppermute(x, axis, [(i, i ^ flip) for i in range(size)])  9.55 us
    pallas_call x2, Pallas kernels, front(): pl.pallas_call(front_body, in_specs=[pl.BlockSpec(memory_space=pltpu.SMEM...  4.74 us
    pallas_call x1, Pallas kernels, back(): pl.pallas_call(back_body, in_specs=[pl.BlockSpec(memory_space=pltpu.SMEM)...  2.45 us
    pallas_call x1, Pallas kernels, inverse(): pl.pallas_call(invert, out_shape=jax.ShapeDtypeStruct((RANK2, RANK2), F32...  2.1 us
    pallas_call x1, Pallas kernels, factor(): pl.pallas_call(factor_body, in_specs=[pl.BlockSpec(memory_space=pltpu.SME...  1.61 us
  transfers between devices with their start and end apart: 13, of which 10 were waited for; matrix products, arithmetic and copies ran while one was open for 0% of the time, Pallas kernels for 10%

profile of v8, /device:TPU:32, one launch (start us, length us, event | category | flops | bytes accessed | tf_op | source)
XLA Modules:
  0.0 77.8 jit_solution(5524429246952270494)
XLA Ops:
  0.6 2.8 %p_partial.2 = (bf16[2,2048,128]{2,1,0:T(8,128)(2,1)S(1)}, bf16[2,2048,128]{2,1,0:T(8,128)(2,1)S(1)}, bf16[2048,128]{1,0:T(8,128)(2,1)S(1)}, bf16[2,1024,128]{2,...) custom-call(s32[1]{0:T(128)} %bitcast.1.half_ref, ...), custom_call_target="tpu_custom_call" | custom-call | flops 134217728 | bytes 4194304 | tf_op jit(solution)/shard_map/p_partial/pallas_call | solution.py:79
  3.5 2.0 %p_partial.3 = (bf16[2,2048,128]{2,1,0:T(8,128)(2,1)S(1)}, bf16[2,2048,128]{2,1,0:T(8,128)(2,1)S(1)}, f32[2048,128]{1,0:T(8,128)S(1)}) custom-call(s32[1]{0:T(128)} %bitcast.half_ref, bf16[1,2,4096,128]{3,2,1,0:T(8,128)(2,1)} %g_hbm.3, bf16[1,2,4096,128]{3,2,1,0:T(8,128)(2,1)} %m_hbm.3, bf16[1,2,4096,128]{3,2,1,0:T(8,128)(2,1)} %e_hbm.3, ...), custom_call_target="tpu_custom_call" | custom-call | flops 134217728 | bytes 4194304 | tf_op jit(solution)/shard_map/p_partial/pallas_call | solution.py:79
  5.5 0.1 add_convert_fusion
  5.6 19.0 %all_to_all.10.x_ref = bf16[16,128,128]{2,1,0:T(8,128)(2,1)S(1)} all-to-all(bf16[16,128,128]{2,1,0:T(8,128)(2,1)S(1)} %bitcast.14), channel_id=1, replica_groups=mesh['z'=8,'x'=4,'y'=4,'c'=2] {'y','x'}, dimensions={0} | all-to-all | bytes 1048576 | tf_op jit(solution)/shard_map/p_sum/all_to_all | solution.py:318
  24.7 5.5 %collective-permute-start.1 = (bf16[128,128]{1,0:T(8,128)(2,1)S(1)}, bf16[128,128]{1,0:T(8,128)(2,1)S(1)}, u32[]{:S(2)}, u32[]{:S(2)}) collective-permute-start(bf16[128,128]{1,0:T(8,128)(2,1)S(1)} %bitcast.13), channel_id=1, source_target_pairs={{0,192},{32,224},{64,128},{96,160},{128,64},{160,96},{192,0},{224,... | collective-permute-start | bytes 98312 | tf_op jit(solution)/shard_map/p_sum/ppermute | solution.py:310
  30.2 1.9 %collective-permute-done.1 = bf16[128,128]{1,0:T(8,128)(2,1)S(1)} collective-permute-done((bf16[128,128]{1,0:T(8,128)(2,1)S(1)}, bf16[128,128]{1,0:T(8,128)(2,1)S(1)}, u32[]{:S(2)}, u32[]{:S(2)}) %collective-permute-start.1) | collective-permute-done | bytes 32800 | tf_op jit(solution)/shard_map/p_sum/ppermute | solution.py:310
  32.1 1.1 %collective-permute-start.4 = (bf16[128,128]{1,0:T(8,128)(2,1)S(1)}, bf16[128,128]{1,0:T(8,128)(2,1)S(1)}, u32[]{:S(2)}, u32[]{:S(2)}) collective-permute-start(bf16[128,128]{1,0:T(8,128)(2,1)S(1)} %add_convert_fusion.3), channel_id=1, source_target_pairs={{0,96},{32,64},{64,32},{96,0},{128,224},{160,192},{192,160},{224,1... | collective-permute-start | bytes 98312 | tf_op jit(solution)/shard_map/p_sum/ppermute | solution.py:310
  33.2 2.4 %collective-permute-start.3 = (bf16[128,128]{1,0:T(8,128)(2,1)S(1)}, bf16[128,128]{1,0:T(8,128)(2,1)S(1)}, u32[]{:S(2)}, u32[]{:S(2)}) collective-permute-start(bf16[128,128]{1,0:T(8,128)(2,1)S(1)} %add_convert_fusion.3), channel_id=1, source_target_pairs={{0,64},{32,96},{64,0},{96,32},{128,192},{160,224},{192,128},{224,1... | collective-permute-start | bytes 98312 | tf_op jit(solution)/shard_map/p_sum/ppermute | solution.py:310
  35.6 0.1 collective-permute-start.2
  35.7 1.3 %p_sum.4 = bf16[1,2,4096,128]{3,2,1,0:T(8,128)(2,1)} custom-call(s32[1]{0:T(128)} %bitcast.half_ref, bf16[2,2048,128]{2,1,0:T(8,128)(2,1)S(1)} %get-tuple-element.37.own_ref, bf16[2,2048,128]{2,1,0:T(8,128)(2,1)S(1)} %get-tuple-element.38.other_ref), custom_call_target="tpu_custom_call" | custom-call | bytes 4194304 | tf_op jit(solution)/shard_map/p_sum/pallas_call | solution.py:210
  37.0 1.0 %collective-permute-done.3 = bf16[128,128]{1,0:T(8,128)(2,1)S(1)} collective-permute-done((bf16[128,128]{1,0:T(8,128)(2,1)S(1)}, bf16[128,128]{1,0:T(8,128)(2,1)S(1)}, u32[]{:S(2)}, u32[]{:S(2)}) %collective-permute-start.3) | collective-permute-done | bytes 32800 | tf_op jit(solution)/shard_map/p_sum/ppermute | solution.py:310
  38.0 1.5 %collective-permute-done.2 = bf16[128,128]{1,0:T(8,128)(2,1)S(1)} collective-permute-done((bf16[128,128]{1,0:T(8,128)(2,1)S(1)}, bf16[128,128]{1,0:T(8,128)(2,1)S(1)}, u32[]{:S(2)}, u32[]{:S(2)}) %collective-permute-start.2) | collective-permute-done | bytes 32800 | tf_op jit(solution)/shard_map/p_sum/ppermute | solution.py:310
  39.6 13.0 %all_to_all.11 = bf16[16,128,128]{2,1,0:T(8,128)(2,1)S(1)} all-to-all(bf16[16,128,128]{2,1,0:T(8,128)(2,1)S(1)} %p_sum.5), channel_id=1, replica_groups=mesh['z'=8,'x'=4,'y'=4,'c'=2] {'y','x'}, dimensions={0} | all-to-all | bytes 1048576 | tf_op jit(solution)/shard_map/p_sum/all_to_all | solution.py:318
  52.6 0.5 u_sum.4
  53.1 1.4 %collective-permute-done.5.p_ref.pt_ref = bf16[2048,128]{1,0:T(8,128)(2,1)S(1)} collective-permute-done((bf16[2048,128]{1,0:T(8,128)(2,1)S(1)}, bf16[2048,128]{1,0:T(8,128)(2,1)S(1)}, u32[]{:S(2)}, u32[]{:S(2)}) %collective-permute-start.5) | collective-permute-done | bytes 524320 | tf_op jit(solution)/shard_map/p_sum/ppermute | solution.py:306
  54.5 0.5 u_sum.5
  55.0 3.7 %collective-permute-start.6 = (bf16[128,128]{1,0:T(8,128)(2,1)S(1)}, bf16[128,128]{1,0:T(8,128)(2,1)S(1)}, u32[]{:S(2)}, u32[]{:S(2)}) collective-permute-start(bf16[128,128]{1,0:T(8,128)(2,1)S(1)} %get-tuple-element.47), channel_id=1, source_target_pairs={{0,192},{32,224},{64,128},{96,160},{128,64},{160,96},{192,0},{224,... | collective-permute-start | bytes 98312 | tf_op jit(solution)/shard_map/u_sum/ppermute | solution.py:310
  58.7 2.1 %u_sum.6.l_ref = f32[128,128]{1,0:T(8,128)S(1)} custom-call(f32[128,128]{1,0:T(8,128)S(1)} %get-tuple-element.48.g_ref), custom_call_target="tpu_custom_call" | custom-call | flops 262144 | bytes 6291456 | tf_op jit(solution)/shard_map/u_sum/pallas_call | solution.py:189
  60.8 0.9 %collective-permute-done.6 = bf16[128,128]{1,0:T(8,128)(2,1)S(1)} collective-permute-done((bf16[128,128]{1,0:T(8,128)(2,1)S(1)}, bf16[128,128]{1,0:T(8,128)(2,1)S(1)}, u32[]{:S(2)}, u32[]{:S(2)}) %collective-permute-start.6) | collective-permute-done | bytes 32800 | tf_op jit(solution)/shard_map/u_sum/ppermute | solution.py:310
  61.7 1.3 %collective-permute-start.9 = (bf16[128,128]{1,0:T(8,128)(2,1)S(1)}, bf16[128,128]{1,0:T(8,128)(2,1)S(1)}, u32[]{:S(2)}, u32[]{:S(2)}) collective-permute-start(bf16[128,128]{1,0:T(8,128)(2,1)S(1)} %add_convert_fusion.2), channel_id=1, source_target_pairs={{0,96},{32,64},{64,32},{96,0},{128,224},{160,192},{192,160},{224,1... | collective-permute-start | bytes 98312 | tf_op jit(solution)/shard_map/u_sum/ppermute | solution.py:310
  63.0 1.8 %collective-permute-start.8 = (bf16[128,128]{1,0:T(8,128)(2,1)S(1)}, bf16[128,128]{1,0:T(8,128)(2,1)S(1)}, u32[]{:S(2)}, u32[]{:S(2)}) collective-permute-start(bf16[128,128]{1,0:T(8,128)(2,1)S(1)} %add_convert_fusion.2), channel_id=1, source_target_pairs={{0,64},{32,96},{64,0},{96,32},{128,192},{160,224},{192,128},{224,1... | collective-permute-start | bytes 98312 | tf_op jit(solution)/shard_map/u_sum/ppermute | solution.py:310
  64.8 0.5 collective-permute-start.7
  65.3 1.6 %u_sum.7 = (bf16[4096,128]{1,0:T(8,128)(2,1)}, bf16[4096,128]{1,0:T(8,128)(2,1)S(1)}) custom-call(s32[1]{0:T(128)} %bitcast.half_ref, f32[128,128]{1,0:T(8,128)S(1)} %u_sum.6.l_ref, bf16[2048,128]{1,0:T(8,128)(2,1)S(1)} %bitcast.12, bf16[2048,128]{1,0:T(8,128)(2,1)S(1)} %collective-permute-done.5.p_ref.pt_ref), custom_call_target="tpu_custom_call" | custom-call | flops 268435456 | bytes 6291456 | tf_op jit(solution)/shard_map/u_sum/pallas_call | solution.py:242
  66.9 1.0 %collective-permute-done.8 = bf16[128,128]{1,0:T(8,128)(2,1)S(1)} collective-permute-done((bf16[128,128]{1,0:T(8,128)(2,1)S(1)}, bf16[128,128]{1,0:T(8,128)(2,1)S(1)}, u32[]{:S(2)}, u32[]{:S(2)}) %collective-permute-start.8) | collective-permute-done | bytes 32800 | tf_op jit(solution)/shard_map/u_sum/ppermute | solution.py:310
  67.9 0.8 %collective-permute-done.7 = bf16[128,128]{1,0:T(8,128)(2,1)S(1)} collective-permute-done((bf16[128,128]{1,0:T(8,128)(2,1)S(1)}, bf16[128,128]{1,0:T(8,128)(2,1)S(1)}, u32[]{:S(2)}, u32[]{:S(2)}) %collective-permute-start.7) | collective-permute-done | bytes 32800 | tf_op jit(solution)/shard_map/u_sum/ppermute | solution.py:310
  68.7 0.6 collective-permute-start.12
  69.3 2.1 %collective-permute-start.11 = (bf16[128,128]{1,0:T(8,128)(2,1)S(1)}, bf16[128,128]{1,0:T(8,128)(2,1)S(1)}, u32[]{:S(2)}, u32[]{:S(2)}) collective-permute-start(bf16[128,128]{1,0:T(8,128)(2,1)S(1)} %add_convert_fusion.1.u_ref), channel_id=1, source_target_pairs={{0,16},{8,24},{16,0},{24,8},{1,17},{9,25},{17,1},{25,9},{2,18},{10... | collective-permute-start | bytes 98312 | tf_op jit(solution)/shard_map/u_sum/ppermute | solution.py:310
  71.5 1.5 %collective-permute-start.10 = (bf16[128,128]{1,0:T(8,128)(2,1)S(1)}, bf16[128,128]{1,0:T(8,128)(2,1)S(1)}, u32[]{:S(2)}, u32[]{:S(2)}) collective-permute-start(bf16[128,128]{1,0:T(8,128)(2,1)S(1)} %add_convert_fusion.1.u_ref), channel_id=1, source_target_pairs={{0,8},{8,0},{16,24},{24,16},{1,9},{9,1},{17,25},{25,17},{2,10},{10... | collective-permute-start | bytes 98312 | tf_op jit(solution)/shard_map/u_sum/ppermute | solution.py:310
  72.9 1.0 %collective-permute-done.12.d_ref = bf16[128,128]{1,0:T(8,128)(2,1)S(1)} collective-permute-done((bf16[128,128]{1,0:T(8,128)(2,1)S(1)}, bf16[128,128]{1,0:T(8,128)(2,1)S(1)}, u32[]{:S(2)}, u32[]{:S(2)}) %collective-permute-start.12) | collective-permute-done | bytes 32800 | tf_op jit(solution)/shard_map/u_sum/ppermute | solution.py:310
  73.9 0.8 %collective-permute-done.11.b_ref = bf16[128,128]{1,0:T(8,128)(2,1)S(1)} collective-permute-done((bf16[128,128]{1,0:T(8,128)(2,1)S(1)}, bf16[128,128]{1,0:T(8,128)(2,1)S(1)}, u32[]{:S(2)}, u32[]{:S(2)}) %collective-permute-start.11) | collective-permute-done | bytes 32800 | tf_op jit(solution)/shard_map/u_sum/ppermute | solution.py:310
  74.8 0.6 collective-permute-done.10.a_ref
  75.4 2.4 %back.1 = (bf16[1,2,4096,128]{3,2,1,0:T(8,128)(2,1)}, f32[128,128]{1,0:T(8,128)}) custom-call(s32[1]{0:T(128)} %bitcast.half_ref, bf16[4096,128]{1,0:T(8,128)(2,1)S(1)} %get-tuple-element.53.f_ref, bf16[2,2048,128]{2,1,0:T(8,128)(2,1)S(1)} %get-tuple-element.44.c_ref.co_ref, bf16[2,2048,128]{2,1,0:T(8,128)(2,1)S(1)} %get-tuple-element.43.c_ref.ct_ref, ...), custom_call_target="tpu_custom_call" | custom-call | flops 268435456 | bytes 6291456 | tf_op jit(solution)/shard_map/back/pallas_call | solution.py:287
  (11 shorter events, 0.3 us)
Async XLA Ops:
  3.4 2.1 %collective-permute-start = (bf16[2048,128]{1,0:T(8,128)(2,1)S(1)}, bf16[2048,128]{1,0:T(8,128)(2,1)S(1)}, u32[]{:S(2)}, u32[]{:S(2)}) collective-permute-start(bf16[2048,128]{1,0:T(8,128)(2,1)S(1)} %get-tuple-element.36), channel_id=1, source_target_pairs={{0,1},{1,0},{2,3},{3,2},{4,5},{5,4},{6,7},{7,6},{8,9},{9,8},{10,11... | collective-permute-start | bytes 1572872 | tf_op jit(solution)/shard_map/p_partial/ppermute | solution.py:306
  24.7 7.4 %collective-permute-start.1 = (bf16[128,128]{1,0:T(8,128)(2,1)S(1)}, bf16[128,128]{1,0:T(8,128)(2,1)S(1)}, u32[]{:S(2)}, u32[]{:S(2)}) collective-permute-start(bf16[128,128]{1,0:T(8,128)(2,1)S(1)} %bitcast.13), channel_id=1, source_target_pairs={{0,192},{32,224},{64,128},{96,160},{128,64},{160,96},{192,0},{224,... | collective-permute-start | bytes 98312 | tf_op jit(solution)/shard_map/p_sum/ppermute | solution.py:310
  32.1 4.9 %collective-permute-start.4 = (bf16[128,128]{1,0:T(8,128)(2,1)S(1)}, bf16[128,128]{1,0:T(8,128)(2,1)S(1)}, u32[]{:S(2)}, u32[]{:S(2)}) collective-permute-start(bf16[128,128]{1,0:T(8,128)(2,1)S(1)} %add_convert_fusion.3), channel_id=1, source_target_pairs={{0,96},{32,64},{64,32},{96,0},{128,224},{160,192},{192,160},{224,1... | collective-permute-start | bytes 98312 | tf_op jit(solution)/shard_map/p_sum/ppermute | solution.py:310
  33.2 4.8 %collective-permute-start.3 = (bf16[128,128]{1,0:T(8,128)(2,1)S(1)}, bf16[128,128]{1,0:T(8,128)(2,1)S(1)}, u32[]{:S(2)}, u32[]{:S(2)}) collective-permute-start(bf16[128,128]{1,0:T(8,128)(2,1)S(1)} %add_convert_fusion.3), channel_id=1, source_target_pairs={{0,64},{32,96},{64,0},{96,32},{128,192},{160,224},{192,128},{224,1... | collective-permute-start | bytes 98312 | tf_op jit(solution)/shard_map/p_sum/ppermute | solution.py:310
  35.6 3.9 %collective-permute-start.2 = (bf16[128,128]{1,0:T(8,128)(2,1)S(1)}, bf16[128,128]{1,0:T(8,128)(2,1)S(1)}, u32[]{:S(2)}, u32[]{:S(2)}) collective-permute-start(bf16[128,128]{1,0:T(8,128)(2,1)S(1)} %add_convert_fusion.3), channel_id=1, source_target_pairs={{0,32},{32,0},{64,96},{96,64},{128,160},{160,128},{192,224},{224,1... | collective-permute-start | bytes 98312 | tf_op jit(solution)/shard_map/p_sum/ppermute | solution.py:310
  52.6 1.9 %collective-permute-start.5 = (bf16[2048,128]{1,0:T(8,128)(2,1)S(1)}, bf16[2048,128]{1,0:T(8,128)(2,1)S(1)}, u32[]{:S(2)}, u32[]{:S(2)}) collective-permute-start(bf16[2048,128]{1,0:T(8,128)(2,1)S(1)} %bitcast.10), channel_id=1, source_target_pairs={{0,1},{1,0},{2,3},{3,2},{4,5},{5,4},{6,7},{7,6},{8,9},{9,8},{10,11... | collective-permute-start | bytes 1572872 | tf_op jit(solution)/shard_map/p_sum/ppermute | solution.py:306
  55.0 6.7 %collective-permute-start.6 = (bf16[128,128]{1,0:T(8,128)(2,1)S(1)}, bf16[128,128]{1,0:T(8,128)(2,1)S(1)}, u32[]{:S(2)}, u32[]{:S(2)}) collective-permute-start(bf16[128,128]{1,0:T(8,128)(2,1)S(1)} %get-tuple-element.47), channel_id=1, source_target_pairs={{0,192},{32,224},{64,128},{96,160},{128,64},{160,96},{192,0},{224,... | collective-permute-start | bytes 98312 | tf_op jit(solution)/shard_map/u_sum/ppermute | solution.py:310
  61.7 5.2 %collective-permute-start.9 = (bf16[128,128]{1,0:T(8,128)(2,1)S(1)}, bf16[128,128]{1,0:T(8,128)(2,1)S(1)}, u32[]{:S(2)}, u32[]{:S(2)}) collective-permute-start(bf16[128,128]{1,0:T(8,128)(2,1)S(1)} %add_convert_fusion.2), channel_id=1, source_target_pairs={{0,96},{32,64},{64,32},{96,0},{128,224},{160,192},{192,160},{224,1... | collective-permute-start | bytes 98312 | tf_op jit(solution)/shard_map/u_sum/ppermute | solution.py:310
  63.0 4.9 %collective-permute-start.8 = (bf16[128,128]{1,0:T(8,128)(2,1)S(1)}, bf16[128,128]{1,0:T(8,128)(2,1)S(1)}, u32[]{:S(2)}, u32[]{:S(2)}) collective-permute-start(bf16[128,128]{1,0:T(8,128)(2,1)S(1)} %add_convert_fusion.2), channel_id=1, source_target_pairs={{0,64},{32,96},{64,0},{96,32},{128,192},{160,224},{192,128},{224,1... | collective-permute-start | bytes 98312 | tf_op jit(solution)/shard_map/u_sum/ppermute | solution.py:310
  64.8 3.9 %collective-permute-start.7 = (bf16[128,128]{1,0:T(8,128)(2,1)S(1)}, bf16[128,128]{1,0:T(8,128)(2,1)S(1)}, u32[]{:S(2)}, u32[]{:S(2)}) collective-permute-start(bf16[128,128]{1,0:T(8,128)(2,1)S(1)} %add_convert_fusion.2), channel_id=1, source_target_pairs={{0,32},{32,0},{64,96},{96,64},{128,160},{160,128},{192,224},{224,1... | collective-permute-start | bytes 98312 | tf_op jit(solution)/shard_map/u_sum/ppermute | solution.py:310
  68.7 5.2 %collective-permute-start.12 = (bf16[128,128]{1,0:T(8,128)(2,1)S(1)}, bf16[128,128]{1,0:T(8,128)(2,1)S(1)}, u32[]{:S(2)}, u32[]{:S(2)}) collective-permute-start(bf16[128,128]{1,0:T(8,128)(2,1)S(1)} %add_convert_fusion.1.u_ref), channel_id=1, source_target_pairs={{0,24},{8,16},{16,8},{24,0},{1,25},{9,17},{17,9},{25,1},{2,26},{10... | collective-permute-start | bytes 98312 | tf_op jit(solution)/shard_map/u_sum/ppermute | solution.py:310
  69.3 5.4 %collective-permute-start.11 = (bf16[128,128]{1,0:T(8,128)(2,1)S(1)}, bf16[128,128]{1,0:T(8,128)(2,1)S(1)}, u32[]{:S(2)}, u32[]{:S(2)}) collective-permute-start(bf16[128,128]{1,0:T(8,128)(2,1)S(1)} %add_convert_fusion.1.u_ref), channel_id=1, source_target_pairs={{0,16},{8,24},{16,0},{24,8},{1,17},{9,25},{17,1},{25,9},{2,18},{10... | collective-permute-start | bytes 98312 | tf_op jit(solution)/shard_map/u_sum/ppermute | solution.py:310
  71.5 3.9 %collective-permute-start.10 = (bf16[128,128]{1,0:T(8,128)(2,1)S(1)}, bf16[128,128]{1,0:T(8,128)(2,1)S(1)}, u32[]{:S(2)}, u32[]{:S(2)}) collective-permute-start(bf16[128,128]{1,0:T(8,128)(2,1)S(1)} %add_convert_fusion.1.u_ref), channel_id=1, source_target_pairs={{0,8},{8,0},{16,24},{24,16},{1,9},{9,1},{17,25},{25,17},{2,10},{10... | collective-permute-start | bytes 98312 | tf_op jit(solution)/shard_map/u_sum/ppermute | solution.py:310

commit v9 on v8

--- a/solution.py
+++ b/solution.py
@@ -350,7 +350,7 @@
         got = [pair(u, "z", NZ, k) for k in (1, 2, 3)]
         got, p_factor, f = lax.optimization_barrier((got, *factor(mine, inv, p_mine, p_theirs)))
         u = tree(u, got)
-        got = [pair(u, "x", NX, k) for k in (1, 2, 3)]
+        got = [pair(u, "x", NX, k) for k in (1, 3, 2)]
     with jax.named_scope("back"):
         error_out, q_factor = back(mine, f, c_own, c_other, inv, (u, *got))
     return momentum_out, error_out, p_factor, q_factor

time: 78.7 us -> 78.6 us (level)
  waiting for transfers between devices: 11 us -> 12.2 us
    ppermute x11, waiting for transfers between devices: 9.55 us -> 10.8 us  [pair(): return lax.ppermute(x, axis, [(i, i ^ flip) for i in range(size)])]
where the time goes in v9:
time: 78.6 us; the launch traced here: 78.4 us
  blocking collectives  32 us (41%)
  starting transfers between devices  20 us (25%)
  Pallas kernels  13.3 us (17%)
  waiting for transfers between devices  12.2 us (16%)
    all_to_all x2, blocking collectives, exchange(): return lax.all_to_all(x, axes, 0, 0)  32 us
    ppermute x11, starting transfers between devices, pair(): return lax.ppermute(x, axis, [(i, i ^ flip) for i in range(size)])  19.9 us
    ppermute x11, waiting for transfers between devices, pair(): return lax.ppermute(x, axis, [(i, i ^ flip) for i in range(size)])  10.8 us
    pallas_call x2, Pallas kernels, front(): pl.pallas_call(front_body, in_specs=[pl.BlockSpec(memory_space=pltpu.SMEM...  4.74 us
    pallas_call x1, Pallas kernels, back(): pl.pallas_call(back_body, in_specs=[pl.BlockSpec(memory_space=pltpu.SMEM)...  2.45 us
    pallas_call x1, Pallas kernels, inverse(): pl.pallas_call(invert, out_shape=jax.ShapeDtypeStruct((RANK2, RANK2), F32...  2.1 us
    pallas_call x1, Pallas kernels, factor(): pl.pallas_call(factor_body, in_specs=[pl.BlockSpec(memory_space=pltpu.SME...  1.61 us
  transfers between devices with their start and end apart: 13, of which 10 were waited for; matrix products, arithmetic and copies ran while one was open for 0% of the time, Pallas kernels for 10%

profile of v9, /device:TPU:32, one launch (start us, length us, event | category | flops | bytes accessed | tf_op | source)
XLA Modules:
  0.0 78.4 jit_solution(11514417738435652890)
XLA Ops:
  0.6 2.8 %p_partial.2 = (bf16[2,2048,128]{2,1,0:T(8,128)(2,1)S(1)}, bf16[2,2048,128]{2,1,0:T(8,128)(2,1)S(1)}, bf16[2048,128]{1,0:T(8,128)(2,1)S(1)}, bf16[2,1024,128]{2,...) custom-call(s32[1]{0:T(128)} %bitcast.1.half_ref, ...), custom_call_target="tpu_custom_call" | custom-call | flops 134217728 | bytes 4194304 | tf_op jit(solution)/shard_map/p_partial/pallas_call | solution.py:79
  3.5 2.0 %p_partial.3 = (bf16[2,2048,128]{2,1,0:T(8,128)(2,1)S(1)}, bf16[2,2048,128]{2,1,0:T(8,128)(2,1)S(1)}, f32[2048,128]{1,0:T(8,128)S(1)}) custom-call(s32[1]{0:T(128)} %bitcast.half_ref, bf16[1,2,4096,128]{3,2,1,0:T(8,128)(2,1)} %g_hbm.3, bf16[1,2,4096,128]{3,2,1,0:T(8,128)(2,1)} %m_hbm.3, bf16[1,2,4096,128]{3,2,1,0:T(8,128)(2,1)} %e_hbm.3, ...), custom_call_target="tpu_custom_call" | custom-call | flops 134217728 | bytes 4194304 | tf_op jit(solution)/shard_map/p_partial/pallas_call | solution.py:79
  5.5 0.1 add_convert_fusion
  5.6 19.0 %all_to_all.10.x_ref = bf16[16,128,128]{2,1,0:T(8,128)(2,1)S(1)} all-to-all(bf16[16,128,128]{2,1,0:T(8,128)(2,1)S(1)} %bitcast.14), channel_id=1, replica_groups=mesh['z'=8,'x'=4,'y'=4,'c'=2] {'y','x'}, dimensions={0} | all-to-all | bytes 1048576 | tf_op jit(solution)/shard_map/p_sum/all_to_all | solution.py:318
  24.7 5.5 %collective-permute-start.1 = (bf16[128,128]{1,0:T(8,128)(2,1)S(1)}, bf16[128,128]{1,0:T(8,128)(2,1)S(1)}, u32[]{:S(2)}, u32[]{:S(2)}) collective-permute-start(bf16[128,128]{1,0:T(8,128)(2,1)S(1)} %bitcast.13), channel_id=1, source_target_pairs={{0,192},{32,224},{64,128},{96,160},{128,64},{160,96},{192,0},{224,... | collective-permute-start | bytes 98312 | tf_op jit(solution)/shard_map/p_sum/ppermute | solution.py:310
  30.2 1.9 %collective-permute-done.1 = bf16[128,128]{1,0:T(8,128)(2,1)S(1)} collective-permute-done((bf16[128,128]{1,0:T(8,128)(2,1)S(1)}, bf16[128,128]{1,0:T(8,128)(2,1)S(1)}, u32[]{:S(2)}, u32[]{:S(2)}) %collective-permute-start.1) | collective-permute-done | bytes 32800 | tf_op jit(solution)/shard_map/p_sum/ppermute | solution.py:310
  32.1 1.1 %collective-permute-start.4 = (bf16[128,128]{1,0:T(8,128)(2,1)S(1)}, bf16[128,128]{1,0:T(8,128)(2,1)S(1)}, u32[]{:S(2)}, u32[]{:S(2)}) collective-permute-start(bf16[128,128]{1,0:T(8,128)(2,1)S(1)} %add_convert_fusion.3), channel_id=1, source_target_pairs={{0,96},{32,64},{64,32},{96,0},{128,224},{160,192},{192,160},{224,1... | collective-permute-start | bytes 98312 | tf_op jit(solution)/shard_map/p_sum/ppermute | solution.py:310
  33.2 2.4 %collective-permute-start.3 = (bf16[128,128]{1,0:T(8,128)(2,1)S(1)}, bf16[128,128]{1,0:T(8,128)(2,1)S(1)}, u32[]{:S(2)}, u32[]{:S(2)}) collective-permute-start(bf16[128,128]{1,0:T(8,128)(2,1)S(1)} %add_convert_fusion.3), channel_id=1, source_target_pairs={{0,64},{32,96},{64,0},{96,32},{128,192},{160,224},{192,128},{224,1... | collective-permute-start | bytes 98312 | tf_op jit(solution)/shard_map/p_sum/ppermute | solution.py:310
  35.6 0.1 collective-permute-start.2
  35.7 1.3 %p_sum.4 = bf16[1,2,4096,128]{3,2,1,0:T(8,128)(2,1)} custom-call(s32[1]{0:T(128)} %bitcast.half_ref, bf16[2,2048,128]{2,1,0:T(8,128)(2,1)S(1)} %get-tuple-element.37.own_ref, bf16[2,2048,128]{2,1,0:T(8,128)(2,1)S(1)} %get-tuple-element.38.other_ref), custom_call_target="tpu_custom_call" | custom-call | bytes 4194304 | tf_op jit(solution)/shard_map/p_sum/pallas_call | solution.py:210
  37.0 1.0 %collective-permute-done.3 = bf16[128,128]{1,0:T(8,128)(2,1)S(1)} collective-permute-done((bf16[128,128]{1,0:T(8,128)(2,1)S(1)}, bf16[128,128]{1,0:T(8,128)(2,1)S(1)}, u32[]{:S(2)}, u32[]{:S(2)}) %collective-permute-start.3) | collective-permute-done | bytes 32800 | tf_op jit(solution)/shard_map/p_sum/ppermute | solution.py:310
  38.0 1.5 %collective-permute-done.2 = bf16[128,128]{1,0:T(8,128)(2,1)S(1)} collective-permute-done((bf16[128,128]{1,0:T(8,128)(2,1)S(1)}, bf16[128,128]{1,0:T(8,128)(2,1)S(1)}, u32[]{:S(2)}, u32[]{:S(2)}) %collective-permute-start.2) | collective-permute-done | bytes 32800 | tf_op jit(solution)/shard_map/p_sum/ppermute | solution.py:310
  39.6 13.0 %all_to_all.11 = bf16[16,128,128]{2,1,0:T(8,128)(2,1)S(1)} all-to-all(bf16[16,128,128]{2,1,0:T(8,128)(2,1)S(1)} %p_sum.5), channel_id=1, replica_groups=mesh['z'=8,'x'=4,'y'=4,'c'=2] {'y','x'}, dimensions={0} | all-to-all | bytes 1048576 | tf_op jit(solution)/shard_map/p_sum/all_to_all | solution.py:318
  52.6 0.5 u_sum.4
  53.1 1.4 %collective-permute-done.5.p_ref.pt_ref = bf16[2048,128]{1,0:T(8,128)(2,1)S(1)} collective-permute-done((bf16[2048,128]{1,0:T(8,128)(2,1)S(1)}, bf16[2048,128]{1,0:T(8,128)(2,1)S(1)}, u32[]{:S(2)}, u32[]{:S(2)}) %collective-permute-start.5) | collective-permute-done | bytes 524320 | tf_op jit(solution)/shard_map/p_sum/ppermute | solution.py:306
  54.5 0.5 u_sum.5
  55.0 3.7 %collective-permute-start.6 = (bf16[128,128]{1,0:T(8,128)(2,1)S(1)}, bf16[128,128]{1,0:T(8,128)(2,1)S(1)}, u32[]{:S(2)}, u32[]{:S(2)}) collective-permute-start(bf16[128,128]{1,0:T(8,128)(2,1)S(1)} %get-tuple-element.47), channel_id=1, source_target_pairs={{0,192},{32,224},{64,128},{96,160},{128,64},{160,96},{192,0},{224,... | collective-permute-start | bytes 98312 | tf_op jit(solution)/shard_map/u_sum/ppermute | solution.py:310
  58.7 2.1 %u_sum.6.l_ref = f32[128,128]{1,0:T(8,128)S(1)} custom-call(f32[128,128]{1,0:T(8,128)S(1)} %get-tuple-element.48.g_ref), custom_call_target="tpu_custom_call" | custom-call | flops 262144 | bytes 6291456 | tf_op jit(solution)/shard_map/u_sum/pallas_call | solution.py:189
  60.8 0.9 %collective-permute-done.6 = bf16[128,128]{1,0:T(8,128)(2,1)S(1)} collective-permute-done((bf16[128,128]{1,0:T(8,128)(2,1)S(1)}, bf16[128,128]{1,0:T(8,128)(2,1)S(1)}, u32[]{:S(2)}, u32[]{:S(2)}) %collective-permute-start.6) | collective-permute-done | bytes 32800 | tf_op jit(solution)/shard_map/u_sum/ppermute | solution.py:310
  61.7 1.3 %collective-permute-start.9 = (bf16[128,128]{1,0:T(8,128)(2,1)S(1)}, bf16[128,128]{1,0:T(8,128)(2,1)S(1)}, u32[]{:S(2)}, u32[]{:S(2)}) collective-permute-start(bf16[128,128]{1,0:T(8,128)(2,1)S(1)} %add_convert_fusion.2), channel_id=1, source_target_pairs={{0,96},{32,64},{64,32},{96,0},{128,224},{160,192},{192,160},{224,1... | collective-permute-start | bytes 98312 | tf_op jit(solution)/shard_map/u_sum/ppermute | solution.py:310
  63.0 1.8 %collective-permute-start.8 = (bf16[128,128]{1,0:T(8,128)(2,1)S(1)}, bf16[128,128]{1,0:T(8,128)(2,1)S(1)}, u32[]{:S(2)}, u32[]{:S(2)}) collective-permute-start(bf16[128,128]{1,0:T(8,128)(2,1)S(1)} %add_convert_fusion.2), channel_id=1, source_target_pairs={{0,64},{32,96},{64,0},{96,32},{128,192},{160,224},{192,128},{224,1... | collective-permute-start | bytes 98312 | tf_op jit(solution)/shard_map/u_sum/ppermute | solution.py:310
  64.8 0.5 collective-permute-start.7
  65.3 1.6 %u_sum.7 = (bf16[4096,128]{1,0:T(8,128)(2,1)}, bf16[4096,128]{1,0:T(8,128)(2,1)S(1)}) custom-call(s32[1]{0:T(128)} %bitcast.half_ref, f32[128,128]{1,0:T(8,128)S(1)} %u_sum.6.l_ref, bf16[2048,128]{1,0:T(8,128)(2,1)S(1)} %bitcast.12, bf16[2048,128]{1,0:T(8,128)(2,1)S(1)} %collective-permute-done.5.p_ref.pt_ref), custom_call_target="tpu_custom_call" | custom-call | flops 268435456 | bytes 6291456 | tf_op jit(solution)/shard_map/u_sum/pallas_call | solution.py:242
  66.9 1.0 %collective-permute-done.8 = bf16[128,128]{1,0:T(8,128)(2,1)S(1)} collective-permute-done((bf16[128,128]{1,0:T(8,128)(2,1)S(1)}, bf16[128,128]{1,0:T(8,128)(2,1)S(1)}, u32[]{:S(2)}, u32[]{:S(2)}) %collective-permute-start.8) | collective-permute-done | bytes 32800 | tf_op jit(solution)/shard_map/u_sum/ppermute | solution.py:310
  67.9 0.8 %collective-permute-done.7 = bf16[128,128]{1,0:T(8,128)(2,1)S(1)} collective-permute-done((bf16[128,128]{1,0:T(8,128)(2,1)S(1)}, bf16[128,128]{1,0:T(8,128)(2,1)S(1)}, u32[]{:S(2)}, u32[]{:S(2)}) %collective-permute-start.7) | collective-permute-done | bytes 32800 | tf_op jit(solution)/shard_map/u_sum/ppermute | solution.py:310
  68.7 0.9 %collective-permute-start.12 = (bf16[128,128]{1,0:T(8,128)(2,1)S(1)}, bf16[128,128]{1,0:T(8,128)(2,1)S(1)}, u32[]{:S(2)}, u32[]{:S(2)}) collective-permute-start(bf16[128,128]{1,0:T(8,128)(2,1)S(1)} %add_convert_fusion.1.u_ref), channel_id=1, source_target_pairs={{0,16},{8,24},{16,0},{24,8},{1,17},{9,25},{17,1},{25,9},{2,18},{10... | collective-permute-start | bytes 98312 | tf_op jit(solution)/shard_map/u_sum/ppermute | solution.py:310
  69.6 2.4 %collective-permute-start.11 = (bf16[128,128]{1,0:T(8,128)(2,1)S(1)}, bf16[128,128]{1,0:T(8,128)(2,1)S(1)}, u32[]{:S(2)}, u32[]{:S(2)}) collective-permute-start(bf16[128,128]{1,0:T(8,128)(2,1)S(1)} %add_convert_fusion.1.u_ref), channel_id=1, source_target_pairs={{0,24},{8,16},{16,8},{24,0},{1,25},{9,17},{17,9},{25,1},{2,26},{10... | collective-permute-start | bytes 98312 | tf_op jit(solution)/shard_map/u_sum/ppermute | solution.py:310
  72.1 0.2 collective-permute-start.10
  72.3 1.9 %collective-permute-done.12.d_ref = bf16[128,128]{1,0:T(8,128)(2,1)S(1)} collective-permute-done((bf16[128,128]{1,0:T(8,128)(2,1)S(1)}, bf16[128,128]{1,0:T(8,128)(2,1)S(1)}, u32[]{:S(2)}, u32[]{:S(2)}) %collective-permute-start.12) | collective-permute-done | bytes 32800 | tf_op jit(solution)/shard_map/u_sum/ppermute | solution.py:310
  74.2 0.5 collective-permute-done.11.b_ref
  74.8 1.2 %collective-permute-done.10.a_ref = bf16[128,128]{1,0:T(8,128)(2,1)S(1)} collective-permute-done((bf16[128,128]{1,0:T(8,128)(2,1)S(1)}, bf16[128,128]{1,0:T(8,128)(2,1)S(1)}, u32[]{:S(2)}, u32[]{:S(2)}) %collective-permute-start.10) | collective-permute-done | bytes 32800 | tf_op jit(solution)/shard_map/u_sum/ppermute | solution.py:310
  76.0 2.5 %back.1 = (bf16[1,2,4096,128]{3,2,1,0:T(8,128)(2,1)}, f32[128,128]{1,0:T(8,128)}) custom-call(s32[1]{0:T(128)} %bitcast.half_ref, bf16[4096,128]{1,0:T(8,128)(2,1)S(1)} %get-tuple-element.53.f_ref, bf16[2,2048,128]{2,1,0:T(8,128)(2,1)S(1)} %get-tuple-element.44.c_ref.co_ref, bf16[2,2048,128]{2,1,0:T(8,128)(2,1)S(1)} %get-tuple-element.43.c_ref.ct_ref, ...), custom_call_target="tpu_custom_call" | custom-call | flops 268435456 | bytes 6291456 | tf_op jit(solution)/shard_map/back/pallas_call | solution.py:287
  (11 shorter events, 0.3 us)
Async XLA Ops:
  3.4 2.1 %collective-permute-start = (bf16[2048,128]{1,0:T(8,128)(2,1)S(1)}, bf16[2048,128]{1,0:T(8,128)(2,1)S(1)}, u32[]{:S(2)}, u32[]{:S(2)}) collective-permute-start(bf16[2048,128]{1,0:T(8,128)(2,1)S(1)} %get-tuple-element.36), channel_id=1, source_target_pairs={{0,1},{1,0},{2,3},{3,2},{4,5},{5,4},{6,7},{7,6},{8,9},{9,8},{10,11... | collective-permute-start | bytes 1572872 | tf_op jit(solution)/shard_map/p_partial/ppermute | solution.py:306
  24.7 7.4 %collective-permute-start.1 = (bf16[128,128]{1,0:T(8,128)(2,1)S(1)}, bf16[128,128]{1,0:T(8,128)(2,1)S(1)}, u32[]{:S(2)}, u32[]{:S(2)}) collective-permute-start(bf16[128,128]{1,0:T(8,128)(2,1)S(1)} %bitcast.13), channel_id=1, source_target_pairs={{0,192},{32,224},{64,128},{96,160},{128,64},{160,96},{192,0},{224,... | collective-permute-start | bytes 98312 | tf_op jit(solution)/shard_map/p_sum/ppermute | solution.py:310
  32.1 4.9 %collective-permute-start.4 = (bf16[128,128]{1,0:T(8,128)(2,1)S(1)}, bf16[128,128]{1,0:T(8,128)(2,1)S(1)}, u32[]{:S(2)}, u32[]{:S(2)}) collective-permute-start(bf16[128,128]{1,0:T(8,128)(2,1)S(1)} %add_convert_fusion.3), channel_id=1, source_target_pairs={{0,96},{32,64},{64,32},{96,0},{128,224},{160,192},{192,160},{224,1... | collective-permute-start | bytes 98312 | tf_op jit(solution)/shard_map/p_sum/ppermute | solution.py:310
  33.2 4.8 %collective-permute-start.3 = (bf16[128,128]{1,0:T(8,128)(2,1)S(1)}, bf16[128,128]{1,0:T(8,128)(2,1)S(1)}, u32[]{:S(2)}, u32[]{:S(2)}) collective-permute-start(bf16[128,128]{1,0:T(8,128)(2,1)S(1)} %add_convert_fusion.3), channel_id=1, source_target_pairs={{0,64},{32,96},{64,0},{96,32},{128,192},{160,224},{192,128},{224,1... | collective-permute-start | bytes 98312 | tf_op jit(solution)/shard_map/p_sum/ppermute | solution.py:310
  35.6 3.9 %collective-permute-start.2 = (bf16[128,128]{1,0:T(8,128)(2,1)S(1)}, bf16[128,128]{1,0:T(8,128)(2,1)S(1)}, u32[]{:S(2)}, u32[]{:S(2)}) collective-permute-start(bf16[128,128]{1,0:T(8,128)(2,1)S(1)} %add_convert_fusion.3), channel_id=1, source_target_pairs={{0,32},{32,0},{64,96},{96,64},{128,160},{160,128},{192,224},{224,1... | collective-permute-start | bytes 98312 | tf_op jit(solution)/shard_map/p_sum/ppermute | solution.py:310
  52.6 1.9 %collective-permute-start.5 = (bf16[2048,128]{1,0:T(8,128)(2,1)S(1)}, bf16[2048,128]{1,0:T(8,128)(2,1)S(1)}, u32[]{:S(2)}, u32[]{:S(2)}) collective-permute-start(bf16[2048,128]{1,0:T(8,128)(2,1)S(1)} %bitcast.10), channel_id=1, source_target_pairs={{0,1},{1,0},{2,3},{3,2},{4,5},{5,4},{6,7},{7,6},{8,9},{9,8},{10,11... | collective-permute-start | bytes 1572872 | tf_op jit(solution)/shard_map/p_sum/ppermute | solution.py:306
  55.0 6.7 %collective-permute-start.6 = (bf16[128,128]{1,0:T(8,128)(2,1)S(1)}, bf16[128,128]{1,0:T(8,128)(2,1)S(1)}, u32[]{:S(2)}, u32[]{:S(2)}) collective-permute-start(bf16[128,128]{1,0:T(8,128)(2,1)S(1)} %get-tuple-element.47), channel_id=1, source_target_pairs={{0,192},{32,224},{64,128},{96,160},{128,64},{160,96},{192,0},{224,... | collective-permute-start | bytes 98312 | tf_op jit(solution)/shard_map/u_sum/ppermute | solution.py:310
  61.7 5.2 %collective-permute-start.9 = (bf16[128,128]{1,0:T(8,128)(2,1)S(1)}, bf16[128,128]{1,0:T(8,128)(2,1)S(1)}, u32[]{:S(2)}, u32[]{:S(2)}) collective-permute-start(bf16[128,128]{1,0:T(8,128)(2,1)S(1)} %add_convert_fusion.2), channel_id=1, source_target_pairs={{0,96},{32,64},{64,32},{96,0},{128,224},{160,192},{192,160},{224,1... | collective-permute-start | bytes 98312 | tf_op jit(solution)/shard_map/u_sum/ppermute | solution.py:310
  63.0 4.9 %collective-permute-start.8 = (bf16[128,128]{1,0:T(8,128)(2,1)S(1)}, bf16[128,128]{1,0:T(8,128)(2,1)S(1)}, u32[]{:S(2)}, u32[]{:S(2)}) collective-permute-start(bf16[128,128]{1,0:T(8,128)(2,1)S(1)} %add_convert_fusion.2), channel_id=1, source_target_pairs={{0,64},{32,96},{64,0},{96,32},{128,192},{160,224},{192,128},{224,1... | collective-permute-start | bytes 98312 | tf_op jit(solution)/shard_map/u_sum/ppermute | solution.py:310
  64.8 3.9 %collective-permute-start.7 = (bf16[128,128]{1,0:T(8,128)(2,1)S(1)}, bf16[128,128]{1,0:T(8,128)(2,1)S(1)}, u32[]{:S(2)}, u32[]{:S(2)}) collective-permute-start(bf16[128,128]{1,0:T(8,128)(2,1)S(1)} %add_convert_fusion.2), channel_id=1, source_target_pairs={{0,32},{32,0},{64,96},{96,64},{128,160},{160,128},{192,224},{224,1... | collective-permute-start | bytes 98312 | tf_op jit(solution)/shard_map/u_sum/ppermute | solution.py:310
  68.7 5.5 %collective-permute-start.12 = (bf16[128,128]{1,0:T(8,128)(2,1)S(1)}, bf16[128,128]{1,0:T(8,128)(2,1)S(1)}, u32[]{:S(2)}, u32[]{:S(2)}) collective-permute-start(bf16[128,128]{1,0:T(8,128)(2,1)S(1)} %add_convert_fusion.1.u_ref), channel_id=1, source_target_pairs={{0,16},{8,24},{16,0},{24,8},{1,17},{9,25},{17,1},{25,9},{2,18},{10... | collective-permute-start | bytes 98312 | tf_op jit(solution)/shard_map/u_sum/ppermute | solution.py:310
  69.6 5.1 %collective-permute-start.11 = (bf16[128,128]{1,0:T(8,128)(2,1)S(1)}, bf16[128,128]{1,0:T(8,128)(2,1)S(1)}, u32[]{:S(2)}, u32[]{:S(2)}) collective-permute-start(bf16[128,128]{1,0:T(8,128)(2,1)S(1)} %add_convert_fusion.1.u_ref), channel_id=1, source_target_pairs={{0,24},{8,16},{16,8},{24,0},{1,25},{9,17},{17,9},{25,1},{2,26},{10... | collective-permute-start | bytes 98312 | tf_op jit(solution)/shard_map/u_sum/ppermute | solution.py:310
  72.1 3.9 %collective-permute-start.10 = (bf16[128,128]{1,0:T(8,128)(2,1)S(1)}, bf16[128,128]{1,0:T(8,128)(2,1)S(1)}, u32[]{:S(2)}, u32[]{:S(2)}) collective-permute-start(bf16[128,128]{1,0:T(8,128)(2,1)S(1)} %add_convert_fusion.1.u_ref), channel_id=1, source_target_pairs={{0,8},{8,0},{16,24},{24,16},{1,9},{9,1},{17,25},{25,17},{2,10},{10... | collective-permute-start | bytes 98312 | tf_op jit(solution)/shard_map/u_sum/ppermute | solution.py:310
